TPU v7x, 256 devices: a whole 4x4x8 slice. The times are simulated.
256 devices in a mesh: shot: 32 (over x, z_hi, core), tile: 8 (over z_lo, y).
Axes of the slice: x: 4, y: 4, z: 8 (z_hi: 4, z_lo: 2; z = z_hi * 2 + z_lo), core: 2. Of those that a mesh axis runs over, the one named last changes fastest.
Arguments:
- velocity: float32 [128, 64, 128], P('shot', 'tile'), may hold values from 0.2 to 0.55
- density: float32 [128, 64, 128], P('shot', 'tile'), may hold values from 1 to 3
- anchors: int32 [32], replicated, may hold values from 0 to 16
- src_state: float32 [4, 2048, 64, 128], P(None, 'shot', 'tile'), may hold values from -6 to 6
- rcv_state: float32 [4, 2048, 64, 128], P(None, 'shot', 'tile'), may hold values from -6 to 6
- src_pos: int32 [32, 16], P('shot'), may hold values from 0 to 524287
- wavelet: float32 [32, 16, 4], P('shot'), may hold values from -6 to 6
- rec_pos: int32 [32, 128], P('shot'), may hold values from 0 to 524287
- traces: float32 [32, 128, 4], P('shot'), may hold values from -6 to 6
Outputs:
- stacked_image: float32 [128, 64, 128], P('shot', 'tile')
Inputs may be any that keep to these rules, and one draw needn't show every extreme that they name: `anchors`: each aperture covers 16 whole strips of the slab.
All inputs are finite; a program needn't handle non-finite values.
Results may differ from a plain program's by a relative error of at most 0.00002.
Values sent between devices are 32-bit elements; how exact they have to be, the bound alone decides.
No kernel may reach another device: no remote copies, remote signals or barrier semaphores. Data moves between devices by JAX's collectives and lax.ppermute only.
A program may use at most 64 MiB of HBM per device.

v0:
```python
import jax
import jax.numpy as jnp
from jax import lax
from jax.sharding import PartitionSpec as P

STEPS = 4


def shifted(block, axis, distance):
    devices = range(lax.axis_size(axis))
    route = [(i - distance, i) for i in devices if i - distance in devices]
    return lax.ppermute(block, axis, route)


def next_cell(field, dimension):
    length = field.shape[dimension]
    remainder = lax.slice_in_dim(field, 1, length, axis=dimension)
    border = jnp.zeros_like(lax.slice_in_dim(field, 0, 1, axis=dimension))
    return jnp.concatenate([remainder, border], axis=dimension)


def prev_cell(field, dimension):
    length = field.shape[dimension]
    remainder = lax.slice_in_dim(field, 0, length - 1, axis=dimension)
    border = jnp.zeros_like(lax.slice_in_dim(field, 0, 1, axis=dimension))
    return jnp.concatenate([border, remainder], axis=dimension)


def velocity_core(pressure, pressure_after, vel_x, vel_y, vel_z, buoyancy):
    vel_x = vel_x - buoyancy * (next_cell(pressure, 0) - pressure)
    vel_y = vel_y - buoyancy * (pressure_after - pressure)
    vel_z = vel_z - buoyancy * (next_cell(pressure, 2) - pressure)
    return (vel_x, vel_y, vel_z)


def pressure_core(pressure, vel_x, vel_y, vel_y_before, vel_z, modulus):
    spread = vel_x - prev_cell(vel_x, 0) + (vel_y - vel_y_before) + (vel_z - prev_cell(vel_z, 2))
    return pressure - modulus * spread


def velocity_shifted(pressure, vel_x, vel_y, vel_z, buoyancy):
    following = shifted(pressure[:, 0, :], "tile", -1)
    pressure_after = jnp.concatenate([pressure[:, 1:, :], following[:, None, :]], axis=1)
    return velocity_core(pressure, pressure_after, vel_x, vel_y, vel_z, buoyancy)


def pressure_shifted(pressure, vel_x, vel_y, vel_z, modulus):
    preceding = shifted(vel_y[:, -1, :], "tile", 1)
    vel_y_before = jnp.concatenate([preceding[:, None, :], vel_y[:, :-1, :]], axis=1)
    return pressure_core(pressure, vel_x, vel_y, vel_y_before, vel_z, modulus)


def inject_points(pressure, position, amplitudes, first_col, full_cols):
    span_rows, block_cols, depth_cells = pressure.shape
    cell_x = position // (full_cols * depth_cells)
    cell_y = position // depth_cells % full_cols
    cell_z = position % depth_cells
    local_y = cell_y - first_col
    inside = (local_y >= 0) & (local_y < block_cols)
    return pressure.at[cell_x, jnp.clip(local_y, 0, block_cols - 1), cell_z].add(
        jnp.where(inside, amplitudes, 0.0)
    )


def run_passes(
    forward,
    backward,
    modulus,
    buoyancy,
    velocity_fn,
    pressure_fn,
    src_pos,
    wavelet,
    rec_pos,
    traces,
    first_col,
    full_cols,
):
    pressure, vel_x, vel_y, vel_z = (forward[0], forward[1], forward[2], forward[3])
    saved_pressure = []
    for step_index in range(STEPS):
        vel_x, vel_y, vel_z = velocity_fn(pressure, vel_x, vel_y, vel_z, buoyancy)
        pressure = pressure_fn(pressure, vel_x, vel_y, vel_z, modulus)
        pressure = inject_points(
            pressure, src_pos[0], wavelet[0][:, step_index], first_col, full_cols
        )
        saved_pressure.append(pressure)
    pressure, vel_x, vel_y, vel_z = (backward[0], backward[1], backward[2], backward[3])
    correlation = jnp.zeros_like(saved_pressure[0])
    for step_index in range(STEPS):
        pressure = pressure_fn(pressure, vel_x, vel_y, vel_z, modulus)
        vel_x, vel_y, vel_z = velocity_fn(pressure, vel_x, vel_y, vel_z, buoyancy)
        pressure = inject_points(
            pressure, rec_pos[0], traces[0][:, STEPS - 1 - step_index], first_col, full_cols
        )
        correlation = correlation + saved_pressure[STEPS - 1 - step_index] * pressure
    return correlation / STEPS


def local(velocity, density, anchors, src_state, rcv_state, src_pos, wavelet, rec_pos, traces):
    group_index = lax.axis_index("shot")
    tile_index = lax.axis_index("tile")
    shot_count = lax.axis_size("shot")
    tile_count = lax.axis_size("tile")
    strip_rows, tile_cols, depth_cells = velocity.shape
    span_rows = src_state.shape[1]
    full_cols = tile_cols * tile_count
    vel_column, den_column = (
        lax.all_gather(velocity, "shot", axis=0, tiled=True),
        lax.all_gather(density, "shot", axis=0, tiled=True),
    )
    row_start = anchors[group_index] * strip_rows
    vel = lax.dynamic_slice_in_dim(vel_column, row_start, span_rows, 0)
    den = lax.dynamic_slice_in_dim(den_column, row_start, span_rows, 0)
    modulus = den * vel * vel
    buoyancy = 1.0 / den
    correlation = run_passes(
        src_state,
        rcv_state,
        modulus,
        buoyancy,
        velocity_shifted,
        pressure_shifted,
        src_pos,
        wavelet,
        rec_pos,
        traces,
        tile_index * tile_cols,
        full_cols,
    )
    column = jnp.zeros((shot_count * strip_rows, tile_cols, depth_cells), jnp.float32)
    column = lax.dynamic_update_slice_in_dim(column, correlation, row_start, 0)
    stacked = lax.psum_scatter(column, "shot", scatter_dimension=0, tiled=True)
    return stacked


def solution(mesh):
    return jax.shard_map(
        local,
        mesh=mesh,
        in_specs=(
            P("shot", "tile", None),
            P("shot", "tile", None),
            P(),
            P(None, "shot", "tile", None),
            P(None, "shot", "tile", None),
            P("shot", None),
            P("shot", None, None),
            P("shot", None),
            P("shot", None, None),
        ),
        out_specs=P("shot", "tile", None),
        check_vma=False,
    )
```

profile of v0, /device:TPU:24, one launch (start us, length us, event | category | flops | bytes accessed | tf_op | source)
XLA Modules:
  0.0 320.7 jit_solution(14246577068535445172)
XLA Ops:
  6.5 1.1 slice_bitcast_fusion.2
  7.6 2.7 collective-permute-start
  10.3 1.8 slice_bitcast_fusion
  12.1 5.3 %collective-permute-start.8 = (f32[64,128]{1,0:T(8,128)S(1)}, f32[64,128]{1,0:T(8,128)S(1)}, u32[]{:S(2)}, u32[]{:S(2)}) collective-permute-start(f32[64,128]{1,0:T(8,128)S(1)} %bitcast.227), channel_id=1, source_target_pairs={{0,1},{1,2},{2,3},{3,4},{4,5},{5,6},{6,7},{8,9},{9,10},{10,11},{11... | collective-permute-start | bytes 98312 | tf_op jit(solution)/shard_map/ppermute | solution.py:12
  17.4 1.7 slice_bitcast_fusion.4
  19.1 0.7 slice_bitcast_fusion.3
  19.8 49.1 %all_gather.6 = f32[128,8,128]{2,1,0:T(8,128)S(1)} all-gather(f32[4,8,128]{2,1,0:T(8,128)S(1)} %copy-done.25), channel_id=1, replica_groups=mesh['shot'=32,'tile'=8] {'shot'}, dimensions={0}, use_global_device_ids=true | all-gather | bytes 540672 | tf_op jit(solution)/shard_map/all_gather | solution.py:110
  68.9 43.2 %all_gather.7 = f32[128,8,128]{2,1,0:T(8,128)} all-gather(f32[4,8,128]{2,1,0:T(8,128)S(1)} %copy-done.26), channel_id=1, replica_groups=mesh['shot'=32,'tile'=8] {'shot'}, dimensions={0}, use_global_device_ids=true | all-gather | bytes 540672 | tf_op jit(solution)/shard_map/all_gather | solution.py:109
  112.1 0.7 copy-done.27
  112.9 0.1 slice.343
  113.1 0.6 copy-done.31
  113.7 0.6 dynamic_slice.9
  115.0 1.5 bitcast_subtract_fusion.3
  116.6 1.9 collective-permute-start.1
  118.5 0.2 fusion.27
  118.8 3.6 %collective-permute-done.1 = f32[64,128]{1,0:T(8,128)S(1)} collective-permute-done((f32[64,128]{1,0:T(8,128)S(1)}, f32[64,128]{1,0:T(8,128)S(1)}, u32[]{:S(2)}, u32[]{:S(2)}) %collective-permute-start.1) | collective-permute-done | bytes 32800 | tf_op jit(solution)/shard_map/ppermute | solution.py:12
  122.4 1.1 fusion.5
  123.5 1.5 scatter_fusion
  125.0 1.9 collective-permute-start.2
  127.0 0.1 slice.351
  127.2 5.8 %collective-permute-done.2 = f32[64,128]{1,0:T(8,128)S(1)} collective-permute-done((f32[64,128]{1,0:T(8,128)S(1)}, f32[64,128]{1,0:T(8,128)S(1)}, u32[]{:S(2)}, u32[]{:S(2)}) %collective-permute-start.2) | collective-permute-done | bytes 32800 | tf_op jit(solution)/shard_map/ppermute | solution.py:12
  132.9 0.2 multiply_subtract_fusion.10
  133.2 1.9 collective-permute-start.3
  135.1 3.8 %collective-permute-done.3 = f32[64,128]{1,0:T(8,128)S(1)} collective-permute-done((f32[64,128]{1,0:T(8,128)S(1)}, f32[64,128]{1,0:T(8,128)S(1)}, u32[]{:S(2)}, u32[]{:S(2)}) %collective-permute-start.3) | collective-permute-done | bytes 32800 | tf_op jit(solution)/shard_map/ppermute | solution.py:12
  139.0 0.2 fusion.11
  139.2 1.5 scatter_fusion.1
  140.7 1.9 collective-permute-start.4
  142.6 0.1 slice.359
  142.8 5.8 %collective-permute-done.4 = f32[64,128]{1,0:T(8,128)S(1)} collective-permute-done((f32[64,128]{1,0:T(8,128)S(1)}, f32[64,128]{1,0:T(8,128)S(1)}, u32[]{:S(2)}, u32[]{:S(2)}) %collective-permute-start.4) | collective-permute-done | bytes 32800 | tf_op jit(solution)/shard_map/ppermute | solution.py:12
  148.6 0.2 multiply_subtract_fusion.8
  148.9 2.1 collective-permute-start.5
  151.0 3.9 %collective-permute-start.9 = (f32[64,128]{1,0:T(8,128)S(1)}, f32[64,128]{1,0:T(8,128)S(1)}, u32[]{:S(2)}, u32[]{:S(2)}) collective-permute-start(f32[64,128]{1,0:T(8,128)S(1)} %bitcast.229), channel_id=1, source_target_pairs={{1,0},{2,1},{3,2},{4,3},{5,4},{6,5},{7,6},{9,8},{10,9},{11,10},{12... | collective-permute-start | bytes 98312 | tf_op jit(solution)/shard_map/ppermute | solution.py:12
  155.0 0.2 fusion.17
  155.2 1.5 scatter_fusion.2
  156.7 1.9 collective-permute-start.6
  158.7 0.1 slice.378
  158.9 0.1 slice.367
  159.0 0.1 collective-permute-done.9
  159.2 5.4 %collective-permute-done.6 = f32[64,128]{1,0:T(8,128)S(1)} collective-permute-done((f32[64,128]{1,0:T(8,128)S(1)}, f32[64,128]{1,0:T(8,128)S(1)}, u32[]{:S(2)}, u32[]{:S(2)}) %collective-permute-start.6) | collective-permute-done | bytes 32800 | tf_op jit(solution)/shard_map/ppermute | solution.py:12
  164.6 1.2 multiply_subtract_fusion.6
  165.9 1.9 collective-permute-start.10
  167.9 8.0 %scatter_fusion.4 = f32[64,8,128]{2,1,0:T(8,128)S(1)} fusion(f32[64,8,128]{2,1,0:T(8,128)S(1)} %get-tuple-element.9, s32[128]{0:T(128)S(1)} %fusion.60, f32[128]{0:T(128)S(1)} %get-tuple-element.44), kind=kCustom, calls=%fused_computation.4 | custom fusion | flops 128 | bytes 3072 | tf_op jit(solution)/shard_map/scatter-add | solution.py:60
  176.0 0.1 fusion.33
  176.1 3.9 %collective-permute-start.11 = (f32[64,128]{1,0:T(8,128)S(1)}, f32[64,128]{1,0:T(8,128)S(1)}, u32[]{:S(2)}, u32[]{:S(2)}) collective-permute-start(f32[64,128]{1,0:T(8,128)S(1)} %bitcast.236), channel_id=1, source_target_pairs={{1,0},{2,1},{3,2},{4,3},{5,4},{6,5},{7,6},{9,8},{10,9},{11,10},{12... | collective-permute-start | bytes 98312 | tf_op jit(solution)/shard_map/ppermute | solution.py:12
  180.1 1.0 slice.365
  181.0 4.0 %collective-permute-start.7 = (f32[64,128]{1,0:T(8,128)S(1)}, f32[64,128]{1,0:T(8,128)S(1)}, u32[]{:S(2)}, u32[]{:S(2)}) collective-permute-start(f32[64,128]{1,0:T(8,128)S(1)} %bitcast.230), channel_id=1, source_target_pairs={{0,1},{1,2},{2,3},{3,4},{4,5},{5,6},{6,7},{8,9},{9,10},{10,11},{11... | collective-permute-start | bytes 98312 | tf_op jit(solution)/shard_map/ppermute | solution.py:12
  185.1 0.1 slice.386
  185.3 0.2 multiply_subtract_fusion.3
  185.5 1.9 collective-permute-start.12
  187.5 0.7 slice.362
  188.2 0.7 slice.381
  188.9 8.0 %scatter_fusion.5 = f32[64,8,128]{2,1,0:T(8,128)S(1)} fusion(f32[64,8,128]{2,1,0:T(8,128)S(1)} %fusion.33, s32[128]{0:T(128)S(1)} %fusion.60, f32[128]{0:T(128)S(1)} %get-tuple-element.43), kind=kCustom, calls=%fused_computation.5 | custom fusion | flops 128 | bytes 3072 | tf_op jit(solution)/shard_map/scatter-add | solution.py:60
  197.0 1.8 fusion.23
  198.8 3.9 %collective-permute-start.13 = (f32[64,128]{1,0:T(8,128)S(1)}, f32[64,128]{1,0:T(8,128)S(1)}, u32[]{:S(2)}, u32[]{:S(2)}) collective-permute-start(f32[64,128]{1,0:T(8,128)S(1)} %bitcast.240), channel_id=1, source_target_pairs={{1,0},{2,1},{3,2},{4,3},{5,4},{6,5},{7,6},{9,8},{10,9},{11,10},{12... | collective-permute-start | bytes 98312 | tf_op jit(solution)/shard_map/ppermute | solution.py:12
  202.7 0.1 slice.394
  202.9 3.8 %collective-permute-done.13 = f32[64,128]{1,0:T(8,128)S(1)} collective-permute-done((f32[64,128]{1,0:T(8,128)S(1)}, f32[64,128]{1,0:T(8,128)S(1)}, u32[]{:S(2)}, u32[]{:S(2)}) %collective-permute-start.13) | collective-permute-done | bytes 32800 | tf_op jit(solution)/shard_map/ppermute | solution.py:12
  206.7 1.0 multiply_subtract_fusion.1
  207.7 2.1 collective-permute-start.14
  209.8 1.5 scatter_fusion.3
  211.4 8.0 %scatter_fusion.6 = f32[64,8,128]{2,1,0:T(8,128)S(1)} fusion(f32[64,8,128]{2,1,0:T(8,128)S(1)} %get-tuple-element.38, s32[128]{0:T(128)S(1)} %fusion.60, f32[128]{0:T(128)S(1)} %get-tuple-element.42), kind=kCustom, calls=%fused_computation.6 | custom fusion | flops 128 | bytes 3072 | tf_op jit(solution)/shard_map/scatter-add | solution.py:60
  219.4 0.2 fusion.45
  219.6 8.0 %scatter_fusion.7 = f32[64,8,128]{2,1,0:T(8,128)S(1)} fusion(f32[64,8,128]{2,1,0:T(8,128)S(1)} %fusion.45, s32[128]{0:T(128)S(1)} %fusion.60, f32[128]{0:T(128)S(1)} %get-tuple-element.7), kind=kCustom, calls=%fused_computation.7 | custom fusion | flops 128 | bytes 3072 | tf_op jit(solution)/shard_map/scatter-add | solution.py:60
  227.7 0.8 copy-done.21
  228.5 85.3 %reduce-scatter.2.cloned.1.call-done = f32[4,8,128]{2,1,0:T(8,128)} async-done(((f32[128,8,128]{2,1,0:T(8,128)}), f32[4,8,128]{2,1,0:T(8,128)}) %reduce-scatter.2.cloned.1.call-update) | async-done | bytes 16400 | tf_op jit(solution)/shard_map/reduce_scatter | solution.py:133
  (111 shorter events, 1.2 us)
Async XLA Ops:
  6.5 12.5 %copy-start = (f32[4,64,8,128]{3,2,1,0:T(8,128)S(1)}, f32[4,64,8,128]{3,2,1,0:T(8,128)}, u32[]{:S(2)}) copy-start(f32[4,64,8,128]{3,2,1,0:T(8,128)} %param.13) | copy-start | bytes 3145732
  6.5 307.3 %reduce-scatter.2.cloned.1.call-start = ((), (), s32[]{:S(2)}) async-start(), calls=%async_computation.1 | async-start | bytes 540672 | tf_op jit(solution)/shard_map/reduce_scatter | solution.py:133
  7.6 107.3 %collective-permute-start = (f32[64,128]{1,0:T(8,128)S(1)}, f32[64,128]{1,0:T(8,128)S(1)}, u32[]{:S(2)}, u32[]{:S(2)}) collective-permute-start(f32[64,128]{1,0:T(8,128)S(1)} %bitcast.228), channel_id=1, source_target_pairs={{1,0},{2,1},{3,2},{4,3},{5,4},{6,5},{7,6},{9,8},{10,9},{11,10},{12... | collective-permute-start | bytes 98312 | tf_op jit(solution)/shard_map/ppermute | solution.py:12
  12.1 106.4 %collective-permute-start.8 = (f32[64,128]{1,0:T(8,128)S(1)}, f32[64,128]{1,0:T(8,128)S(1)}, u32[]{:S(2)}, u32[]{:S(2)}) collective-permute-start(f32[64,128]{1,0:T(8,128)S(1)} %bitcast.227), channel_id=1, source_target_pairs={{0,1},{1,2},{2,3},{3,4},{4,5},{5,6},{6,7},{8,9},{9,10},{10,11},{11... | collective-permute-start | bytes 98312 | tf_op jit(solution)/shard_map/ppermute | solution.py:12
  19.1 0.7 copy-start.25
  19.8 49.1 %copy-start.26 = (f32[4,8,128]{2,1,0:T(8,128)S(1)}, f32[4,8,128]{2,1,0:T(8,128)}, u32[]{:S(2)}) copy-start(f32[4,8,128]{2,1,0:T(8,128)} %param.9) | copy-start | bytes 49156
  112.1 0.7 copy-start.27
  112.1 0.7 copy-start.29
  113.1 0.7 copy-start.31
  115.0 3.6 %copy-start.22 = (f32[128,8,128]{2,1,0:T(8,128)S(1)}, f32[128,8,128]{2,1,0:T(8,128)}, u32[]{:S(2)}) copy-start(f32[128,8,128]{2,1,0:T(8,128)} %all_gather.7) | copy-start | bytes 1572868
  115.0 3.6 %copy-start.23 = (f32[64,8,128]{2,1,0:T(8,128)S(1)}, f32[64,8,128]{2,1,0:T(8,128)}, u32[]{:S(2)}) copy-start(f32[64,8,128]{2,1,0:T(8,128)} %get-tuple-element.17) | copy-start | bytes 786436
  115.0 3.6 %copy-start.24 = (f32[63,8,128]{2,1,0:T(8,128)S(1)}, f32[63,8,128]{2,1,0:T(8,128)}, u32[]{:S(2)}) copy-start(f32[63,8,128]{2,1,0:T(8,128)} %slice_bitcast_fusion.3) | copy-start | bytes 774148
  116.5 5.9 %copy-start.12 = (f32[64,8,128]{2,1,0:T(8,128)}, f32[64,8,128]{2,1,0:T(8,128)S(1)}, u32[]{:S(2)}) copy-start(f32[64,8,128]{2,1,0:T(8,128)S(1)} %get-tuple-element.14) | copy-start | bytes 786436
  116.6 5.8 %collective-permute-start.1 = (f32[64,128]{1,0:T(8,128)S(1)}, f32[64,128]{1,0:T(8,128)S(1)}, u32[]{:S(2)}, u32[]{:S(2)}) collective-permute-start(f32[64,128]{1,0:T(8,128)S(1)} %bitcast.232), channel_id=1, source_target_pairs={{0,1},{1,2},{2,3},{3,4},{4,5},{5,6},{6,7},{8,9},{9,10},{10,11},{11... | collective-permute-start | bytes 98312 | tf_op jit(solution)/shard_map/ppermute | solution.py:12
  125.0 7.9 %collective-permute-start.2 = (f32[64,128]{1,0:T(8,128)S(1)}, f32[64,128]{1,0:T(8,128)S(1)}, u32[]{:S(2)}, u32[]{:S(2)}) collective-permute-start(f32[64,128]{1,0:T(8,128)S(1)} %bitcast.238), channel_id=1, source_target_pairs={{1,0},{2,1},{3,2},{4,3},{5,4},{6,5},{7,6},{9,8},{10,9},{11,10},{12... | collective-permute-start | bytes 98312 | tf_op jit(solution)/shard_map/ppermute | solution.py:12
  127.1 5.8 %copy-start.13 = (f32[64,8,128]{2,1,0:T(8,128)S(1)}, f32[64,8,128]{2,1,0:T(8,128)}, u32[]{:S(2)}) copy-start(f32[64,8,128]{2,1,0:T(8,128)} %copy-done.12) | copy-start | bytes 786436
  133.1 5.9 %copy-start.14 = (f32[64,8,128]{2,1,0:T(8,128)}, f32[64,8,128]{2,1,0:T(8,128)S(1)}, u32[]{:S(2)}) copy-start(f32[64,8,128]{2,1,0:T(8,128)S(1)} %get-tuple-element.25) | copy-start | bytes 786436
  133.2 5.8 %collective-permute-start.3 = (f32[64,128]{1,0:T(8,128)S(1)}, f32[64,128]{1,0:T(8,128)S(1)}, u32[]{:S(2)}, u32[]{:S(2)}) collective-permute-start(f32[64,128]{1,0:T(8,128)S(1)} %bitcast.241), channel_id=1, source_target_pairs={{0,1},{1,2},{2,3},{3,4},{4,5},{5,6},{6,7},{8,9},{9,10},{10,11},{11... | collective-permute-start | bytes 98312 | tf_op jit(solution)/shard_map/ppermute | solution.py:12
  140.7 7.9 %collective-permute-start.4 = (f32[64,128]{1,0:T(8,128)S(1)}, f32[64,128]{1,0:T(8,128)S(1)}, u32[]{:S(2)}, u32[]{:S(2)}) collective-permute-start(f32[64,128]{1,0:T(8,128)S(1)} %bitcast.239), channel_id=1, source_target_pairs={{1,0},{2,1},{3,2},{4,3},{5,4},{6,5},{7,6},{9,8},{10,9},{11,10},{12... | collective-permute-start | bytes 98312 | tf_op jit(solution)/shard_map/ppermute | solution.py:12
  142.8 5.8 %copy-start.15 = (f32[64,8,128]{2,1,0:T(8,128)S(1)}, f32[64,8,128]{2,1,0:T(8,128)}, u32[]{:S(2)}) copy-start(f32[64,8,128]{2,1,0:T(8,128)} %copy-done.14) | copy-start | bytes 786436
  148.8 6.2 %copy-start.3 = (f32[64,8,128]{2,1,0:T(8,128)}, f32[64,8,128]{2,1,0:T(8,128)S(1)}, u32[]{:S(2)}) copy-start(f32[64,8,128]{2,1,0:T(8,128)S(1)} %get-tuple-element.23) | copy-start | bytes 786436
  148.8 6.2 %copy-start.6 = (f32[64,8,128]{2,1,0:T(8,128)}, f32[64,8,128]{2,1,0:T(8,128)S(1)}, u32[]{:S(2)}) copy-start(f32[64,8,128]{2,1,0:T(8,128)S(1)} %get-tuple-element.22) | copy-start | bytes 786436
  148.8 2.1 copy-start.28
  148.9 2.1 copy-start.30
  148.9 6.1 %collective-permute-start.5 = (f32[64,128]{1,0:T(8,128)S(1)}, f32[64,128]{1,0:T(8,128)S(1)}, u32[]{:S(2)}, u32[]{:S(2)}) collective-permute-start(f32[64,128]{1,0:T(8,128)S(1)} %bitcast.234), channel_id=1, source_target_pairs={{0,1},{1,2},{2,3},{3,4},{4,5},{5,6},{6,7},{8,9},{9,10},{10,11},{11... | collective-permute-start | bytes 98312 | tf_op jit(solution)/shard_map/ppermute | solution.py:12
  151.0 8.2 %collective-permute-start.9 = (f32[64,128]{1,0:T(8,128)S(1)}, f32[64,128]{1,0:T(8,128)S(1)}, u32[]{:S(2)}, u32[]{:S(2)}) collective-permute-start(f32[64,128]{1,0:T(8,128)S(1)} %bitcast.229), channel_id=1, source_target_pairs={{1,0},{2,1},{3,2},{4,3},{5,4},{6,5},{7,6},{9,8},{10,9},{11,10},{12... | collective-permute-start | bytes 98312 | tf_op jit(solution)/shard_map/ppermute | solution.py:12
  156.7 7.9 %collective-permute-start.6 = (f32[64,128]{1,0:T(8,128)S(1)}, f32[64,128]{1,0:T(8,128)S(1)}, u32[]{:S(2)}, u32[]{:S(2)}) collective-permute-start(f32[64,128]{1,0:T(8,128)S(1)} %bitcast.231), channel_id=1, source_target_pairs={{1,0},{2,1},{3,2},{4,3},{5,4},{6,5},{7,6},{9,8},{10,9},{11,10},{12... | collective-permute-start | bytes 98312 | tf_op jit(solution)/shard_map/ppermute | solution.py:12
  158.8 5.8 %copy-start.7 = (f32[64,8,128]{2,1,0:T(8,128)S(1)}, f32[64,8,128]{2,1,0:T(8,128)}, u32[]{:S(2)}) copy-start(f32[64,8,128]{2,1,0:T(8,128)} %copy-done.6) | copy-start | bytes 786436
  159.0 5.6 %copy-start.4 = (f32[64,8,128]{2,1,0:T(8,128)S(1)}, f32[64,8,128]{2,1,0:T(8,128)}, u32[]{:S(2)}) copy-start(f32[64,8,128]{2,1,0:T(8,128)} %copy-done.3) | copy-start | bytes 786436
  165.8 2.0 copy-start.1
  165.8 2.0 copy-start.8
  165.9 10.1 %collective-permute-start.10 = (f32[64,128]{1,0:T(8,128)S(1)}, f32[64,128]{1,0:T(8,128)S(1)}, u32[]{:S(2)}, u32[]{:S(2)}) collective-permute-start(f32[64,128]{1,0:T(8,128)S(1)} %bitcast.237), channel_id=1, source_target_pairs={{0,1},{1,2},{2,3},{3,4},{4,5},{5,6},{6,7},{8,9},{9,10},{10,11},{11... | collective-permute-start | bytes 98312 | tf_op jit(solution)/shard_map/ppermute | solution.py:12
  167.9 8.1 %copy-start.2 = (f32[64,8,128]{2,1,0:T(8,128)S(1)}, f32[64,8,128]{2,1,0:T(8,128)}, u32[]{:S(2)}) copy-start(f32[64,8,128]{2,1,0:T(8,128)} %copy-done.1) | copy-start | bytes 786436
  167.9 8.1 %copy-start.5 = (f32[64,8,128]{2,1,0:T(8,128)S(1)}, f32[64,8,128]{2,1,0:T(8,128)}, u32[]{:S(2)}) copy-start(f32[64,8,128]{2,1,0:T(8,128)} %get-tuple-element.35) | copy-start | bytes 786436
  167.9 8.1 %copy-start.9 = (f32[64,8,128]{2,1,0:T(8,128)S(1)}, f32[64,8,128]{2,1,0:T(8,128)}, u32[]{:S(2)}) copy-start(f32[64,8,128]{2,1,0:T(8,128)} %copy-done.8) | copy-start | bytes 786436
  176.1 9.1 %collective-permute-start.11 = (f32[64,128]{1,0:T(8,128)S(1)}, f32[64,128]{1,0:T(8,128)S(1)}, u32[]{:S(2)}, u32[]{:S(2)}) collective-permute-start(f32[64,128]{1,0:T(8,128)S(1)} %bitcast.236), channel_id=1, source_target_pairs={{1,0},{2,1},{3,2},{4,3},{5,4},{6,5},{7,6},{9,8},{10,9},{11,10},{12... | collective-permute-start | bytes 98312 | tf_op jit(solution)/shard_map/ppermute | solution.py:12
  181.0 15.9 %collective-permute-start.7 = (f32[64,128]{1,0:T(8,128)S(1)}, f32[64,128]{1,0:T(8,128)S(1)}, u32[]{:S(2)}, u32[]{:S(2)}) collective-permute-start(f32[64,128]{1,0:T(8,128)S(1)} %bitcast.230), channel_id=1, source_target_pairs={{0,1},{1,2},{2,3},{3,4},{4,5},{5,6},{6,7},{8,9},{9,10},{10,11},{11... | collective-permute-start | bytes 98312 | tf_op jit(solution)/shard_map/ppermute | solution.py:12
  185.3 2.2 copy-start.19
  185.5 2.7 copy-start.10
  185.5 11.4 %collective-permute-start.12 = (f32[64,128]{1,0:T(8,128)S(1)}, f32[64,128]{1,0:T(8,128)S(1)}, u32[]{:S(2)}, u32[]{:S(2)}) collective-permute-start(f32[64,128]{1,0:T(8,128)S(1)} %bitcast.235), channel_id=1, source_target_pairs={{0,1},{1,2},{2,3},{3,4},{4,5},{5,6},{6,7},{8,9},{9,10},{10,11},{11... | collective-permute-start | bytes 98312 | tf_op jit(solution)/shard_map/ppermute | solution.py:12
  188.9 8.0 %copy-start.11 = (f32[64,8,128]{2,1,0:T(8,128)S(1)}, f32[64,8,128]{2,1,0:T(8,128)}, u32[]{:S(2)}) copy-start(f32[64,8,128]{2,1,0:T(8,128)} %copy-done.10) | copy-start | bytes 786436
  198.8 7.9 %collective-permute-start.13 = (f32[64,128]{1,0:T(8,128)S(1)}, f32[64,128]{1,0:T(8,128)S(1)}, u32[]{:S(2)}, u32[]{:S(2)}) collective-permute-start(f32[64,128]{1,0:T(8,128)S(1)} %bitcast.240), channel_id=1, source_target_pairs={{1,0},{2,1},{3,2},{4,3},{5,4},{6,5},{7,6},{9,8},{10,9},{11,10},{12... | collective-permute-start | bytes 98312 | tf_op jit(solution)/shard_map/ppermute | solution.py:12
  207.7 2.1 copy-start.16
  207.7 11.7 %collective-permute-start.14 = (f32[64,128]{1,0:T(8,128)S(1)}, f32[64,128]{1,0:T(8,128)S(1)}, u32[]{:S(2)}, u32[]{:S(2)}) collective-permute-start(f32[64,128]{1,0:T(8,128)S(1)} %bitcast.233), channel_id=1, source_target_pairs={{0,1},{1,2},{2,3},{3,4},{4,5},{5,6},{6,7},{8,9},{9,10},{10,11},{11... | collective-permute-start | bytes 98312 | tf_op jit(solution)/shard_map/ppermute | solution.py:12
  209.8 1.5 copy-start.20
  211.3 8.0 %copy-start.17 = (f32[64,8,128]{2,1,0:T(8,128)S(1)}, f32[64,8,128]{2,1,0:T(8,128)}, u32[]{:S(2)}) copy-start(f32[64,8,128]{2,1,0:T(8,128)} %copy-done.16) | copy-start | bytes 786436
  211.3 8.0 %copy-start.18 = (f32[64,8,128]{2,1,0:T(8,128)S(1)}, f32[64,8,128]{2,1,0:T(8,128)}, u32[]{:S(2)}) copy-start(f32[64,8,128]{2,1,0:T(8,128)} %get-tuple-element.29) | copy-start | bytes 786436
  227.7 0.8 copy-start.21
Sparse Core Ops, SparseCore 0:
  228.7 85.1 reduce-scatter.1
where the time goes:
time: 322 us; the launch traced here: 321 us
  waiting for transfers between devices  114 us (35%)
  blocking collectives  92.3 us (29%)
  other arithmetic  46.1 us (14%)
  starting transfers between devices  41.4 us (13%)
  between operations  15 us (5%)
  local copies, waits for them, and re-layouts  12.1 us (4%)
    reduce_scatter x1, waiting for transfers between devices, local(): stacked = lax.psum_scatter(column, 'shot', scatter_dimension=0, tiled=True)  85.3 us
    all_gather x1, blocking collectives, local(): lax.all_gather(density, 'shot', axis=0, tiled=True)  49.1 us
    all_gather x1, blocking collectives, local(): lax.all_gather(velocity, 'shot', axis=0, tiled=True)  43.2 us
    ppermute x15, starting transfers between devices, shifted(): return lax.ppermute(block, axis, route)  41.4 us
    scatter-add x8, other arithmetic, inject_points(): pressure.at[cell_x, jnp.clip(local_y, 0, block_cols - 1), cell_z]  37.9 us
    ppermute x15, waiting for transfers between devices, shifted(): return lax.ppermute(block, axis, route)  28.4 us
  transfers between devices with their start and end apart: 16, of which 8 were waited for; matrix products, arithmetic and copies ran while one was open for 12% of the time, Pallas kernels for 0%

commit v1 on v0

v1 whole, which is shorter than its diff:
```python
import functools

import jax
import jax.numpy as jnp
from jax import lax
from jax.experimental import pallas as pl
from jax.experimental.pallas import tpu as pltpu
from jax.sharding import PartitionSpec as P

STEPS = 4
UNROLL = 2
F32 = jnp.float32
ROWS = 64
COLS = 8
DEPTH = 128
PLANES = COLS + 2 * STEPS
NX, NZH, NC, NT = 4, 4, 2, 8

VMEM = pl.BlockSpec(memory_space=pltpu.VMEM)
SMEM = pl.BlockSpec(memory_space=pltpu.SMEM)
ANY = pl.BlockSpec(memory_space=pl.ANY)


def shape(*dims):
    return jax.ShapeDtypeStruct(dims, F32)


def params(mib):
    return pltpu.CompilerParams(vmem_limit_bytes=mib * 1024 * 1024)


def place():
    shot = lax.axis_index("shot")
    return shot // (NZH * NC), (shot // NC) % NZH, shot % NC, shot


def pack_kernel(src, rcv, own, to_prev, to_next):
    lane = lax.broadcasted_iota(jnp.int32, (COLS, DEPTH), 1)
    col = lax.broadcasted_iota(jnp.int32, (COLS, DEPTH), 0)

    def row(x, before):
        after = []
        for f, state in enumerate((src, rcv)):
            p, vx, vy, vz = (state[i, x] for i in range(4))
            spread = vx - before[f]
            spread += vy - jnp.where(col == 0, 0.0, pltpu.roll(vy, 1, 0))
            spread += vz - jnp.where(lane == 0, 0.0, pltpu.roll(vz, 1, 1))
            own[2 * f, pl.ds(x, COLS, stride=ROWS), :] = p
            own[2 * f + 1, pl.ds(x, COLS, stride=ROWS), :] = spread
            last = (COLS - 1)
            to_next[7 + 8 * f - f, pl.ds(x, 1), :] = vy[last:, :]
            after.append(vx)
        return tuple(after)

    zero = jnp.zeros((COLS, DEPTH), F32)
    lax.fori_loop(0, ROWS, row, (zero, zero), unroll=4)

    def plane(f, y):
        return own[f, y * ROWS : (y + 1) * ROWS, :]

    for i, (f, y) in enumerate(
        [(0, 0), (0, 1), (0, 2), (0, 3), (1, 0), (1, 1), (1, 2)]
        + [(2, 0), (2, 1), (2, 2), (3, 0), (3, 1), (3, 2)]
    ):
        to_prev[i] = plane(f, y)
    for i, (f, y) in (
        list(enumerate([(0, 4), (0, 5), (0, 6), (0, 7), (1, 5), (1, 6), (1, 7)]))
        + list(enumerate([(2, 5), (2, 6), (2, 7), (3, 5), (3, 6), (3, 7)], 8))
    ):
        to_next[i] = plane(f, y)


def inject_kernel(src_pos, wavelet, rec_pos, traces, src_out, rec_out):
    src_out[...] = jnp.zeros(src_out.shape, F32)
    rec_out[...] = jnp.zeros(rec_out.shape, F32)
    first = lax.axis_index("tile") * COLS - STEPS
    lane = lax.broadcasted_iota(jnp.int32, (1, DEPTH), 1)
    for pos, amp, out in ((src_pos, wavelet, src_out), (rec_pos, traces, rec_out)):

        def point(k, _, pos=pos, amp=amp, out=out):
            cell = pos[0, k]
            x = cell // (COLS * NT * DEPTH)
            y = (cell // DEPTH) % (COLS * NT) - first
            hit = lane == cell % DEPTH

            @pl.when((y >= 0) & (y < PLANES))
            def _():
                old = [out[s, y, pl.ds(x, 1), :] for s in range(STEPS)]
                for s in range(STEPS):
                    out[s, y, pl.ds(x, 1), :] = old[s] + jnp.where(hit, amp[0, k, s], 0.0)

            return 0

        lax.fori_loop(0, pos.shape[1], point, 0)


def window_kernel(anchors, a0, a1, a2, a3, own, other, strips, sem):
    copies = [pltpu.make_async_copy(a, strips.at[d], sem.at[d]) for d, a in enumerate((a0, a1, a2, a3))]
    for copy in copies:
        copy.start()
    x, z, c, g = place()
    for copy in copies:
        copy.wait()
    for group, out in ((g, own), (g + 1 - 2 * c, other)):
        b = anchors[group]
        first = (b + (c + b) % 2) // 2
        for i in range(8):
            j = first + i
            block = strips.at[(x - j // NZH + NX) % NX, (z - j % NZH + NZH) % NZH]
            vel, den = block[0], block[1]
            out[i, 0] = den * vel * vel
            out[i, 1] = 1.0 / den


def model_kernel(anchors, own, other, out, to_prev, to_next):
    _, _, c, g = place()
    odd = (c + anchors[g]) % 2
    for strips, start in ((own, odd), (other, 1 - odd)):
        for i in range(8):
            for r in range(4):
                x = 4 * (start + 2 * i) + r
                for f in range(2):
                    out[f, pl.ds(x, COLS, stride=ROWS), :] = strips[i, f, r]

    def plane(f, y):
        return out[f, y * ROWS : (y + 1) * ROWS, :]

    for i, (f, y) in enumerate([(0, 0), (0, 1), (0, 2), (1, 0), (1, 1), (1, 2)]):
        to_prev[i] = plane(f, y)
    for i, (f, y) in enumerate([(0, 5), (0, 6), (0, 7), (1, 4), (1, 5), (1, 6), (1, 7)]):
        to_next[i] = plane(f, y)


def march_kernel(
    anchors, own, prev, nxt, mine, model, model_prev, model_next, add_s, add_r,
    keep, send,
    ps, pr, ds, dr, mod, buoy, corr,
):
    vy = (prev.at[7], prev.at[14], mine.at[7], mine.at[14])
    ps[0, 0:4] = prev[0:4]
    ps[0, 4:12] = own[0]
    ps[0, 12:16] = nxt[0:4]
    pr[0, 1:4] = prev[8:11]
    pr[0, 4:12] = own[2]
    pr[0, 12:15] = nxt[7:10]
    for d, f, at, after in ((ds, 0, 4, 4), (dr, 1, 11, 10)):
        d[1:4] = prev[at : at + 3]
        d[4] = own[2 * f + 1, 0] - vy[f][...]
        d[5:12] = own[2 * f + 1, 1:8]
        d[12] = nxt[after] - vy[2 + f][...]
        d[13:15] = nxt[after + 1 : after + 3]
    mod[1:4] = model_prev[0:3]
    mod[4:12] = model[0]
    mod[12:15] = model_next[0:3]
    buoy[0:4] = model_prev[3:7]
    buoy[4:12] = model[1]
    buoy[12:15] = model_next[3:6]
    keep[...] = jnp.zeros(keep.shape, F32)
    send[...] = jnp.zeros(send.shape, F32)

    lane = lax.broadcasted_iota(jnp.int32, (8, DEPTH), 1)
    row = lax.broadcasted_iota(jnp.int32, (8, DEPTH), 0)
    first_lane, last_lane, first_row, last_row = lane == 0, lane == DEPTH - 1, row == 0, row == 7
    blocks = range(ROWS // 8)
    zero = jnp.zeros((8, DEPTH), F32)

    def get(ref, *at):
        return [ref[(*at, slice(8 * v, 8 * v + 8))] for v in blocks]

    def spread_of(p, after, before, b):
        down = [pltpu.roll(p[v], 7, 0) for v in blocks] + [zero]
        flux_y = [b[v] * (after[v] - p[v]) for v in blocks]
        out, last = [], zero
        for v in blocks:
            flux_x = b[v] * (jnp.where(last_row, down[v + 1], down[v]) - p[v])
            flux_z = b[v] * (jnp.where(last_lane, 0.0, pltpu.roll(p[v], DEPTH - 1, 1)) - p[v])
            turned = pltpu.roll(flux_x, 1, 0)
            spread = (flux_x - jnp.where(first_row, last, turned)) + (flux_y[v] - before[v])
            spread += flux_z - jnp.where(first_lane, 0.0, pltpu.roll(flux_z, 1, 1))
            last = turned
            out.append(spread)
        return out, flux_y

    def plane(s, y, carry):
        m, b = get(mod, y), get(buoy, y)
        fields = ((ps, ds, add_s, s), (pr, dr, add_r, STEPS - s)) if s else ((ps, ds, add_s, 0),)
        new, ends = [], []
        for (p_all, d_all, add, amp), (p, before) in zip(fields, carry):
            after = get(p_all, s, y + 1)
            spread, flux = spread_of(p, after, before, b)
            ends.append((after, flux))
            out = []
            for v in blocks:
                cut = slice(8 * v, 8 * v + 8)
                d = d_all[y, cut] - spread[v]
                out.append(p[v] + add[amp, y, cut] - m[v] * d)
                if s < STEPS - 1:
                    d_all[y, cut] = d
                    p_all[s + 1, y, cut] = out[v]
            new.append(out)
        if s == 0:
            for v in blocks:
                cut = slice(8 * v, 8 * v + 8)
                pr[1, y, cut] = pr[0, y, cut] - m[v] * dr[y, cut]
        if s == STEPS - 1:
            for v in blocks:
                cut = slice(8 * v, 8 * v + 8)
                image = new[0][v] * (pr[1, y, cut] + add_r[3, y, cut])
                image += ps[3, y, cut] * (pr[2, y, cut] + add_r[2, y, cut])
                image += ps[2, y, cut] * (pr[3, y, cut] + add_r[1, y, cut])
                image += ps[1, y, cut] * (new[1][v] + add_r[0, y, cut])
                corr[pl.ds(8 * COLS * v + y - STEPS, 8, stride=COLS), :] = image / STEPS
        return ends

    for s in range(STEPS):
        low, high = s + 1, 15 - s
        carry = []
        for p_all in (ps, pr) if s else (ps,):
            here, before, b = get(p_all, s, low), get(p_all, s, low - 1), get(buoy, low - 1)
            carry.append((here, [b[v] * (here[v] - before[v]) for v in blocks]))

        def planes(i, carry, s=s, low=low):
            for u in range(UNROLL):
                carry = plane(s, low + UNROLL * i + u, carry)
            return carry

        lax.fori_loop(0, (high - low) // UNROLL, planes, carry)

    _, _, c, g = place()
    b = anchors[g]
    odd = (c + b) % 2
    for out, start in ((keep, odd), (send, 1 - odd)):
        at = (b + start) // 2
        for i in range(8):
            out[at + i] = corr[pl.ds(pl.multiple_of(32 * (start + 2 * i), 32), 32), :]


def march(*operands):
    plane = (ROWS, DEPTH)
    return pl.pallas_call(
        march_kernel,
        out_shape=[shape(16, 32, DEPTH)] * 2,
        in_specs=[SMEM] + [VMEM] * 9,
        out_specs=[VMEM] * 2,
        scratch_shapes=[
            pltpu.VMEM((STEPS, PLANES, *plane), F32),
            pltpu.VMEM((STEPS, PLANES, *plane), F32),
            pltpu.VMEM((PLANES, *plane), F32),
            pltpu.VMEM((PLANES, *plane), F32),
            pltpu.VMEM((PLANES, *plane), F32),
            pltpu.VMEM((PLANES, *plane), F32),
            pltpu.VMEM((COLS * ROWS, DEPTH), F32),
        ],
        compiler_params=params(24),
        name="march",
    )(*operands)


def halve_kernel(keep, got, s0, s1, s2, s3):
    x, _, _, _ = place()
    for d, out in enumerate((s0, s1, s2, s3)):
        at = ((x + d) % NX) * NZH
        for i in range(NZH):
            out[i] = keep[at + i] + got[at + i]


def quarter_kernel(s0, r1, r2, r3, u0, u1, u2, u3):
    _, z, _, _ = place()
    for d, out in enumerate((u0, u1, u2, u3)):
        at = (z + d) % NZH
        out[...] = (s0[at] + r1[at]) + (r2[at] + r3[at])


def last_kernel(u0, q1, q2, q3, out):
    out[...] = (u0[...] + q1[...]) + (q2[...] + q3[...])


def along(block, axis, distance):
    route = []
    for s in range(NX * NZH * NC):
        x, z, c = s // (NZH * NC), (s // NC) % NZH, s % NC
        if axis == "x":
            x = (x + distance) % NX
        elif axis == "z":
            z = (z + distance) % NZH
        else:
            c = (c + distance) % NC
        route.append((s, (x * NZH + z) * NC + c))
    return lax.ppermute(block, "shot", route)


def to_tile(block, distance):
    route = [(i, i + distance) for i in range(NT) if 0 <= i + distance < NT]
    return lax.ppermute(block, "tile", route)


def local(velocity, density, anchors, src_state, rcv_state, src_pos, wavelet, rec_pos, traces):
    plane = (ROWS, DEPTH)
    model = jnp.stack([velocity, density])[None]
    zs = [along(model, "z", d) for d in range(1, NZH)]

    own, to_prev, to_next = pl.pallas_call(
        pack_kernel,
        out_shape=[shape(4, COLS * ROWS, DEPTH), shape(13, *plane), shape(15, *plane)],
        in_specs=[VMEM, VMEM],
        out_specs=[VMEM] * 3,
        compiler_params=params(16),
        name="pack",
    )(src_state, rcv_state)

    xs = [jnp.concatenate([model, *zs])]
    xs += [along(xs[0], "x", d) for d in range(1, NX)]

    halo_next = to_tile(to_prev, -1)
    halo_prev = to_tile(to_next, 1)

    inj_src, inj_rec = pl.pallas_call(
        inject_kernel,
        out_shape=[shape(STEPS, PLANES, *plane)] * 2,
        in_specs=[SMEM] * 4,
        out_specs=[VMEM] * 2,
        compiler_params=params(16),
        name="inject",
    )(src_pos, wavelet, rec_pos, traces)

    strips = (8, 2, 4, COLS, DEPTH)
    mine, other = pl.pallas_call(
        window_kernel,
        out_shape=[shape(*strips)] * 2,
        in_specs=[SMEM] + [ANY] * 4,
        out_specs=[VMEM] * 2,
        scratch_shapes=[
            pltpu.VMEM((NX, NZH, 2, 4, COLS, DEPTH), F32),
            pltpu.SemaphoreType.DMA((NX,)),
        ],
        compiler_params=params(16),
        name="window",
    )(anchors, *xs)
    got = along(other, "core", 1)

    mb, mb_prev, mb_next = pl.pallas_call(
        model_kernel,
        out_shape=[shape(2, COLS * ROWS, DEPTH), shape(6, *plane), shape(7, *plane)],
        in_specs=[SMEM, VMEM, VMEM],
        out_specs=[VMEM] * 3,
        compiler_params=params(16),
        name="model",
    )(anchors, mine, got)
    model_next = to_tile(mb_prev, -1)
    model_prev = to_tile(mb_next, 1)

    keep, send = march(
        anchors,
        own.reshape(4, COLS, *plane),
        halo_prev,
        halo_next,
        to_next,
        mb.reshape(2, COLS, *plane),
        model_prev,
        model_next,
        inj_src,
        inj_rec,
    )

    received = along(send, "core", 1)
    parts = pl.pallas_call(
        halve_kernel,
        out_shape=[shape(NZH, 32, DEPTH)] * NX,
        in_specs=[VMEM] * 2,
        out_specs=[VMEM] * NX,
        compiler_params=params(8),
        name="halve",
    )(keep, received)
    moved = [along(parts[d], "x", d) for d in range(1, NX)]
    parts = pl.pallas_call(
        quarter_kernel,
        out_shape=[shape(32, DEPTH)] * NZH,
        in_specs=[VMEM] * NX,
        out_specs=[VMEM] * NZH,
        compiler_params=params(8),
        name="quarter",
    )(parts[0], *moved)
    moved = [along(parts[d], "z", d) for d in range(1, NZH)]
    image = pl.pallas_call(
        last_kernel,
        out_shape=shape(32, DEPTH),
        in_specs=[VMEM] * NZH,
        out_specs=VMEM,
        compiler_params=params(8),
        name="last",
    )(parts[0], *moved)
    return image.reshape(4, COLS, DEPTH)


def solution(mesh):
    return jax.shard_map(
        local,
        mesh=mesh,
        in_specs=(
            P("shot", "tile", None),
            P("shot", "tile", None),
            P(),
            P(None, "shot", "tile", None),
            P(None, "shot", "tile", None),
            P("shot", None),
            P("shot", None, None),
            P("shot", None),
            P("shot", None, None),
        ),
        out_specs=P("shot", "tile", None),
        check_vma=False,
    )
```

time: 322 us -> 75.4 us (0.23)
  waiting for transfers between devices: 114 us -> 14.7 us
  blocking collectives: 92.3 us -> 0 us
  other arithmetic: 46.1 us -> 0.8 us
  Pallas kernels: 0 us -> 17.3 us
  between operations: 15 us -> 0.17 us
  local copies, waits for them, and re-layouts: 12.1 us -> 2.66 us
    all_gather x2 -> x0, blocking collectives: 92.3 us -> none  [the longest x1 49.1 us: local(): lax.all_gather(density, 'shot', axis=0, tiled=True)]
    reduce_scatter x1 -> x0, waiting for transfers between devices: 85.3 us -> none  [local(): stacked = lax.psum_scatter(column, 'shot', scatter_dimension=0, tiled=True)]
    scatter-add x8 -> x0, other arithmetic: 37.9 us -> none  [inject_points(): pressure.at[cell_x, jnp.clip(local_y, 0, block_cols - 1), cell_z]]
    pallas_call x0 -> x8, Pallas kernels: none -> 17.3 us  [the longest x1 6.15 us: local(): pl.pallas_call(inject_kernel, out_shape=[shape(STEPS, PLANES, *plane)] *...]
    ppermute x15 -> x18, waiting for transfers between devices: 28.4 us -> 14.7 us  [the longest x14 12.3 us: along(): return lax.ppermute(block, 'shot', route)]
    sub x13 -> x0, other arithmetic: 8.01 us -> none  [the longest x6 4.29 us: velocity_core(): vel_x = vel_x - buoyancy * (next_cell(pressure, 0) - pressure)]
    slice x44 -> x0, local copies, waits for them, and re-layouts: 6.43 us -> none  [the longest x14 2.67 us: next_cell(): remainder = lax.slice_in_dim(field, 1, length, axis=dimension)]
    ppermute x15 -> x18, starting transfers between devices: 41.4 us -> 39.3 us  [the longest x14 27 us: along(): return lax.ppermute(block, 'shot', route)]
  transfers between devices with their start and end apart: 16 -> 18, of which waited for: 8 -> 7; matrix products, arithmetic and copies ran while one was open for 12% -> 0% of each run, Pallas kernels for 0% -> 14%
where the time goes in v1:
time: 75.4 us; the launch traced here: 74.9 us
  starting transfers between devices  39.3 us (52%)
  Pallas kernels  17.3 us (23%)
  waiting for transfers between devices  14.7 us (19%)
  local copies, waits for them, and re-layouts  2.66 us (4%)
  other arithmetic  0.8 us (1%)
    ppermute x14, starting transfers between devices, along(): return lax.ppermute(block, 'shot', route)  27 us
    ppermute x14, waiting for transfers between devices, along(): return lax.ppermute(block, 'shot', route)  12.3 us
    ppermute x4, starting transfers between devices, to_tile(): return lax.ppermute(block, 'tile', route)  12.3 us
    pallas_call x1, Pallas kernels, local(): pl.pallas_call(inject_kernel, out_shape=[shape(STEPS, PLANES, *plane)] *...  6.15 us
    pallas_call x1, Pallas kernels, march(): pl.pallas_call(march_kernel, out_shape=[shape(16, 32, DEPTH)] * 2, in_spe...  4.78 us
    unnamed x16, local copies, waits for them, and re-layouts  2.66 us
    pallas_call x1, Pallas kernels, local(): pl.pallas_call(pack_kernel, out_shape=[shape(4, COLS * ROWS, DEPTH), shap...  2.44 us
    ppermute x4, waiting for transfers between devices, to_tile(): return lax.ppermute(block, 'tile', route)  2.35 us
  transfers between devices with their start and end apart: 18, of which 7 were waited for; matrix products, arithmetic and copies ran while one was open for 0% of the time, Pallas kernels for 14%

profile of v1, /device:TPU:24, one launch (start us, length us, event | category | flops | bytes accessed | tf_op | source)
XLA Modules:
  0.0 74.9 jit_solution(17141840933020982505)
XLA Ops:
  0.0 0.0 copy-start.2
  0.0 0.0 copy-start.5
  0.0 0.0 copy-start.6
  0.0 0.0 copy-start.4
  0.0 0.0 copy-start.3
  0.0 0.8 %maximum_bitcast_fusion = f32[1,2,4,8,128]{4,3,2,1,0:T(8,128)S(1)} fusion(f32[1,4,8,128]{3,2,1,0:T(8,128)} %bitcast.9, f32[1,4,8,128]{3,2,1,0:T(8,128)} %bitcast.10), kind=kLoop, calls=%fused_computation.1 | loop fusion | flops 8192 | bytes 65536 | tf_op jit(solution)/shard_map/broadcast_in_dim | solution.py:299
  0.8 6.3 %collective-permute-start.4 = (f32[1,2,4,8,128]{4,3,2,1,0:T(8,128)S(1)}, f32[1,2,4,8,128]{4,3,2,1,0:T(8,128)S(1)}, u32[]{:S(2)}, u32[]{:S(2)}) collective-permute-start(f32[1,2,4,8,128]{4,3,2,1,0:T(8,128)S(1)} %maximum_bitcast_fusion), channel_id=1, source_target_pairs={{0,48},{8,56},{16,0},{24,8},{32,16},{40,24},{48,32},{56,40},{64,11... | collective-permute-start | bytes 98312 | tf_op jit(solution)/shard_map/ppermute | solution.py:289
  7.1 0.9 %collective-permute-start.3 = (f32[1,2,4,8,128]{4,3,2,1,0:T(8,128)S(1)}, f32[1,2,4,8,128]{4,3,2,1,0:T(8,128)S(1)}, u32[]{:S(2)}, u32[]{:S(2)}) collective-permute-start(f32[1,2,4,8,128]{4,3,2,1,0:T(8,128)S(1)} %maximum_bitcast_fusion), channel_id=1, source_target_pairs={{0,32},{8,40},{16,48},{24,56},{32,0},{40,8},{48,16},{56,24},{64,96... | collective-permute-start | bytes 98312 | tf_op jit(solution)/shard_map/ppermute | solution.py:289
  8.0 2.9 %collective-permute-start.2 = (f32[1,2,4,8,128]{4,3,2,1,0:T(8,128)S(1)}, f32[1,2,4,8,128]{4,3,2,1,0:T(8,128)S(1)}, u32[]{:S(2)}, u32[]{:S(2)}) collective-permute-start(f32[1,2,4,8,128]{4,3,2,1,0:T(8,128)S(1)} %maximum_bitcast_fusion), channel_id=1, source_target_pairs={{0,16},{8,24},{16,32},{24,40},{32,48},{40,56},{48,0},{56,8},{64,80... | collective-permute-start | bytes 98312 | tf_op jit(solution)/shard_map/ppermute | solution.py:289
  10.9 0.0 collective-permute-done.4
  10.9 4.2 %collective-permute-done.3 = f32[1,2,4,8,128]{4,3,2,1,0:T(8,128)S(1)} collective-permute-done((f32[1,2,4,8,128]{4,3,2,1,0:T(8,128)S(1)}, f32[1,2,4,8,128]{4,3,2,1,0:T(8,128)S(1)}, u32[]{:S(2)}, u32[]{:S(2)}) %collective-permute-start.3) | collective-permute-done | bytes 32800 | tf_op jit(solution)/shard_map/ppermute | solution.py:289
  15.1 0.0 collective-permute-done.2
  15.1 2.8 %collective-permute-start.7 = (f32[4,2,4,8,128]{4,3,2,1,0:T(8,128)S(1)}, f32[4,2,4,8,128]{4,3,2,1,0:T(8,128)S(1)}, u32[]{:S(2)}, u32[]{:S(2)}) collective-permute-start(f32[4,2,4,8,128]{4,3,2,1,0:T(8,128)S(1)} %pad_maximum_fusion.a0), channel_id=1, source_target_pairs={{0,192},{8,200},{16,208},{24,216},{32,224},{40,232},{48,240},{56,2... | collective-permute-start | bytes 393224 | tf_op jit(solution)/shard_map/ppermute | solution.py:289
  17.9 0.8 %collective-permute-start.6 = (f32[4,2,4,8,128]{4,3,2,1,0:T(8,128)S(1)}, f32[4,2,4,8,128]{4,3,2,1,0:T(8,128)S(1)}, u32[]{:S(2)}, u32[]{:S(2)}) collective-permute-start(f32[4,2,4,8,128]{4,3,2,1,0:T(8,128)S(1)} %pad_maximum_fusion.a0), channel_id=1, source_target_pairs={{0,128},{8,136},{16,144},{24,152},{32,160},{40,168},{48,176},{56,1... | collective-permute-start | bytes 393224 | tf_op jit(solution)/shard_map/ppermute | solution.py:289
  18.7 0.9 %collective-permute-start.5 = (f32[4,2,4,8,128]{4,3,2,1,0:T(8,128)S(1)}, f32[4,2,4,8,128]{4,3,2,1,0:T(8,128)S(1)}, u32[]{:S(2)}, u32[]{:S(2)}) collective-permute-start(f32[4,2,4,8,128]{4,3,2,1,0:T(8,128)S(1)} %pad_maximum_fusion.a0), channel_id=1, source_target_pairs={{0,64},{8,72},{16,80},{24,88},{32,96},{40,104},{48,112},{56,120},{... | collective-permute-start | bytes 393224 | tf_op jit(solution)/shard_map/ppermute | solution.py:289
  19.6 0.0 copy-start
  19.6 1.2 %copy-done = f32[4,64,8,128]{3,2,1,0:T(8,128)S(1)} copy-done((f32[4,64,8,128]{3,2,1,0:T(8,128)S(1)}, f32[4,64,8,128]{3,2,1,0:T(8,128)}, u32[]{:S(2)}) %copy-start) | copy-done | bytes 1048600
  20.9 0.0 copy-start.1
  20.9 1.2 %copy-done.1 = f32[4,64,8,128]{3,2,1,0:T(8,128)S(1)} copy-done((f32[4,64,8,128]{3,2,1,0:T(8,128)S(1)}, f32[4,64,8,128]{3,2,1,0:T(8,128)}, u32[]{:S(2)}) %copy-start.1) | copy-done | bytes 1048600
  22.1 2.4 %pack.1 = (f32[4,512,128]{2,1,0:T(8,128)S(1)}, f32[13,64,128]{2,1,0:T(8,128)}, f32[15,64,128]{2,1,0:T(8,128)S(1)}) custom-call(f32[4,64,8,128]{3,2,1,0:T(8,128)S(1)} %copy-done, f32[4,64,8,128]{3,2,1,0:T(8,128)S(1)} %copy-done.1), custom_call_target="tpu_custom_call" | custom-call | tf_op jit(solution)/shard_map/pack/pallas_call | solution.py:302
  24.5 0.0 collective-permute-done.7.a3
  24.5 0.0 collective-permute-done.6.a2
  24.5 1.3 %collective-permute-done.5.a1 = f32[4,2,4,8,128]{4,3,2,1,0:T(8,128)S(1)} collective-permute-done((f32[4,2,4,8,128]{4,3,2,1,0:T(8,128)S(1)}, f32[4,2,4,8,128]{4,3,2,1,0:T(8,128)S(1)}, u32[]{:S(2)}, u32[]{:S(2)}) %collective-permute-start.5) | collective-permute-done | bytes 131104 | tf_op jit(solution)/shard_map/ppermute | solution.py:289
  25.8 0.0 copy-done.2
  25.8 1.5 %window.1 = (f32[8,2,4,8,128]{4,3,2,1,0:T(8,128)S(1)}, f32[8,2,4,8,128]{4,3,2,1,0:T(8,128)S(1)}) custom-call(s32[32]{0:T(128)S(1)} %copy-done.2, f32[4,2,4,8,128]{4,3,2,1,0:T(8,128)S(1)} %pad_maximum_fusion.a0, f32[4,2,4,8,128]{4,3,2,1,0:T(8,128)S(1)} %collective-permute-done.5.a1, f32[4,2,4,8,128]{4,3,2,1,0:T(8,128)S(1)} %collective-permute-done.6.a2, ...), custom_call_target="tpu_custom_call" | custom-call | tf_op jit(solution)/shard_map/window/pallas_call | solution.py:327
  27.3 0.1 collective-permute-start.8
  27.4 2.4 %collective-permute-start = (f32[15,64,128]{2,1,0:T(8,128)S(1)}, f32[15,64,128]{2,1,0:T(8,128)S(1)}, u32[]{:S(2)}, u32[]{:S(2)}) collective-permute-start(f32[15,64,128]{2,1,0:T(8,128)S(1)} %get-tuple-element.26.mine), channel_id=1, source_target_pairs={{0,1},{1,2},{2,3},{3,4},{4,5},{5,6},{6,7},{8,9},{9,10},{10,11},{11... | collective-permute-start | bytes 1474568 | tf_op jit(solution)/shard_map/ppermute | solution.py:294
  29.9 3.4 %collective-permute-start.1 = (f32[13,64,128]{2,1,0:T(8,128)}, f32[13,64,128]{2,1,0:T(8,128)S(1)}, u32[]{:S(2)}, u32[]{:S(2)}) collective-permute-start(f32[13,64,128]{2,1,0:T(8,128)} %get-tuple-element.27), channel_id=1, source_target_pairs={{1,0},{2,1},{3,2},{4,3},{5,4},{6,5},{7,6},{9,8},{10,9},{11,10},{12... | collective-permute-start | bytes 1277960 | tf_op jit(solution)/shard_map/ppermute | solution.py:294
  33.3 0.0 collective-permute-done.8.other
  33.3 1.8 %model.1 = (f32[2,512,128]{2,1,0:T(8,128)S(1)}, f32[6,64,128]{2,1,0:T(8,128)}, f32[7,64,128]{2,1,0:T(8,128)}) custom-call(s32[32]{0:T(128)S(1)} %copy-done.2, f32[8,2,4,8,128]{4,3,2,1,0:T(8,128)S(1)} %get-tuple-element.28.own, f32[8,2,4,8,128]{4,3,2,1,0:T(8,128)S(1)} %collective-permute-done.8.other), custom_call_target="tpu_custom_call" | custom-call | tf_op jit(solution)/shard_map/model/pallas_call | solution.py:341
  35.1 4.5 %collective-permute-start.9 = (f32[7,64,128]{2,1,0:T(8,128)}, f32[7,64,128]{2,1,0:T(8,128)S(1)}, u32[]{:S(2)}, u32[]{:S(2)}) collective-permute-start(f32[7,64,128]{2,1,0:T(8,128)} %get-tuple-element.31), channel_id=1, source_target_pairs={{0,1},{1,2},{2,3},{3,4},{4,5},{5,6},{6,7},{8,9},{9,10},{10,11},{11... | collective-permute-start | bytes 688136 | tf_op jit(solution)/shard_map/ppermute | solution.py:294
  39.6 1.9 %collective-permute-start.10 = (f32[6,64,128]{2,1,0:T(8,128)}, f32[6,64,128]{2,1,0:T(8,128)S(1)}, u32[]{:S(2)}, u32[]{:S(2)}) collective-permute-start(f32[6,64,128]{2,1,0:T(8,128)} %get-tuple-element.32), channel_id=1, source_target_pairs={{1,0},{2,1},{3,2},{4,3},{5,4},{6,5},{7,6},{9,8},{10,9},{11,10},{12... | collective-permute-start | bytes 589832 | tf_op jit(solution)/shard_map/ppermute | solution.py:294
  41.5 0.0 copy-done.5
  41.5 0.1 copy.10.wavelet
  41.6 0.0 copy-done.6
  41.6 0.1 copy.11.traces
  41.7 0.0 copy-done.4
  41.8 0.0 copy-done.3
  41.8 6.1 %inject.1 = (f32[4,16,64,128]{3,2,1,0:T(8,128)S(1)}, f32[4,16,64,128]{3,2,1,0:T(8,128)S(1)}) custom-call(s32[1,16]{1,0:T(1,128)S(1)} %copy-done.3, f32[1,16,4]{2,1,0:T(8,128)S(1)} %copy.10.wavelet, s32[1,128]{1,0:T(1,128)S(1)} %copy-done.4, f32[1,128,4]{2,1,0:T(8,128)S(1)} %copy.11.traces), custom_call_target="tpu_custom_call" | custom-call | tf_op jit(solution)/shard_map/inject/pallas_call | solution.py:317
  47.9 0.0 collective-permute-done.1.nxt
  47.9 0.0 collective-permute-done.prev
  47.9 2.3 %collective-permute-done.10.model_next = f32[6,64,128]{2,1,0:T(8,128)S(1)} collective-permute-done((f32[6,64,128]{2,1,0:T(8,128)}, f32[6,64,128]{2,1,0:T(8,128)S(1)}, u32[]{:S(2)}, u32[]{:S(2)}) %collective-permute-start.10) | collective-permute-done | bytes 196640 | tf_op jit(solution)/shard_map/ppermute | solution.py:294
  50.3 0.0 collective-permute-done.9.model_prev
  50.3 4.8 %march.1 = (f32[16,32,128]{2,1,0:T(8,128)S(1)}, f32[16,32,128]{2,1,0:T(8,128)S(1)}) custom-call(s32[32]{0:T(128)S(1)} %copy-done.2, f32[4,8,64,128]{3,2,1,0:T(8,128)S(1)} %bitcast.7, f32[15,64,128]{2,1,0:T(8,128)S(1)} %collective-permute-done.prev, f32[13,64,128]{2,1,0:T(8,128)S(1)} %collective-permute-done.1.nxt, ...), custom_call_target="tpu_custom_call" | custom-call | tf_op jit(solution)/shard_map/march/pallas_call | solution.py:240
  55.1 0.1 collective-permute-start.11
  55.2 1.5 %collective-permute-done.11.got = f32[16,32,128]{2,1,0:T(8,128)S(1)} collective-permute-done((f32[16,32,128]{2,1,0:T(8,128)S(1)}, f32[16,32,128]{2,1,0:T(8,128)S(1)}, u32[]{:S(2)}, u32[]{:S(2)}) %collective-permute-start.11) | collective-permute-done | bytes 262176 | tf_op jit(solution)/shard_map/ppermute | solution.py:289
  56.7 0.6 collective-permute-start.12
  57.3 2.0 %collective-permute-start.13 = (f32[4,32,128]{2,1,0:T(8,128)S(1)}, f32[4,32,128]{2,1,0:T(8,128)S(1)}, u32[]{:S(2)}, u32[]{:S(2)}) collective-permute-start(f32[4,32,128]{2,1,0:T(8,128)S(1)} %get-tuple-element.39), channel_id=1, source_target_pairs={{0,128},{8,136},{16,144},{24,152},{32,160},{40,168},{48,176},{56,1... | collective-permute-start | bytes 196616 | tf_op jit(solution)/shard_map/ppermute | solution.py:289
  59.3 0.9 %collective-permute-start.14 = (f32[4,32,128]{2,1,0:T(8,128)S(1)}, f32[4,32,128]{2,1,0:T(8,128)S(1)}, u32[]{:S(2)}, u32[]{:S(2)}) collective-permute-start(f32[4,32,128]{2,1,0:T(8,128)S(1)} %get-tuple-element.40), channel_id=1, source_target_pairs={{0,192},{8,200},{16,208},{24,216},{32,224},{40,232},{48,240},{56,2... | collective-permute-start | bytes 196616 | tf_op jit(solution)/shard_map/ppermute | solution.py:289
  60.2 3.3 %collective-permute-done.12.r1 = f32[4,32,128]{2,1,0:T(8,128)S(1)} collective-permute-done((f32[4,32,128]{2,1,0:T(8,128)S(1)}, f32[4,32,128]{2,1,0:T(8,128)S(1)}, u32[]{:S(2)}, u32[]{:S(2)}) %collective-permute-start.12) | collective-permute-done | bytes 65568 | tf_op jit(solution)/shard_map/ppermute | solution.py:289
  63.6 0.0 collective-permute-done.13.r2
  63.6 0.6 collective-permute-done.14.r3
  64.2 0.9 %collective-permute-start.15 = (f32[32,128]{1,0:T(8,128)S(1)}, f32[32,128]{1,0:T(8,128)S(1)}, u32[]{:S(2)}, u32[]{:S(2)}) collective-permute-start(f32[32,128]{1,0:T(8,128)S(1)} %get-tuple-element.42), channel_id=1, source_target_pairs={{0,16},{8,24},{16,32},{24,40},{32,48},{40,56},{48,0},{56,8},{64,80... | collective-permute-start | bytes 49160 | tf_op jit(solution)/shard_map/ppermute | solution.py:289
  65.0 3.7 %collective-permute-start.16 = (f32[32,128]{1,0:T(8,128)S(1)}, f32[32,128]{1,0:T(8,128)S(1)}, u32[]{:S(2)}, u32[]{:S(2)}) collective-permute-start(f32[32,128]{1,0:T(8,128)S(1)} %get-tuple-element.43), channel_id=1, source_target_pairs={{0,32},{8,40},{16,48},{24,56},{32,0},{40,8},{48,16},{56,24},{64,96... | collective-permute-start | bytes 49160 | tf_op jit(solution)/shard_map/ppermute | solution.py:289
  68.8 4.0 %collective-permute-start.17 = (f32[32,128]{1,0:T(8,128)S(1)}, f32[32,128]{1,0:T(8,128)S(1)}, u32[]{:S(2)}, u32[]{:S(2)}) collective-permute-start(f32[32,128]{1,0:T(8,128)S(1)} %get-tuple-element.44), channel_id=1, source_target_pairs={{0,48},{8,56},{16,0},{24,8},{32,16},{40,24},{48,32},{56,40},{64,11... | collective-permute-start | bytes 49160 | tf_op jit(solution)/shard_map/ppermute | solution.py:289
  72.8 0.0 collective-permute-done.15.q1
  72.8 0.0 collective-permute-done.16.q2
  72.8 1.4 %collective-permute-done.17.q3 = f32[32,128]{1,0:T(8,128)S(1)} collective-permute-done((f32[32,128]{1,0:T(8,128)S(1)}, f32[32,128]{1,0:T(8,128)S(1)}, u32[]{:S(2)}, u32[]{:S(2)}) %collective-permute-start.17) | collective-permute-done | bytes 16416 | tf_op jit(solution)/shard_map/ppermute | solution.py:289
  74.2 0.6 last.1
  (3 shorter events, 0.1 us)
Async XLA Ops:
  0.0 25.8 %copy-start.2 = (s32[32]{0:T(128)S(1)}, s32[32]{0:T(128)}, u32[]{:S(2)}) copy-start(s32[32]{0:T(128)} %anchors.5) | copy-start | bytes 388
  0.0 41.5 %copy-start.5 = (f32[1,16,4]{1,2,0:T(4,128)S(1)}, f32[1,16,4]{1,2,0:T(4,128)}, u32[]{:S(2)}) copy-start(f32[1,16,4]{1,2,0:T(4,128)} %param.15) | copy-start | bytes 772
  0.0 41.6 %copy-start.6 = (f32[1,128,4]{1,2,0:T(4,128)S(1)}, f32[1,128,4]{1,2,0:T(4,128)}, u32[]{:S(2)}) copy-start(f32[1,128,4]{1,2,0:T(4,128)} %param.17) | copy-start | bytes 6148
  0.0 41.7 %copy-start.4 = (s32[1,128]{1,0:T(1,128)S(1)}, s32[1,128]{1,0:T(1,128)}, u32[]{:S(2)}) copy-start(s32[1,128]{1,0:T(1,128)} %rec_pos.1) | copy-start | bytes 1540
  0.0 41.7 %copy-start.3 = (s32[1,16]{1,0:T(1,128)S(1)}, s32[1,16]{1,0:T(1,128)}, u32[]{:S(2)}) copy-start(s32[1,16]{1,0:T(1,128)} %src_pos.1) | copy-start | bytes 196
  0.8 10.1 %collective-permute-start.4 = (f32[1,2,4,8,128]{4,3,2,1,0:T(8,128)S(1)}, f32[1,2,4,8,128]{4,3,2,1,0:T(8,128)S(1)}, u32[]{:S(2)}, u32[]{:S(2)}) collective-permute-start(f32[1,2,4,8,128]{4,3,2,1,0:T(8,128)S(1)} %maximum_bitcast_fusion), channel_id=1, source_target_pairs={{0,48},{8,56},{16,0},{24,8},{32,16},{40,24},{48,32},{56,40},{64,11... | collective-permute-start | bytes 98312 | tf_op jit(solution)/shard_map/ppermute | solution.py:289
  7.1 8.0 %collective-permute-start.3 = (f32[1,2,4,8,128]{4,3,2,1,0:T(8,128)S(1)}, f32[1,2,4,8,128]{4,3,2,1,0:T(8,128)S(1)}, u32[]{:S(2)}, u32[]{:S(2)}) collective-permute-start(f32[1,2,4,8,128]{4,3,2,1,0:T(8,128)S(1)} %maximum_bitcast_fusion), channel_id=1, source_target_pairs={{0,32},{8,40},{16,48},{24,56},{32,0},{40,8},{48,16},{56,24},{64,96... | collective-permute-start | bytes 98312 | tf_op jit(solution)/shard_map/ppermute | solution.py:289
  8.0 7.1 %collective-permute-start.2 = (f32[1,2,4,8,128]{4,3,2,1,0:T(8,128)S(1)}, f32[1,2,4,8,128]{4,3,2,1,0:T(8,128)S(1)}, u32[]{:S(2)}, u32[]{:S(2)}) collective-permute-start(f32[1,2,4,8,128]{4,3,2,1,0:T(8,128)S(1)} %maximum_bitcast_fusion), channel_id=1, source_target_pairs={{0,16},{8,24},{16,32},{24,40},{32,48},{40,56},{48,0},{56,8},{64,80... | collective-permute-start | bytes 98312 | tf_op jit(solution)/shard_map/ppermute | solution.py:289
  15.1 9.4 %collective-permute-start.7 = (f32[4,2,4,8,128]{4,3,2,1,0:T(8,128)S(1)}, f32[4,2,4,8,128]{4,3,2,1,0:T(8,128)S(1)}, u32[]{:S(2)}, u32[]{:S(2)}) collective-permute-start(f32[4,2,4,8,128]{4,3,2,1,0:T(8,128)S(1)} %pad_maximum_fusion.a0), channel_id=1, source_target_pairs={{0,192},{8,200},{16,208},{24,216},{32,224},{40,232},{48,240},{56,2... | collective-permute-start | bytes 393224 | tf_op jit(solution)/shard_map/ppermute | solution.py:289
  17.9 6.6 %collective-permute-start.6 = (f32[4,2,4,8,128]{4,3,2,1,0:T(8,128)S(1)}, f32[4,2,4,8,128]{4,3,2,1,0:T(8,128)S(1)}, u32[]{:S(2)}, u32[]{:S(2)}) collective-permute-start(f32[4,2,4,8,128]{4,3,2,1,0:T(8,128)S(1)} %pad_maximum_fusion.a0), channel_id=1, source_target_pairs={{0,128},{8,136},{16,144},{24,152},{32,160},{40,168},{48,176},{56,1... | collective-permute-start | bytes 393224 | tf_op jit(solution)/shard_map/ppermute | solution.py:289
  18.7 7.1 %collective-permute-start.5 = (f32[4,2,4,8,128]{4,3,2,1,0:T(8,128)S(1)}, f32[4,2,4,8,128]{4,3,2,1,0:T(8,128)S(1)}, u32[]{:S(2)}, u32[]{:S(2)}) collective-permute-start(f32[4,2,4,8,128]{4,3,2,1,0:T(8,128)S(1)} %pad_maximum_fusion.a0), channel_id=1, source_target_pairs={{0,64},{8,72},{16,80},{24,88},{32,96},{40,104},{48,112},{56,120},{... | collective-permute-start | bytes 393224 | tf_op jit(solution)/shard_map/ppermute | solution.py:289
  19.6 1.2 %copy-start = (f32[4,64,8,128]{3,2,1,0:T(8,128)S(1)}, f32[4,64,8,128]{3,2,1,0:T(8,128)}, u32[]{:S(2)}) copy-start(f32[4,64,8,128]{3,2,1,0:T(8,128)} %src.1) | copy-start | bytes 3145732
  20.9 1.2 %copy-start.1 = (f32[4,64,8,128]{3,2,1,0:T(8,128)S(1)}, f32[4,64,8,128]{3,2,1,0:T(8,128)}, u32[]{:S(2)}) copy-start(f32[4,64,8,128]{3,2,1,0:T(8,128)} %rcv.1) | copy-start | bytes 3145732
  27.3 6.0 %collective-permute-start.8 = (f32[8,2,4,8,128]{4,3,2,1,0:T(8,128)S(1)}, f32[8,2,4,8,128]{4,3,2,1,0:T(8,128)S(1)}, u32[]{:S(2)}, u32[]{:S(2)}) collective-permute-start(f32[8,2,4,8,128]{4,3,2,1,0:T(8,128)S(1)} %get-tuple-element.29), channel_id=1, source_target_pairs={{0,8},{8,0},{16,24},{24,16},{32,40},{40,32},{48,56},{56,48},{64,72... | collective-permute-start | bytes 786440 | tf_op jit(solution)/shard_map/ppermute | solution.py:289
  27.4 20.5 %collective-permute-start = (f32[15,64,128]{2,1,0:T(8,128)S(1)}, f32[15,64,128]{2,1,0:T(8,128)S(1)}, u32[]{:S(2)}, u32[]{:S(2)}) collective-permute-start(f32[15,64,128]{2,1,0:T(8,128)S(1)} %get-tuple-element.26.mine), channel_id=1, source_target_pairs={{0,1},{1,2},{2,3},{3,4},{4,5},{5,6},{6,7},{8,9},{9,10},{10,11},{11... | collective-permute-start | bytes 1474568 | tf_op jit(solution)/shard_map/ppermute | solution.py:294
  29.9 18.0 %collective-permute-start.1 = (f32[13,64,128]{2,1,0:T(8,128)}, f32[13,64,128]{2,1,0:T(8,128)S(1)}, u32[]{:S(2)}, u32[]{:S(2)}) collective-permute-start(f32[13,64,128]{2,1,0:T(8,128)} %get-tuple-element.27), channel_id=1, source_target_pairs={{1,0},{2,1},{3,2},{4,3},{5,4},{6,5},{7,6},{9,8},{10,9},{11,10},{12... | collective-permute-start | bytes 1277960 | tf_op jit(solution)/shard_map/ppermute | solution.py:294
  35.1 15.2 %collective-permute-start.9 = (f32[7,64,128]{2,1,0:T(8,128)}, f32[7,64,128]{2,1,0:T(8,128)S(1)}, u32[]{:S(2)}, u32[]{:S(2)}) collective-permute-start(f32[7,64,128]{2,1,0:T(8,128)} %get-tuple-element.31), channel_id=1, source_target_pairs={{0,1},{1,2},{2,3},{3,4},{4,5},{5,6},{6,7},{8,9},{9,10},{10,11},{11... | collective-permute-start | bytes 688136 | tf_op jit(solution)/shard_map/ppermute | solution.py:294
  39.6 10.7 %collective-permute-start.10 = (f32[6,64,128]{2,1,0:T(8,128)}, f32[6,64,128]{2,1,0:T(8,128)S(1)}, u32[]{:S(2)}, u32[]{:S(2)}) collective-permute-start(f32[6,64,128]{2,1,0:T(8,128)} %get-tuple-element.32), channel_id=1, source_target_pairs={{1,0},{2,1},{3,2},{4,3},{5,4},{6,5},{7,6},{9,8},{10,9},{11,10},{12... | collective-permute-start | bytes 589832 | tf_op jit(solution)/shard_map/ppermute | solution.py:294
  55.1 1.6 %collective-permute-start.11 = (f32[16,32,128]{2,1,0:T(8,128)S(1)}, f32[16,32,128]{2,1,0:T(8,128)S(1)}, u32[]{:S(2)}, u32[]{:S(2)}) collective-permute-start(f32[16,32,128]{2,1,0:T(8,128)S(1)} %get-tuple-element.36), channel_id=1, source_target_pairs={{0,8},{8,0},{16,24},{24,16},{32,40},{40,32},{48,56},{56,48},{64,72... | collective-permute-start | bytes 786440 | tf_op jit(solution)/shard_map/ppermute | solution.py:289
  56.7 6.8 %collective-permute-start.12 = (f32[4,32,128]{2,1,0:T(8,128)S(1)}, f32[4,32,128]{2,1,0:T(8,128)S(1)}, u32[]{:S(2)}, u32[]{:S(2)}) collective-permute-start(f32[4,32,128]{2,1,0:T(8,128)S(1)} %get-tuple-element.38), channel_id=1, source_target_pairs={{0,64},{8,72},{16,80},{24,88},{32,96},{40,104},{48,112},{56,120},{... | collective-permute-start | bytes 196616 | tf_op jit(solution)/shard_map/ppermute | solution.py:289
  57.3 6.2 %collective-permute-start.13 = (f32[4,32,128]{2,1,0:T(8,128)S(1)}, f32[4,32,128]{2,1,0:T(8,128)S(1)}, u32[]{:S(2)}, u32[]{:S(2)}) collective-permute-start(f32[4,32,128]{2,1,0:T(8,128)S(1)} %get-tuple-element.39), channel_id=1, source_target_pairs={{0,128},{8,136},{16,144},{24,152},{32,160},{40,168},{48,176},{56,1... | collective-permute-start | bytes 196616 | tf_op jit(solution)/shard_map/ppermute | solution.py:289
  59.3 4.8 %collective-permute-start.14 = (f32[4,32,128]{2,1,0:T(8,128)S(1)}, f32[4,32,128]{2,1,0:T(8,128)S(1)}, u32[]{:S(2)}, u32[]{:S(2)}) collective-permute-start(f32[4,32,128]{2,1,0:T(8,128)S(1)} %get-tuple-element.40), channel_id=1, source_target_pairs={{0,192},{8,200},{16,208},{24,216},{32,224},{40,232},{48,240},{56,2... | collective-permute-start | bytes 196616 | tf_op jit(solution)/shard_map/ppermute | solution.py:289
  64.2 8.7 %collective-permute-start.15 = (f32[32,128]{1,0:T(8,128)S(1)}, f32[32,128]{1,0:T(8,128)S(1)}, u32[]{:S(2)}, u32[]{:S(2)}) collective-permute-start(f32[32,128]{1,0:T(8,128)S(1)} %get-tuple-element.42), channel_id=1, source_target_pairs={{0,16},{8,24},{16,32},{24,40},{32,48},{40,56},{48,0},{56,8},{64,80... | collective-permute-start | bytes 49160 | tf_op jit(solution)/shard_map/ppermute | solution.py:289
  65.0 7.8 %collective-permute-start.16 = (f32[32,128]{1,0:T(8,128)S(1)}, f32[32,128]{1,0:T(8,128)S(1)}, u32[]{:S(2)}, u32[]{:S(2)}) collective-permute-start(f32[32,128]{1,0:T(8,128)S(1)} %get-tuple-element.43), channel_id=1, source_target_pairs={{0,32},{8,40},{16,48},{24,56},{32,0},{40,8},{48,16},{56,24},{64,96... | collective-permute-start | bytes 49160 | tf_op jit(solution)/shard_map/ppermute | solution.py:289
  68.8 5.5 %collective-permute-start.17 = (f32[32,128]{1,0:T(8,128)S(1)}, f32[32,128]{1,0:T(8,128)S(1)}, u32[]{:S(2)}, u32[]{:S(2)}) collective-permute-start(f32[32,128]{1,0:T(8,128)S(1)} %get-tuple-element.44), channel_id=1, source_target_pairs={{0,48},{8,56},{16,0},{24,8},{32,16},{40,24},{48,32},{56,40},{64,11... | collective-permute-start | bytes 49160 | tf_op jit(solution)/shard_map/ppermute | solution.py:289

commit v2 on v1

--- a/solution.py
+++ b/solution.py
@@ -1,10 +1,9 @@
-import functools
-
 import jax
 import jax.numpy as jnp
 from jax import lax
 from jax.experimental import pallas as pl
 from jax.experimental.pallas import tpu as pltpu
+from jax.sharding import Mesh
 from jax.sharding import PartitionSpec as P
 
 STEPS = 4
@@ -19,6 +18,7 @@
 VMEM = pl.BlockSpec(memory_space=pltpu.VMEM)
 SMEM = pl.BlockSpec(memory_space=pltpu.SMEM)
 ANY = pl.BlockSpec(memory_space=pl.ANY)
+HBM = pl.BlockSpec(memory_space=pltpu.HBM)
 
 
 def shape(*dims):
@@ -30,11 +30,22 @@
 
 
 def place():
-    shot = lax.axis_index("shot")
-    return shot // (NZH * NC), (shot // NC) % NZH, shot % NC, shot
-
-
-def pack_kernel(src, rcv, own, to_prev, to_next):
+    c = lax.axis_index("core")
+    return c, (lax.axis_index("x") * NZH + lax.axis_index("zh")) * NC + c
+
+
+def first_strip(b, c):
+    return (b + ((c + b) & 1)) >> 1
+
+
+def pack_kernel(src_in, rcv_in, own, to_prev, to_next, src, rcv, sem):
+    half = ROWS // 2
+    copies = []
+    for h in range(2):
+        cut = slice(h * half, h * half + half)
+        for f, (a, b) in enumerate(((src_in, src), (rcv_in, rcv))):
+            copies.append(pltpu.make_async_copy(a.at[:, cut], b.at[:, cut], sem.at[h, f]))
+            copies[-1].start()
     lane = lax.broadcasted_iota(jnp.int32, (COLS, DEPTH), 1)
     col = lax.broadcasted_iota(jnp.int32, (COLS, DEPTH), 0)
 
@@ -47,13 +58,15 @@
             spread += vz - jnp.where(lane == 0, 0.0, pltpu.roll(vz, 1, 1))
             own[2 * f, pl.ds(x, COLS, stride=ROWS), :] = p
             own[2 * f + 1, pl.ds(x, COLS, stride=ROWS), :] = spread
-            last = (COLS - 1)
-            to_next[7 + 8 * f - f, pl.ds(x, 1), :] = vy[last:, :]
+            to_next[7 + 7 * f, pl.ds(x, 1), :] = vy[COLS - 1 :, :]
             after.append(vx)
         return tuple(after)
 
-    zero = jnp.zeros((COLS, DEPTH), F32)
-    lax.fori_loop(0, ROWS, row, (zero, zero), unroll=4)
+    before = (jnp.zeros((COLS, DEPTH), F32),) * 2
+    for h in range(2):
+        for copy in copies[2 * h : 2 * h + 2]:
+            copy.wait()
+        before = lax.fori_loop(h * half, h * half + half, row, before, unroll=8)
 
     def plane(f, y):
         return own[f, y * ROWS : (y + 1) * ROWS, :]
@@ -71,50 +84,45 @@
 
 
 def inject_kernel(src_pos, wavelet, rec_pos, traces, src_out, rec_out):
-    src_out[...] = jnp.zeros(src_out.shape, F32)
-    rec_out[...] = jnp.zeros(rec_out.shape, F32)
+    for out in (src_out, rec_out):
+        for s in range(STEPS):
+            out[s, 1 : PLANES - 1] = jnp.zeros((PLANES - 2, ROWS, DEPTH), F32)
     first = lax.axis_index("tile") * COLS - STEPS
     lane = lax.broadcasted_iota(jnp.int32, (1, DEPTH), 1)
     for pos, amp, out in ((src_pos, wavelet, src_out), (rec_pos, traces, rec_out)):
 
         def point(k, _, pos=pos, amp=amp, out=out):
             cell = pos[0, k]
-            x = cell // (COLS * NT * DEPTH)
-            y = (cell // DEPTH) % (COLS * NT) - first
-            hit = lane == cell % DEPTH
-
-            @pl.when((y >= 0) & (y < PLANES))
-            def _():
-                old = [out[s, y, pl.ds(x, 1), :] for s in range(STEPS)]
-                for s in range(STEPS):
-                    out[s, y, pl.ds(x, 1), :] = old[s] + jnp.where(hit, amp[0, k, s], 0.0)
-
+            x = cell >> 13
+            y = jnp.clip(((cell >> 7) & (COLS * NT - 1)) - first, 0, PLANES - 1)
+            hit = lane == (cell & (DEPTH - 1))
+            old = [out[s, y, pl.ds(x, 1), :] for s in range(STEPS)]
+            for s in range(STEPS):
+                out[s, y, pl.ds(x, 1), :] = old[s] + jnp.where(hit, amp[s, k], 0.0)
             return 0
 
-        lax.fori_loop(0, pos.shape[1], point, 0)
-
-
-def window_kernel(anchors, a0, a1, a2, a3, own, other, strips, sem):
-    copies = [pltpu.make_async_copy(a, strips.at[d], sem.at[d]) for d, a in enumerate((a0, a1, a2, a3))]
-    for copy in copies:
-        copy.start()
-    x, z, c, g = place()
-    for copy in copies:
-        copy.wait()
+        lax.fori_loop(0, pos.shape[1], point, 0, unroll=8)
+
+
+def window_kernel(anchors, a0, a1, a2, a3, own, other):
+    x, z = lax.axis_index("x"), lax.axis_index("zh")
+    c, g = place()
     for group, out in ((g, own), (g + 1 - 2 * c, other)):
-        b = anchors[group]
-        first = (b + (c + b) % 2) // 2
-        for i in range(8):
-            j = first + i
-            block = strips.at[(x - j // NZH + NX) % NX, (z - j % NZH + NZH) % NZH]
-            vel, den = block[0], block[1]
-            out[i, 0] = den * vel * vel
-            out[i, 1] = 1.0 / den
+        first = first_strip(anchors[group], c)
+        for dx, strips in enumerate((a0, a1, a2, a3)):
+            for dz in range(NZH):
+                i = ((x - dx) & (NX - 1)) * NZH + ((z - dz) & (NZH - 1)) - first
+
+                @pl.when((i >= 0) & (i < 8))
+                def _(i=i, strips=strips, dz=dz, out=out):
+                    vel, den = strips[dz, 0], strips[dz, 1]
+                    out[i, 0] = den * vel * vel
+                    out[i, 1] = 1.0 / den
 
 
 def model_kernel(anchors, own, other, out, to_prev, to_next):
-    _, _, c, g = place()
-    odd = (c + anchors[g]) % 2
+    c, g = place()
+    odd = (c + anchors[g]) & 1
     for strips, start in ((own, odd), (other, 1 - odd)):
         for i in range(8):
             for r in range(4):
@@ -136,25 +144,34 @@
     keep, send,
     ps, pr, ds, dr, mod, buoy, corr,
 ):
-    vy = (prev.at[7], prev.at[14], mine.at[7], mine.at[14])
-    ps[0, 0:4] = prev[0:4]
+    tile = lax.axis_index("tile")
+    inner_low, inner_high = tile > 0, tile < NT - 1
+
+    def below(value):
+        return jnp.where(inner_low, value, 0.0)
+
+    def above(value):
+        return jnp.where(inner_high, value, 0.0)
+
+    ps[0, 0:4] = below(prev[0:4])
     ps[0, 4:12] = own[0]
-    ps[0, 12:16] = nxt[0:4]
-    pr[0, 1:4] = prev[8:11]
+    ps[0, 12:16] = above(nxt[0:4])
+    pr[0, 1:4] = below(prev[8:11])
     pr[0, 4:12] = own[2]
-    pr[0, 12:15] = nxt[7:10]
-    for d, f, at, after in ((ds, 0, 4, 4), (dr, 1, 11, 10)):
-        d[1:4] = prev[at : at + 3]
-        d[4] = own[2 * f + 1, 0] - vy[f][...]
+    pr[0, 12:15] = above(nxt[7:10])
+    for d, f, at, vy, after in ((ds, 0, 4, 7, 4), (dr, 1, 11, 14, 10)):
+        d[1:4] = below(prev[at : at + 3])
+        d[4] = own[2 * f + 1, 0] - below(prev[vy])
         d[5:12] = own[2 * f + 1, 1:8]
-        d[12] = nxt[after] - vy[2 + f][...]
-        d[13:15] = nxt[after + 1 : after + 3]
-    mod[1:4] = model_prev[0:3]
+        d[12] = above(nxt[after] - mine[vy])
+        d[13:15] = above(nxt[after + 1 : after + 3])
+    mod[1:4] = below(model_prev[0:3])
     mod[4:12] = model[0]
-    mod[12:15] = model_next[0:3]
-    buoy[0:4] = model_prev[3:7]
+    mod[12:15] = above(model_next[0:3])
+    buoy[0:4] = below(model_prev[3:7])
     buoy[4:12] = model[1]
-    buoy[12:15] = model_next[3:6]
+    buoy[12:15] = above(model_next[3:6])
+
     keep[...] = jnp.zeros(keep.shape, F32)
     send[...] = jnp.zeros(send.shape, F32)
 
@@ -226,11 +243,10 @@
 
         lax.fori_loop(0, (high - low) // UNROLL, planes, carry)
 
-    _, _, c, g = place()
-    b = anchors[g]
-    odd = (c + b) % 2
+    c, g = place()
+    odd = (c + anchors[g]) & 1
     for out, start in ((keep, odd), (send, 1 - odd)):
-        at = (b + start) // 2
+        at = (anchors[g] + start) >> 1
         for i in range(8):
             out[at + i] = corr[pl.ds(pl.multiple_of(32 * (start + 2 * i), 32), 32), :]
 
@@ -251,23 +267,23 @@
             pltpu.VMEM((PLANES, *plane), F32),
             pltpu.VMEM((COLS * ROWS, DEPTH), F32),
         ],
-        compiler_params=params(24),
+        compiler_params=params(10),
         name="march",
     )(*operands)
 
 
 def halve_kernel(keep, got, s0, s1, s2, s3):
-    x, _, _, _ = place()
+    x = lax.axis_index("x")
     for d, out in enumerate((s0, s1, s2, s3)):
-        at = ((x + d) % NX) * NZH
+        at = ((x + d) & (NX - 1)) * NZH
         for i in range(NZH):
             out[i] = keep[at + i] + got[at + i]
 
 
 def quarter_kernel(s0, r1, r2, r3, u0, u1, u2, u3):
-    _, z, _, _ = place()
+    z = lax.axis_index("zh")
     for d, out in enumerate((u0, u1, u2, u3)):
-        at = (z + d) % NZH
+        at = (z + d) & (NZH - 1)
         out[...] = (s0[at] + r1[at]) + (r2[at] + r3[at])
 
 
@@ -275,40 +291,39 @@
     out[...] = (u0[...] + q1[...]) + (q2[...] + q3[...])
 
 
+def other_core(block):
+    return lax.ppermute(block, "core", [(0, 1), (1, 0)])
+
+
+def to_tile(block, distance):
+    return lax.ppermute(block, "tile", [(i, (i + distance) % NT) for i in range(NT)])
+
+
 def along(block, axis, distance):
-    route = []
-    for s in range(NX * NZH * NC):
-        x, z, c = s // (NZH * NC), (s // NC) % NZH, s % NC
-        if axis == "x":
-            x = (x + distance) % NX
-        elif axis == "z":
-            z = (z + distance) % NZH
-        else:
-            c = (c + distance) % NC
-        route.append((s, (x * NZH + z) * NC + c))
-    return lax.ppermute(block, "shot", route)
-
-
-def to_tile(block, distance):
-    route = [(i, i + distance) for i in range(NT) if 0 <= i + distance < NT]
-    return lax.ppermute(block, "tile", route)
+    return lax.ppermute(block, axis, [(i, (i + distance) % 4) for i in range(4)])
 
 
 def local(velocity, density, anchors, src_state, rcv_state, src_pos, wavelet, rec_pos, traces):
     plane = (ROWS, DEPTH)
-    model = jnp.stack([velocity, density])[None]
-    zs = [along(model, "z", d) for d in range(1, NZH)]
+    strip = jnp.stack([velocity, density])[None]
+    zs = [along(strip, "zh", d) for d in range(1, NZH)]
 
     own, to_prev, to_next = pl.pallas_call(
         pack_kernel,
         out_shape=[shape(4, COLS * ROWS, DEPTH), shape(13, *plane), shape(15, *plane)],
-        in_specs=[VMEM, VMEM],
+        in_specs=[HBM, HBM],
         out_specs=[VMEM] * 3,
-        compiler_params=params(16),
+        scratch_shapes=[
+            pltpu.VMEM((4, ROWS, COLS, DEPTH), F32),
+            pltpu.VMEM((4, ROWS, COLS, DEPTH), F32),
+            pltpu.SemaphoreType.DMA((2, 2)),
+        ],
+        compiler_params=params(8),
         name="pack",
-    )(src_state, rcv_state)
-
-    xs = [jnp.concatenate([model, *zs])]
+    )(*(pltpu.with_memory_space_constraint(state, pltpu.HBM) for state in (src_state, rcv_state)))
+    *zs, own, to_prev, to_next = lax.optimization_barrier((*zs, own, to_prev, to_next))
+
+    xs = [jnp.concatenate([strip, *zs])]
     xs += [along(xs[0], "x", d) for d in range(1, NX)]
 
     halo_next = to_tile(to_prev, -1)
@@ -319,31 +334,27 @@
         out_shape=[shape(STEPS, PLANES, *plane)] * 2,
         in_specs=[SMEM] * 4,
         out_specs=[VMEM] * 2,
-        compiler_params=params(16),
+        compiler_params=params(2),
         name="inject",
-    )(src_pos, wavelet, rec_pos, traces)
-
-    strips = (8, 2, 4, COLS, DEPTH)
+    )(src_pos, wavelet[0].T, rec_pos, traces[0].T)
+
     mine, other = pl.pallas_call(
         window_kernel,
-        out_shape=[shape(*strips)] * 2,
-        in_specs=[SMEM] + [ANY] * 4,
+        out_shape=[shape(8, *strip.shape[1:])] * 2,
+        in_specs=[SMEM] + [VMEM] * 4,
         out_specs=[VMEM] * 2,
-        scratch_shapes=[
-            pltpu.VMEM((NX, NZH, 2, 4, COLS, DEPTH), F32),
-            pltpu.SemaphoreType.DMA((NX,)),
-        ],
-        compiler_params=params(16),
+        compiler_params=params(2),
         name="window",
     )(anchors, *xs)
-    got = along(other, "core", 1)
+    got = other_core(other)
+    got, halo_prev, halo_next = lax.optimization_barrier((got, halo_prev, halo_next))
 
     mb, mb_prev, mb_next = pl.pallas_call(
         model_kernel,
         out_shape=[shape(2, COLS * ROWS, DEPTH), shape(6, *plane), shape(7, *plane)],
         in_specs=[SMEM, VMEM, VMEM],
         out_specs=[VMEM] * 3,
-        compiler_params=params(16),
+        compiler_params=params(2),
         name="model",
     )(anchors, mine, got)
     model_next = to_tile(mb_prev, -1)
@@ -362,51 +373,51 @@
         inj_rec,
     )
 
-    received = along(send, "core", 1)
     parts = pl.pallas_call(
         halve_kernel,
         out_shape=[shape(NZH, 32, DEPTH)] * NX,
-        in_specs=[VMEM] * 2,
+        in_specs=[VMEM, VMEM],
         out_specs=[VMEM] * NX,
-        compiler_params=params(8),
+        compiler_params=params(2),
         name="halve",
-    )(keep, received)
+    )(keep, other_core(send))
     moved = [along(parts[d], "x", d) for d in range(1, NX)]
     parts = pl.pallas_call(
         quarter_kernel,
         out_shape=[shape(32, DEPTH)] * NZH,
         in_specs=[VMEM] * NX,
         out_specs=[VMEM] * NZH,
-        compiler_params=params(8),
+        compiler_params=params(2),
         name="quarter",
     )(parts[0], *moved)
-    moved = [along(parts[d], "z", d) for d in range(1, NZH)]
+    moved = [along(parts[d], "zh", d) for d in range(1, NZH)]
     image = pl.pallas_call(
         last_kernel,
         out_shape=shape(32, DEPTH),
         in_specs=[VMEM] * NZH,
         out_specs=VMEM,
-        compiler_params=params(8),
+        compiler_params=params(2),
         name="last",
     )(parts[0], *moved)
-    return image.reshape(4, COLS, DEPTH)
+    return image.reshape(velocity.shape)
 
 
 def solution(mesh):
+    shot = ("x", "zh", "core")
     return jax.shard_map(
         local,
-        mesh=mesh,
+        mesh=Mesh(mesh.devices.reshape(NX, NZH, NC, NT), (*shot, "tile")),
         in_specs=(
-            P("shot", "tile", None),
-            P("shot", "tile", None),
+            P(shot, "tile", None),
+            P(shot, "tile", None),
             P(),
-            P(None, "shot", "tile", None),
-            P(None, "shot", "tile", None),
-            P("shot", None),
-            P("shot", None, None),
-            P("shot", None),
-            P("shot", None, None),
+            P(None, shot, "tile", None),
+            P(None, shot, "tile", None),
+            P(shot, None),
+            P(shot, None, None),
+            P(shot, None),
+            P(shot, None, None),
         ),
-        out_specs=P("shot", "tile", None),
+        out_specs=P(shot, "tile", None),
         check_vma=False,
     )

time: 75.4 us -> 67.1 us (0.89)
  waiting for transfers between devices: 14.7 us -> 20.4 us
  starting transfers between devices: 39.3 us -> 33.6 us
  Pallas kernels: 17.3 us -> 11.9 us
  local copies, waits for them, and re-layouts: 2.66 us -> 0.02 us
    ppermute x18, waiting for transfers between devices: 14.7 us -> 20.4 us  [the longest x12 12.2 us: along(): lax.ppermute(block, axis, [(i, (i + distance) % 4) for i in range(4)])]
    ppermute x18, starting transfers between devices: 39.3 us -> 33.6 us  [the longest x12 27.2 us: along(): lax.ppermute(block, axis, [(i, (i + distance) % 4) for i in range(4)])]
    pallas_call x1, Pallas kernels: 6.15 us -> 1.97 us  [local(): pl.pallas_call(inject_kernel, out_shape=[shape(STEPS, PLANES, *plane)] *...]
    unnamed x16 -> x10, local copies, waits for them, and re-layouts: 2.66 us -> 0.02 us
    pallas_call x1, Pallas kernels: 1.77 us -> 1 us  [local(): pl.pallas_call(model_kernel, out_shape=[shape(2, COLS * ROWS, DEPTH), sha...]
  transfers between devices with their start and end apart: 18 -> 18, of which waited for: 7 -> 11; matrix products, arithmetic and copies ran while one was open for 0% -> 0% of each run, Pallas kernels for 14% -> 8%
where the time goes in v2:
time: 67.1 us; the launch traced here: 66.8 us
  starting transfers between devices  33.6 us (50%)
  waiting for transfers between devices  20.4 us (30%)
  Pallas kernels  11.9 us (18%)
  other arithmetic  0.8 us (1%)
    ppermute x12, starting transfers between devices, along(): lax.ppermute(block, axis, [(i, (i + distance) % 4) for i in range(4)])  27.2 us
    ppermute x12, waiting for transfers between devices, along(): lax.ppermute(block, axis, [(i, (i + distance) % 4) for i in range(4)])  12.2 us
    ppermute x4, starting transfers between devices, to_tile(): lax.ppermute(block, 'tile', [(i, (i + distance) % NT) for i in range(NT)])  6.23 us
    ppermute x4, waiting for transfers between devices, to_tile(): lax.ppermute(block, 'tile', [(i, (i + distance) % NT) for i in range(NT)])  5.14 us
    pallas_call x1, Pallas kernels, march(): pl.pallas_call(march_kernel, out_shape=[shape(16, 32, DEPTH)] * 2, in_spe...  4.78 us
    ppermute x2, waiting for transfers between devices, other_core(): return lax.ppermute(block, 'core', [(0, 1), (1, 0)])  3.04 us
    pallas_call x1, Pallas kernels, local(): pl.pallas_call(pack_kernel, out_shape=[shape(4, COLS * ROWS, DEPTH), shap...  2.63 us
    pallas_call x1, Pallas kernels, local(): pl.pallas_call(inject_kernel, out_shape=[shape(STEPS, PLANES, *plane)] *...  1.97 us
  transfers between devices with their start and end apart: 18, of which 11 were waited for; matrix products, arithmetic and copies ran while one was open for 0% of the time, Pallas kernels for 8%

profile of v2, /device:TPU:24, one launch (start us, length us, event | category | flops | bytes accessed | tf_op | source)
XLA Modules:
  0.0 66.8 jit_solution(6274583956039860206)
XLA Ops:
  0.0 0.0 copy-start
  0.0 0.0 copy-start.2
  0.0 0.0 copy-start.4
  0.0 0.0 copy-start.1
  0.0 0.0 copy-start.3
  0.0 0.8 %maximum_bitcast_fusion = f32[1,2,4,8,128]{4,3,2,1,0:T(8,128)S(1)} fusion(f32[1,4,8,128]{3,2,1,0:T(8,128)} %bitcast.17, f32[1,4,8,128]{3,2,1,0:T(8,128)} %bitcast.18), kind=kLoop, calls=%fused_computation.1 | loop fusion | flops 8192 | bytes 65536 | tf_op jit(solution)/shard_map/broadcast_in_dim | solution.py:308
  0.8 6.3 %collective-permute-start.2 = (f32[1,2,4,8,128]{4,3,2,1,0:T(8,128)S(1)}, f32[1,2,4,8,128]{4,3,2,1,0:T(8,128)S(1)}, u32[]{:S(2)}, u32[]{:S(2)}) collective-permute-start(f32[1,2,4,8,128]{4,3,2,1,0:T(8,128)S(1)} %maximum_bitcast_fusion), channel_id=1, source_target_pairs={{0,48},{16,0},{32,16},{48,32},{1,49},{17,1},{33,17},{49,33},{2,50}... | collective-permute-start | bytes 98312 | tf_op jit(solution)/shard_map/ppermute | solution.py:303
  7.1 0.9 %collective-permute-start.1 = (f32[1,2,4,8,128]{4,3,2,1,0:T(8,128)S(1)}, f32[1,2,4,8,128]{4,3,2,1,0:T(8,128)S(1)}, u32[]{:S(2)}, u32[]{:S(2)}) collective-permute-start(f32[1,2,4,8,128]{4,3,2,1,0:T(8,128)S(1)} %maximum_bitcast_fusion), channel_id=1, source_target_pairs={{0,32},{16,48},{32,0},{48,16},{1,33},{17,49},{33,1},{49,17},{2,34}... | collective-permute-start | bytes 98312 | tf_op jit(solution)/shard_map/ppermute | solution.py:303
  8.0 2.9 %collective-permute-start = (f32[1,2,4,8,128]{4,3,2,1,0:T(8,128)S(1)}, f32[1,2,4,8,128]{4,3,2,1,0:T(8,128)S(1)}, u32[]{:S(2)}, u32[]{:S(2)}) collective-permute-start(f32[1,2,4,8,128]{4,3,2,1,0:T(8,128)S(1)} %maximum_bitcast_fusion), channel_id=1, source_target_pairs={{0,16},{16,32},{32,48},{48,0},{1,17},{17,33},{33,49},{49,1},{2,18}... | collective-permute-start | bytes 98312 | tf_op jit(solution)/shard_map/ppermute | solution.py:303
  10.9 2.6 %pack.1 = (f32[4,512,128]{2,1,0:T(8,128)S(1)}, f32[13,64,128]{2,1,0:T(8,128)S(1)}, f32[15,64,128]{2,1,0:T(8,128)S(1)}) custom-call(f32[4,64,8,128]{3,2,1,0:T(8,128)} %src_in.1, f32[4,64,8,128]{3,2,1,0:T(8,128)} %rcv_in.1), custom_call_target="tpu_custom_call" | custom-call | tf_op jit(solution)/shard_map/pack/pallas_call | solution.py:311
  13.6 0.0 collective-permute-done.2
  13.6 1.5 %collective-permute-done.1 = f32[1,2,4,8,128]{4,3,2,1,0:T(8,128)S(1)} collective-permute-done((f32[1,2,4,8,128]{4,3,2,1,0:T(8,128)S(1)}, f32[1,2,4,8,128]{4,3,2,1,0:T(8,128)S(1)}, u32[]{:S(2)}, u32[]{:S(2)}) %collective-permute-start.1) | collective-permute-done | bytes 32800 | tf_op jit(solution)/shard_map/ppermute | solution.py:303
  15.1 0.0 collective-permute-done
  15.1 0.7 %collective-permute-start.8 = (f32[13,64,128]{2,1,0:T(8,128)S(1)}, f32[13,64,128]{2,1,0:T(8,128)S(1)}, u32[]{:S(2)}, u32[]{:S(2)}) collective-permute-start(f32[13,64,128]{2,1,0:T(8,128)S(1)} %get-tuple-element.43), channel_id=1, source_target_pairs={{0,7},{1,0},{2,1},{3,2},{4,3},{5,4},{6,5},{7,6},{8,15},{9,8},{10,9... | collective-permute-start | bytes 1277960 | tf_op jit(solution)/shard_map/ppermute | solution.py:299
  15.8 3.4 %collective-permute-start.7 = (f32[15,64,128]{2,1,0:T(8,128)S(1)}, f32[15,64,128]{2,1,0:T(8,128)S(1)}, u32[]{:S(2)}, u32[]{:S(2)}) collective-permute-start(f32[15,64,128]{2,1,0:T(8,128)S(1)} %get-tuple-element.42.mine), channel_id=1, source_target_pairs={{0,1},{1,2},{2,3},{3,4},{4,5},{5,6},{6,7},{7,0},{8,9},{9,10},{10,1... | collective-permute-start | bytes 1474568 | tf_op jit(solution)/shard_map/ppermute | solution.py:299
  19.2 2.8 %collective-permute-start.5 = (f32[4,2,4,8,128]{4,3,2,1,0:T(8,128)S(1)}, f32[4,2,4,8,128]{4,3,2,1,0:T(8,128)S(1)}, u32[]{:S(2)}, u32[]{:S(2)}) collective-permute-start(f32[4,2,4,8,128]{4,3,2,1,0:T(8,128)S(1)} %pad_maximum_fusion.a0), channel_id=1, source_target_pairs={{0,192},{64,0},{128,64},{192,128},{1,193},{65,1},{129,65},{193,129... | collective-permute-start | bytes 393224 | tf_op jit(solution)/shard_map/ppermute | solution.py:303
  22.1 0.8 %collective-permute-start.4 = (f32[4,2,4,8,128]{4,3,2,1,0:T(8,128)S(1)}, f32[4,2,4,8,128]{4,3,2,1,0:T(8,128)S(1)}, u32[]{:S(2)}, u32[]{:S(2)}) collective-permute-start(f32[4,2,4,8,128]{4,3,2,1,0:T(8,128)S(1)} %pad_maximum_fusion.a0), channel_id=1, source_target_pairs={{0,128},{64,192},{128,0},{192,64},{1,129},{65,193},{129,1},{193,65... | collective-permute-start | bytes 393224 | tf_op jit(solution)/shard_map/ppermute | solution.py:303
  22.9 0.9 %collective-permute-start.3 = (f32[4,2,4,8,128]{4,3,2,1,0:T(8,128)S(1)}, f32[4,2,4,8,128]{4,3,2,1,0:T(8,128)S(1)}, u32[]{:S(2)}, u32[]{:S(2)}) collective-permute-start(f32[4,2,4,8,128]{4,3,2,1,0:T(8,128)S(1)} %pad_maximum_fusion.a0), channel_id=1, source_target_pairs={{0,64},{64,128},{128,192},{192,0},{1,65},{65,129},{129,193},{193,1... | collective-permute-start | bytes 393224 | tf_op jit(solution)/shard_map/ppermute | solution.py:303
  23.8 2.2 %collective-permute-done.5.a3 = f32[4,2,4,8,128]{4,3,2,1,0:T(8,128)S(1)} collective-permute-done((f32[4,2,4,8,128]{4,3,2,1,0:T(8,128)S(1)}, f32[4,2,4,8,128]{4,3,2,1,0:T(8,128)S(1)}, u32[]{:S(2)}, u32[]{:S(2)}) %collective-permute-start.5) | collective-permute-done | bytes 131104 | tf_op jit(solution)/shard_map/ppermute | solution.py:303
  26.0 2.6 %collective-permute-done.4.a2 = f32[4,2,4,8,128]{4,3,2,1,0:T(8,128)S(1)} collective-permute-done((f32[4,2,4,8,128]{4,3,2,1,0:T(8,128)S(1)}, f32[4,2,4,8,128]{4,3,2,1,0:T(8,128)S(1)}, u32[]{:S(2)}, u32[]{:S(2)}) %collective-permute-start.4) | collective-permute-done | bytes 131104 | tf_op jit(solution)/shard_map/ppermute | solution.py:303
  28.6 1.3 %collective-permute-done.3.a1 = f32[4,2,4,8,128]{4,3,2,1,0:T(8,128)S(1)} collective-permute-done((f32[4,2,4,8,128]{4,3,2,1,0:T(8,128)S(1)}, f32[4,2,4,8,128]{4,3,2,1,0:T(8,128)S(1)}, u32[]{:S(2)}, u32[]{:S(2)}) %collective-permute-start.3) | collective-permute-done | bytes 131104 | tf_op jit(solution)/shard_map/ppermute | solution.py:303
  30.0 0.0 copy-done
  30.0 0.9 %window.1 = (f32[8,2,4,8,128]{4,3,2,1,0:T(8,128)S(1)}, f32[8,2,4,8,128]{4,3,2,1,0:T(8,128)S(1)}) custom-call(s32[32]{0:T(128)S(1)} %copy-done, f32[4,2,4,8,128]{4,3,2,1,0:T(8,128)S(1)} %pad_maximum_fusion.a0, f32[4,2,4,8,128]{4,3,2,1,0:T(8,128)S(1)} %collective-permute-done.3.a1, f32[4,2,4,8,128]{4,3,2,1,0:T(8,128)S(1)} %collective-permute-done.4.a2, ...), custom_call_target="tpu_custom_call" | custom-call | tf_op jit(solution)/shard_map/window/pallas_call | solution.py:341
  30.8 0.1 collective-permute-start.6
  30.9 1.5 %collective-permute-done.6.other = f32[8,2,4,8,128]{4,3,2,1,0:T(8,128)S(1)} collective-permute-done((f32[8,2,4,8,128]{4,3,2,1,0:T(8,128)S(1)}, f32[8,2,4,8,128]{4,3,2,1,0:T(8,128)S(1)}, u32[]{:S(2)}, u32[]{:S(2)}) %collective-permute-start.6) | collective-permute-done | bytes 262176 | tf_op jit(solution)/shard_map/ppermute | solution.py:295
  32.4 0.0 collective-permute-done.8.nxt
  32.5 0.0 collective-permute-done.7.prev
  32.5 1.0 %model.1 = (f32[2,512,128]{2,1,0:T(8,128)S(1)}, f32[6,64,128]{2,1,0:T(8,128)S(1)}, f32[7,64,128]{2,1,0:T(8,128)S(1)}) custom-call(s32[32]{0:T(128)S(1)} %copy-done, f32[8,2,4,8,128]{4,3,2,1,0:T(8,128)S(1)} %get-tuple-element.46.own, f32[8,2,4,8,128]{4,3,2,1,0:T(8,128)S(1)} %collective-permute-done.6.other), custom_call_target="tpu_custom_call" | custom-call | tf_op jit(solution)/shard_map/model/pallas_call | solution.py:352
  33.5 0.1 collective-permute-start.9
  33.6 2.0 %collective-permute-start.10 = (f32[6,64,128]{2,1,0:T(8,128)S(1)}, f32[6,64,128]{2,1,0:T(8,128)S(1)}, u32[]{:S(2)}, u32[]{:S(2)}) collective-permute-start(f32[6,64,128]{2,1,0:T(8,128)S(1)} %get-tuple-element.50), channel_id=1, source_target_pairs={{0,7},{1,0},{2,1},{3,2},{4,3},{5,4},{6,5},{7,6},{8,15},{9,8},{10,9... | collective-permute-start | bytes 589832 | tf_op jit(solution)/shard_map/ppermute | solution.py:299
  35.6 0.0 copy-done.2
  35.6 0.0 copy-done.4
  35.6 0.0 copy-done.1
  35.6 0.0 copy-done.3
  35.6 2.0 %inject.1 = (f32[4,16,64,128]{3,2,1,0:T(8,128)S(1)}, f32[4,16,64,128]{3,2,1,0:T(8,128)S(1)}) custom-call(s32[1,16]{1,0:T(1,128)S(1)} %copy-done.3, f32[4,16]{1,0:T(4,128)S(1)} %bitcast.15, s32[1,128]{1,0:T(1,128)S(1)} %copy-done.4, f32[4,128]{1,0:T(4,128)S(1)} %bitcast.16), custom_call_target="tpu_custom_call" | custom-call | tf_op jit(solution)/shard_map/inject/pallas_call | solution.py:332
  37.6 5.1 %collective-permute-done.10.model_next = f32[6,64,128]{2,1,0:T(8,128)S(1)} collective-permute-done((f32[6,64,128]{2,1,0:T(8,128)S(1)}, f32[6,64,128]{2,1,0:T(8,128)S(1)}, u32[]{:S(2)}, u32[]{:S(2)}) %collective-permute-start.10) | collective-permute-done | bytes 196640 | tf_op jit(solution)/shard_map/ppermute | solution.py:299
  42.7 0.0 collective-permute-done.9.model_prev
  42.7 4.8 %march.1 = (f32[16,32,128]{2,1,0:T(8,128)S(1)}, f32[16,32,128]{2,1,0:T(8,128)S(1)}) custom-call(s32[32]{0:T(128)S(1)} %copy-done, f32[4,8,64,128]{3,2,1,0:T(8,128)S(1)} %bitcast.13, f32[15,64,128]{2,1,0:T(8,128)S(1)} %collective-permute-done.7.prev, f32[13,64,128]{2,1,0:T(8,128)S(1)} %collective-permute-done.8.nxt, ...), custom_call_target="tpu_custom_call" | custom-call | tf_op jit(solution)/shard_map/march/pallas_call | solution.py:256
  47.5 0.1 collective-permute-start.11
  47.6 1.5 %collective-permute-done.11.got = f32[16,32,128]{2,1,0:T(8,128)S(1)} collective-permute-done((f32[16,32,128]{2,1,0:T(8,128)S(1)}, f32[16,32,128]{2,1,0:T(8,128)S(1)}, u32[]{:S(2)}, u32[]{:S(2)}) %collective-permute-start.11) | collective-permute-done | bytes 262176 | tf_op jit(solution)/shard_map/ppermute | solution.py:295
  49.1 0.2 collective-permute-start.12
  49.3 2.7 %collective-permute-start.13 = (f32[4,32,128]{2,1,0:T(8,128)S(1)}, f32[4,32,128]{2,1,0:T(8,128)S(1)}, u32[]{:S(2)}, u32[]{:S(2)}) collective-permute-start(f32[4,32,128]{2,1,0:T(8,128)S(1)} %get-tuple-element.57), channel_id=1, source_target_pairs={{0,128},{64,192},{128,0},{192,64},{1,129},{65,193},{129,1},{193,65... | collective-permute-start | bytes 196616 | tf_op jit(solution)/shard_map/ppermute | solution.py:303
  52.1 1.4 %collective-permute-start.14 = (f32[4,32,128]{2,1,0:T(8,128)S(1)}, f32[4,32,128]{2,1,0:T(8,128)S(1)}, u32[]{:S(2)}, u32[]{:S(2)}) collective-permute-start(f32[4,32,128]{2,1,0:T(8,128)S(1)} %get-tuple-element.58), channel_id=1, source_target_pairs={{0,192},{64,0},{128,64},{192,128},{1,193},{65,1},{129,65},{193,129... | collective-permute-start | bytes 196616 | tf_op jit(solution)/shard_map/ppermute | solution.py:303
  53.5 2.5 %collective-permute-done.12.r1 = f32[4,32,128]{2,1,0:T(8,128)S(1)} collective-permute-done((f32[4,32,128]{2,1,0:T(8,128)S(1)}, f32[4,32,128]{2,1,0:T(8,128)S(1)}, u32[]{:S(2)}, u32[]{:S(2)}) %collective-permute-start.12) | collective-permute-done | bytes 65568 | tf_op jit(solution)/shard_map/ppermute | solution.py:303
  56.0 0.0 collective-permute-done.13.r2
  56.0 0.6 collective-permute-done.14.r3
  56.6 1.9 %collective-permute-start.15 = (f32[32,128]{1,0:T(8,128)S(1)}, f32[32,128]{1,0:T(8,128)S(1)}, u32[]{:S(2)}, u32[]{:S(2)}) collective-permute-start(f32[32,128]{1,0:T(8,128)S(1)} %get-tuple-element.60), channel_id=1, source_target_pairs={{0,16},{16,32},{32,48},{48,0},{1,17},{17,33},{33,49},{49,1},{2,18}... | collective-permute-start | bytes 49160 | tf_op jit(solution)/shard_map/ppermute | solution.py:303
  58.4 2.5 %collective-permute-start.16 = (f32[32,128]{1,0:T(8,128)S(1)}, f32[32,128]{1,0:T(8,128)S(1)}, u32[]{:S(2)}, u32[]{:S(2)}) collective-permute-start(f32[32,128]{1,0:T(8,128)S(1)} %get-tuple-element.61), channel_id=1, source_target_pairs={{0,32},{16,48},{32,0},{48,16},{1,33},{17,49},{33,1},{49,17},{2,34}... | collective-permute-start | bytes 49160 | tf_op jit(solution)/shard_map/ppermute | solution.py:303
  60.9 3.9 %collective-permute-start.17 = (f32[32,128]{1,0:T(8,128)S(1)}, f32[32,128]{1,0:T(8,128)S(1)}, u32[]{:S(2)}, u32[]{:S(2)}) collective-permute-start(f32[32,128]{1,0:T(8,128)S(1)} %get-tuple-element.62), channel_id=1, source_target_pairs={{0,48},{16,0},{32,16},{48,32},{1,49},{17,1},{33,17},{49,33},{2,50}... | collective-permute-start | bytes 49160 | tf_op jit(solution)/shard_map/ppermute | solution.py:303
  64.8 0.0 collective-permute-done.15.q1
  64.8 1.3 %collective-permute-done.16.q2 = f32[32,128]{1,0:T(8,128)S(1)} collective-permute-done((f32[32,128]{1,0:T(8,128)S(1)}, f32[32,128]{1,0:T(8,128)S(1)}, u32[]{:S(2)}, u32[]{:S(2)}) %collective-permute-start.16) | collective-permute-done | bytes 16416 | tf_op jit(solution)/shard_map/ppermute | solution.py:303
  66.1 0.1 collective-permute-done.17.q3
  66.2 0.6 last.1
  (3 shorter events, 0.1 us)
Async XLA Ops:
  0.0 30.0 %copy-start = (s32[32]{0:T(128)S(1)}, s32[32]{0:T(128)}, u32[]{:S(2)}) copy-start(s32[32]{0:T(128)} %anchors.5) | copy-start | bytes 388
  0.0 35.6 %copy-start.2 = (f32[1,128,4]{1,2,0:T(4,128)S(1)}, f32[1,128,4]{1,2,0:T(4,128)}, u32[]{:S(2)}) copy-start(f32[1,128,4]{1,2,0:T(4,128)} %param.17) | copy-start | bytes 6148
  0.0 35.6 %copy-start.4 = (s32[1,128]{1,0:T(1,128)S(1)}, s32[1,128]{1,0:T(1,128)}, u32[]{:S(2)}) copy-start(s32[1,128]{1,0:T(1,128)} %rec_pos.1) | copy-start | bytes 1540
  0.0 35.6 %copy-start.1 = (f32[1,16,4]{1,2,0:T(4,128)S(1)}, f32[1,16,4]{1,2,0:T(4,128)}, u32[]{:S(2)}) copy-start(f32[1,16,4]{1,2,0:T(4,128)} %param.15) | copy-start | bytes 772
  0.0 35.6 %copy-start.3 = (s32[1,16]{1,0:T(1,128)S(1)}, s32[1,16]{1,0:T(1,128)}, u32[]{:S(2)}) copy-start(s32[1,16]{1,0:T(1,128)} %src_pos.1) | copy-start | bytes 196
  0.8 12.8 %collective-permute-start.2 = (f32[1,2,4,8,128]{4,3,2,1,0:T(8,128)S(1)}, f32[1,2,4,8,128]{4,3,2,1,0:T(8,128)S(1)}, u32[]{:S(2)}, u32[]{:S(2)}) collective-permute-start(f32[1,2,4,8,128]{4,3,2,1,0:T(8,128)S(1)} %maximum_bitcast_fusion), channel_id=1, source_target_pairs={{0,48},{16,0},{32,16},{48,32},{1,49},{17,1},{33,17},{49,33},{2,50}... | collective-permute-start | bytes 98312 | tf_op jit(solution)/shard_map/ppermute | solution.py:303
  7.1 8.0 %collective-permute-start.1 = (f32[1,2,4,8,128]{4,3,2,1,0:T(8,128)S(1)}, f32[1,2,4,8,128]{4,3,2,1,0:T(8,128)S(1)}, u32[]{:S(2)}, u32[]{:S(2)}) collective-permute-start(f32[1,2,4,8,128]{4,3,2,1,0:T(8,128)S(1)} %maximum_bitcast_fusion), channel_id=1, source_target_pairs={{0,32},{16,48},{32,0},{48,16},{1,33},{17,49},{33,1},{49,17},{2,34}... | collective-permute-start | bytes 98312 | tf_op jit(solution)/shard_map/ppermute | solution.py:303
  8.0 7.1 %collective-permute-start = (f32[1,2,4,8,128]{4,3,2,1,0:T(8,128)S(1)}, f32[1,2,4,8,128]{4,3,2,1,0:T(8,128)S(1)}, u32[]{:S(2)}, u32[]{:S(2)}) collective-permute-start(f32[1,2,4,8,128]{4,3,2,1,0:T(8,128)S(1)} %maximum_bitcast_fusion), channel_id=1, source_target_pairs={{0,16},{16,32},{32,48},{48,0},{1,17},{17,33},{33,49},{49,1},{2,18}... | collective-permute-start | bytes 98312 | tf_op jit(solution)/shard_map/ppermute | solution.py:303
  15.1 17.4 %collective-permute-start.8 = (f32[13,64,128]{2,1,0:T(8,128)S(1)}, f32[13,64,128]{2,1,0:T(8,128)S(1)}, u32[]{:S(2)}, u32[]{:S(2)}) collective-permute-start(f32[13,64,128]{2,1,0:T(8,128)S(1)} %get-tuple-element.43), channel_id=1, source_target_pairs={{0,7},{1,0},{2,1},{3,2},{4,3},{5,4},{6,5},{7,6},{8,15},{9,8},{10,9... | collective-permute-start | bytes 1277960 | tf_op jit(solution)/shard_map/ppermute | solution.py:299
  15.8 16.6 %collective-permute-start.7 = (f32[15,64,128]{2,1,0:T(8,128)S(1)}, f32[15,64,128]{2,1,0:T(8,128)S(1)}, u32[]{:S(2)}, u32[]{:S(2)}) collective-permute-start(f32[15,64,128]{2,1,0:T(8,128)S(1)} %get-tuple-element.42.mine), channel_id=1, source_target_pairs={{0,1},{1,2},{2,3},{3,4},{4,5},{5,6},{6,7},{7,0},{8,9},{9,10},{10,1... | collective-permute-start | bytes 1474568 | tf_op jit(solution)/shard_map/ppermute | solution.py:299
  19.2 6.8 %collective-permute-start.5 = (f32[4,2,4,8,128]{4,3,2,1,0:T(8,128)S(1)}, f32[4,2,4,8,128]{4,3,2,1,0:T(8,128)S(1)}, u32[]{:S(2)}, u32[]{:S(2)}) collective-permute-start(f32[4,2,4,8,128]{4,3,2,1,0:T(8,128)S(1)} %pad_maximum_fusion.a0), channel_id=1, source_target_pairs={{0,192},{64,0},{128,64},{192,128},{1,193},{65,1},{129,65},{193,129... | collective-permute-start | bytes 393224 | tf_op jit(solution)/shard_map/ppermute | solution.py:303
  22.1 6.6 %collective-permute-start.4 = (f32[4,2,4,8,128]{4,3,2,1,0:T(8,128)S(1)}, f32[4,2,4,8,128]{4,3,2,1,0:T(8,128)S(1)}, u32[]{:S(2)}, u32[]{:S(2)}) collective-permute-start(f32[4,2,4,8,128]{4,3,2,1,0:T(8,128)S(1)} %pad_maximum_fusion.a0), channel_id=1, source_target_pairs={{0,128},{64,192},{128,0},{192,64},{1,129},{65,193},{129,1},{193,65... | collective-permute-start | bytes 393224 | tf_op jit(solution)/shard_map/ppermute | solution.py:303
  22.9 7.1 %collective-permute-start.3 = (f32[4,2,4,8,128]{4,3,2,1,0:T(8,128)S(1)}, f32[4,2,4,8,128]{4,3,2,1,0:T(8,128)S(1)}, u32[]{:S(2)}, u32[]{:S(2)}) collective-permute-start(f32[4,2,4,8,128]{4,3,2,1,0:T(8,128)S(1)} %pad_maximum_fusion.a0), channel_id=1, source_target_pairs={{0,64},{64,128},{128,192},{192,0},{1,65},{65,129},{129,193},{193,1... | collective-permute-start | bytes 393224 | tf_op jit(solution)/shard_map/ppermute | solution.py:303
  30.8 1.6 %collective-permute-start.6 = (f32[8,2,4,8,128]{4,3,2,1,0:T(8,128)S(1)}, f32[8,2,4,8,128]{4,3,2,1,0:T(8,128)S(1)}, u32[]{:S(2)}, u32[]{:S(2)}) collective-permute-start(f32[8,2,4,8,128]{4,3,2,1,0:T(8,128)S(1)} %get-tuple-element.41), channel_id=1, source_target_pairs={{0,8},{8,0},{1,9},{9,1},{2,10},{10,2},{3,11},{11,3},{4,12},{12,4},... | collective-permute-start | bytes 786440 | tf_op jit(solution)/shard_map/ppermute | solution.py:295
  33.5 9.2 %collective-permute-start.9 = (f32[7,64,128]{2,1,0:T(8,128)S(1)}, f32[7,64,128]{2,1,0:T(8,128)S(1)}, u32[]{:S(2)}, u32[]{:S(2)}) collective-permute-start(f32[7,64,128]{2,1,0:T(8,128)S(1)} %get-tuple-element.49), channel_id=1, source_target_pairs={{0,1},{1,2},{2,3},{3,4},{4,5},{5,6},{6,7},{7,0},{8,9},{9,10},{10,1... | collective-permute-start | bytes 688136 | tf_op jit(solution)/shard_map/ppermute | solution.py:299
  33.6 9.1 %collective-permute-start.10 = (f32[6,64,128]{2,1,0:T(8,128)S(1)}, f32[6,64,128]{2,1,0:T(8,128)S(1)}, u32[]{:S(2)}, u32[]{:S(2)}) collective-permute-start(f32[6,64,128]{2,1,0:T(8,128)S(1)} %get-tuple-element.50), channel_id=1, source_target_pairs={{0,7},{1,0},{2,1},{3,2},{4,3},{5,4},{6,5},{7,6},{8,15},{9,8},{10,9... | collective-permute-start | bytes 589832 | tf_op jit(solution)/shard_map/ppermute | solution.py:299
  47.5 1.6 %collective-permute-start.11 = (f32[16,32,128]{2,1,0:T(8,128)S(1)}, f32[16,32,128]{2,1,0:T(8,128)S(1)}, u32[]{:S(2)}, u32[]{:S(2)}) collective-permute-start(f32[16,32,128]{2,1,0:T(8,128)S(1)} %get-tuple-element.54), channel_id=1, source_target_pairs={{0,8},{8,0},{1,9},{9,1},{2,10},{10,2},{3,11},{11,3},{4,12},{12,4},... | collective-permute-start | bytes 786440 | tf_op jit(solution)/shard_map/ppermute | solution.py:295
  49.1 6.8 %collective-permute-start.12 = (f32[4,32,128]{2,1,0:T(8,128)S(1)}, f32[4,32,128]{2,1,0:T(8,128)S(1)}, u32[]{:S(2)}, u32[]{:S(2)}) collective-permute-start(f32[4,32,128]{2,1,0:T(8,128)S(1)} %get-tuple-element.56), channel_id=1, source_target_pairs={{0,64},{64,128},{128,192},{192,0},{1,65},{65,129},{129,193},{193,1... | collective-permute-start | bytes 196616 | tf_op jit(solution)/shard_map/ppermute | solution.py:303
  49.3 6.6 %collective-permute-start.13 = (f32[4,32,128]{2,1,0:T(8,128)S(1)}, f32[4,32,128]{2,1,0:T(8,128)S(1)}, u32[]{:S(2)}, u32[]{:S(2)}) collective-permute-start(f32[4,32,128]{2,1,0:T(8,128)S(1)} %get-tuple-element.57), channel_id=1, source_target_pairs={{0,128},{64,192},{128,0},{192,64},{1,129},{65,193},{129,1},{193,65... | collective-permute-start | bytes 196616 | tf_op jit(solution)/shard_map/ppermute | solution.py:303
  52.1 4.5 %collective-permute-start.14 = (f32[4,32,128]{2,1,0:T(8,128)S(1)}, f32[4,32,128]{2,1,0:T(8,128)S(1)}, u32[]{:S(2)}, u32[]{:S(2)}) collective-permute-start(f32[4,32,128]{2,1,0:T(8,128)S(1)} %get-tuple-element.58), channel_id=1, source_target_pairs={{0,192},{64,0},{128,64},{192,128},{1,193},{65,1},{129,65},{193,129... | collective-permute-start | bytes 196616 | tf_op jit(solution)/shard_map/ppermute | solution.py:303
  56.6 8.2 %collective-permute-start.15 = (f32[32,128]{1,0:T(8,128)S(1)}, f32[32,128]{1,0:T(8,128)S(1)}, u32[]{:S(2)}, u32[]{:S(2)}) collective-permute-start(f32[32,128]{1,0:T(8,128)S(1)} %get-tuple-element.60), channel_id=1, source_target_pairs={{0,16},{16,32},{32,48},{48,0},{1,17},{17,33},{33,49},{49,1},{2,18}... | collective-permute-start | bytes 49160 | tf_op jit(solution)/shard_map/ppermute | solution.py:303
  58.4 7.7 %collective-permute-start.16 = (f32[32,128]{1,0:T(8,128)S(1)}, f32[32,128]{1,0:T(8,128)S(1)}, u32[]{:S(2)}, u32[]{:S(2)}) collective-permute-start(f32[32,128]{1,0:T(8,128)S(1)} %get-tuple-element.61), channel_id=1, source_target_pairs={{0,32},{16,48},{32,0},{48,16},{1,33},{17,49},{33,1},{49,17},{2,34}... | collective-permute-start | bytes 49160 | tf_op jit(solution)/shard_map/ppermute | solution.py:303
  60.9 5.3 %collective-permute-start.17 = (f32[32,128]{1,0:T(8,128)S(1)}, f32[32,128]{1,0:T(8,128)S(1)}, u32[]{:S(2)}, u32[]{:S(2)}) collective-permute-start(f32[32,128]{1,0:T(8,128)S(1)} %get-tuple-element.62), channel_id=1, source_target_pairs={{0,48},{16,0},{32,16},{48,32},{1,49},{17,1},{33,17},{49,33},{2,50}... | collective-permute-start | bytes 49160 | tf_op jit(solution)/shard_map/ppermute | solution.py:303

commit v3 on v2

--- a/solution.py
+++ b/solution.py
@@ -8,6 +8,7 @@
 
 STEPS = 4
 UNROLL = 2
+GATHER, SCATTER = (3, 1, 2), (2, 1, 3)
 F32 = jnp.float32
 ROWS = 64
 COLS = 8
@@ -104,31 +105,31 @@
         lax.fori_loop(0, pos.shape[1], point, 0, unroll=8)
 
 
-def window_kernel(anchors, a0, a1, a2, a3, own, other):
+def window_kernel(anchors, a0, a1, a2, a3, own_m, own_b, other_m, other_b):
     x, z = lax.axis_index("x"), lax.axis_index("zh")
     c, g = place()
-    for group, out in ((g, own), (g + 1 - 2 * c, other)):
+    for group, out in ((g, (own_m, own_b)), (g + 1 - 2 * c, (other_m, other_b))):
         first = first_strip(anchors[group], c)
-        for dx, strips in enumerate((a0, a1, a2, a3)):
-            for dz in range(NZH):
+        for dx, strips in zip((0, *GATHER), (a0, a1, a2, a3)):
+            for dz, at in zip((0, *GATHER), range(NZH)):
                 i = ((x - dx) & (NX - 1)) * NZH + ((z - dz) & (NZH - 1)) - first
 
                 @pl.when((i >= 0) & (i < 8))
-                def _(i=i, strips=strips, dz=dz, out=out):
-                    vel, den = strips[dz, 0], strips[dz, 1]
-                    out[i, 0] = den * vel * vel
-                    out[i, 1] = 1.0 / den
-
-
-def model_kernel(anchors, own, other, out, to_prev, to_next):
+                def _(i=i, strips=strips, at=at, out=out):
+                    vel, den = strips[at, 0], strips[at, 1]
+                    out[0][i] = den * vel * vel
+                    out[1][i] = 1.0 / den
+
+
+def model_kernel(anchors, own_m, own_b, other_m, other_b, out, to_prev, to_next):
     c, g = place()
     odd = (c + anchors[g]) & 1
-    for strips, start in ((own, odd), (other, 1 - odd)):
+    for strips, start in (((own_m, own_b), odd), ((other_m, other_b), 1 - odd)):
         for i in range(8):
             for r in range(4):
                 x = 4 * (start + 2 * i) + r
                 for f in range(2):
-                    out[f, pl.ds(x, COLS, stride=ROWS), :] = strips[i, f, r]
+                    out[f, pl.ds(x, COLS, stride=ROWS), :] = strips[f][i, r]
 
     def plane(f, y):
         return out[f, y * ROWS : (y + 1) * ROWS, :]
@@ -299,14 +300,14 @@
     return lax.ppermute(block, "tile", [(i, (i + distance) % NT) for i in range(NT)])
 
 
-def along(block, axis, distance):
-    return lax.ppermute(block, axis, [(i, (i + distance) % 4) for i in range(4)])
+def along(blocks, axis, order):
+    return [lax.ppermute(blocks[d - 1], axis, [(i, (i + d) % 4) for i in range(4)]) for d in order]
 
 
 def local(velocity, density, anchors, src_state, rcv_state, src_pos, wavelet, rec_pos, traces):
     plane = (ROWS, DEPTH)
     strip = jnp.stack([velocity, density])[None]
-    zs = [along(strip, "zh", d) for d in range(1, NZH)]
+    zs = along([strip] * 3, "zh", GATHER)
 
     own, to_prev, to_next = pl.pallas_call(
         pack_kernel,
@@ -324,7 +325,7 @@
     *zs, own, to_prev, to_next = lax.optimization_barrier((*zs, own, to_prev, to_next))
 
     xs = [jnp.concatenate([strip, *zs])]
-    xs += [along(xs[0], "x", d) for d in range(1, NX)]
+    xs += along([xs[0]] * 3, "x", GATHER)
 
     halo_next = to_tile(to_prev, -1)
     halo_prev = to_tile(to_next, 1)
@@ -338,25 +339,24 @@
         name="inject",
     )(src_pos, wavelet[0].T, rec_pos, traces[0].T)
 
-    mine, other = pl.pallas_call(
+    *mine, other_m, other_b = pl.pallas_call(
         window_kernel,
-        out_shape=[shape(8, *strip.shape[1:])] * 2,
+        out_shape=[shape(8, *strip.shape[2:])] * 4,
         in_specs=[SMEM] + [VMEM] * 4,
-        out_specs=[VMEM] * 2,
+        out_specs=[VMEM] * 4,
         compiler_params=params(2),
         name="window",
     )(anchors, *xs)
-    got = other_core(other)
-    got, halo_prev, halo_next = lax.optimization_barrier((got, halo_prev, halo_next))
+    got = [other_core(o) for o in (other_m, other_b)]
 
     mb, mb_prev, mb_next = pl.pallas_call(
         model_kernel,
         out_shape=[shape(2, COLS * ROWS, DEPTH), shape(6, *plane), shape(7, *plane)],
-        in_specs=[SMEM, VMEM, VMEM],
+        in_specs=[SMEM] + [VMEM] * 4,
         out_specs=[VMEM] * 3,
         compiler_params=params(2),
         name="model",
-    )(anchors, mine, got)
+    )(anchors, *mine, *got)
     model_next = to_tile(mb_prev, -1)
     model_prev = to_tile(mb_next, 1)
 
@@ -381,7 +381,7 @@
         compiler_params=params(2),
         name="halve",
     )(keep, other_core(send))
-    moved = [along(parts[d], "x", d) for d in range(1, NX)]
+    moved = along(parts[1:], "x", SCATTER)
     parts = pl.pallas_call(
         quarter_kernel,
         out_shape=[shape(32, DEPTH)] * NZH,
@@ -390,7 +390,7 @@
         compiler_params=params(2),
         name="quarter",
     )(parts[0], *moved)
-    moved = [along(parts[d], "zh", d) for d in range(1, NZH)]
+    moved = along(parts[1:], "zh", SCATTER)
     image = pl.pallas_call(
         last_kernel,
         out_shape=shape(32, DEPTH),

time: 67.1 us -> 63.5 us (0.946)
  waiting for transfers between devices: 20.4 us -> 17.7 us
  starting transfers between devices: 33.6 us -> 32.8 us
    ppermute x12, waiting for transfers between devices: 12.2 us -> 8.58 us  [along(): lax.ppermute(blocks[d - 1], axis, [(i, (i + d) % 4) for i in range(4)])]
    ppermute x4, starting transfers between devices: 6.23 us -> 4.13 us  [to_tile(): lax.ppermute(block, 'tile', [(i, (i + distance) % NT) for i in range(NT)])]
    ppermute x4, waiting for transfers between devices: 5.14 us -> 6.52 us  [to_tile(): lax.ppermute(block, 'tile', [(i, (i + distance) % NT) for i in range(NT)])]
    ppermute x12, starting transfers between devices: 27.2 us -> 28 us  [along(): lax.ppermute(blocks[d - 1], axis, [(i, (i + d) % 4) for i in range(4)])]
    ppermute x2 -> x3, waiting for transfers between devices: 3.04 us -> 2.55 us  [other_core(): return lax.ppermute(block, 'core', [(0, 1), (1, 0)])]
  transfers between devices with their start and end apart: 18 -> 19, of which waited for: 11 -> 12; matrix products, arithmetic and copies ran while one was open for 0% -> 0% of each run, Pallas kernels for 8% -> 10%
where the time goes in v3:
time: 63.5 us; the launch traced here: 63.3 us
  starting transfers between devices  32.8 us (52%)
  waiting for transfers between devices  17.7 us (28%)
  Pallas kernels  11.9 us (19%)
  other arithmetic  0.8 us (1%)
    ppermute x12, starting transfers between devices, along(): lax.ppermute(blocks[d - 1], axis, [(i, (i + d) % 4) for i in range(4)])  28 us
    ppermute x12, waiting for transfers between devices, along(): lax.ppermute(blocks[d - 1], axis, [(i, (i + d) % 4) for i in range(4)])  8.58 us
    ppermute x4, waiting for transfers between devices, to_tile(): lax.ppermute(block, 'tile', [(i, (i + distance) % NT) for i in range(NT)])  6.52 us
    pallas_call x1, Pallas kernels, march(): pl.pallas_call(march_kernel, out_shape=[shape(16, 32, DEPTH)] * 2, in_spe...  4.8 us
    ppermute x4, starting transfers between devices, to_tile(): lax.ppermute(block, 'tile', [(i, (i + distance) % NT) for i in range(NT)])  4.13 us
    pallas_call x1, Pallas kernels, local(): pl.pallas_call(pack_kernel, out_shape=[shape(4, COLS * ROWS, DEPTH), shap...  2.63 us
    ppermute x3, waiting for transfers between devices, other_core(): return lax.ppermute(block, 'core', [(0, 1), (1, 0)])  2.55 us
    pallas_call x1, Pallas kernels, local(): pl.pallas_call(inject_kernel, out_shape=[shape(STEPS, PLANES, *plane)] *...  1.97 us
  transfers between devices with their start and end apart: 19, of which 12 were waited for; matrix products, arithmetic and copies ran while one was open for 0% of the time, Pallas kernels for 10%

profile of v3, /device:TPU:24, one launch (start us, length us, event | category | flops | bytes accessed | tf_op | source)
XLA Modules:
  0.0 63.3 jit_solution(515311510224578430)
XLA Ops:
  0.0 0.0 copy-start
  0.0 0.0 copy-start.2
  0.0 0.0 copy-start.4
  0.0 0.0 copy-start.1
  0.0 0.0 copy-start.3
  0.0 0.8 %maximum_bitcast_fusion = f32[1,2,4,8,128]{4,3,2,1,0:T(8,128)S(1)} fusion(f32[1,4,8,128]{3,2,1,0:T(8,128)} %bitcast.17, f32[1,4,8,128]{3,2,1,0:T(8,128)} %bitcast.18), kind=kLoop, calls=%fused_computation.1 | loop fusion | flops 8192 | bytes 65536 | tf_op jit(solution)/shard_map/broadcast_in_dim | solution.py:309
  0.8 7.2 %collective-permute-start.2 = (f32[1,2,4,8,128]{4,3,2,1,0:T(8,128)S(1)}, f32[1,2,4,8,128]{4,3,2,1,0:T(8,128)S(1)}, u32[]{:S(2)}, u32[]{:S(2)}) collective-permute-start(f32[1,2,4,8,128]{4,3,2,1,0:T(8,128)S(1)} %maximum_bitcast_fusion), channel_id=1, source_target_pairs={{0,32},{16,48},{32,0},{48,16},{1,33},{17,49},{33,1},{49,17},{2,34}... | collective-permute-start | bytes 98312 | tf_op jit(solution)/shard_map/ppermute | solution.py:304
  8.0 1.5 %collective-permute-start.1 = (f32[1,2,4,8,128]{4,3,2,1,0:T(8,128)S(1)}, f32[1,2,4,8,128]{4,3,2,1,0:T(8,128)S(1)}, u32[]{:S(2)}, u32[]{:S(2)}) collective-permute-start(f32[1,2,4,8,128]{4,3,2,1,0:T(8,128)S(1)} %maximum_bitcast_fusion), channel_id=1, source_target_pairs={{0,16},{16,32},{32,48},{48,0},{1,17},{17,33},{33,49},{49,1},{2,18}... | collective-permute-start | bytes 98312 | tf_op jit(solution)/shard_map/ppermute | solution.py:304
  9.5 2.7 %collective-permute-start = (f32[1,2,4,8,128]{4,3,2,1,0:T(8,128)S(1)}, f32[1,2,4,8,128]{4,3,2,1,0:T(8,128)S(1)}, u32[]{:S(2)}, u32[]{:S(2)}) collective-permute-start(f32[1,2,4,8,128]{4,3,2,1,0:T(8,128)S(1)} %maximum_bitcast_fusion), channel_id=1, source_target_pairs={{0,48},{16,0},{32,16},{48,32},{1,49},{17,1},{33,17},{49,33},{2,50}... | collective-permute-start | bytes 98312 | tf_op jit(solution)/shard_map/ppermute | solution.py:304
  12.1 2.6 %pack.1 = (f32[4,512,128]{2,1,0:T(8,128)S(1)}, f32[13,64,128]{2,1,0:T(8,128)S(1)}, f32[15,64,128]{2,1,0:T(8,128)S(1)}) custom-call(f32[4,64,8,128]{3,2,1,0:T(8,128)} %src_in.1, f32[4,64,8,128]{3,2,1,0:T(8,128)} %rcv_in.1), custom_call_target="tpu_custom_call" | custom-call | tf_op jit(solution)/shard_map/pack/pallas_call | solution.py:312
  14.8 0.0 collective-permute-done.2
  14.8 0.0 collective-permute-done.1
  14.8 0.0 collective-permute-done
  14.8 3.1 %collective-permute-start.7 = (f32[4,2,4,8,128]{4,3,2,1,0:T(8,128)S(1)}, f32[4,2,4,8,128]{4,3,2,1,0:T(8,128)S(1)}, u32[]{:S(2)}, u32[]{:S(2)}) collective-permute-start(f32[4,2,4,8,128]{4,3,2,1,0:T(8,128)S(1)} %pad_maximum_fusion.a0), channel_id=1, source_target_pairs={{0,128},{64,192},{128,0},{192,64},{1,129},{65,193},{129,1},{193,65... | collective-permute-start | bytes 393224 | tf_op jit(solution)/shard_map/ppermute | solution.py:304
  17.9 0.6 collective-permute-start.6
  18.5 2.6 %collective-permute-start.5 = (f32[4,2,4,8,128]{4,3,2,1,0:T(8,128)S(1)}, f32[4,2,4,8,128]{4,3,2,1,0:T(8,128)S(1)}, u32[]{:S(2)}, u32[]{:S(2)}) collective-permute-start(f32[4,2,4,8,128]{4,3,2,1,0:T(8,128)S(1)} %pad_maximum_fusion.a0), channel_id=1, source_target_pairs={{0,192},{64,0},{128,64},{192,128},{1,193},{65,1},{129,65},{193,129... | collective-permute-start | bytes 393224 | tf_op jit(solution)/shard_map/ppermute | solution.py:304
  21.2 0.7 %collective-permute-start.3 = (f32[15,64,128]{2,1,0:T(8,128)S(1)}, f32[15,64,128]{2,1,0:T(8,128)S(1)}, u32[]{:S(2)}, u32[]{:S(2)}) collective-permute-start(f32[15,64,128]{2,1,0:T(8,128)S(1)} %get-tuple-element.37.mine), channel_id=1, source_target_pairs={{0,1},{1,2},{2,3},{3,4},{4,5},{5,6},{6,7},{7,0},{8,9},{9,10},{10,1... | collective-permute-start | bytes 1474568 | tf_op jit(solution)/shard_map/ppermute | solution.py:300
  21.9 1.3 %collective-permute-start.4 = (f32[13,64,128]{2,1,0:T(8,128)S(1)}, f32[13,64,128]{2,1,0:T(8,128)S(1)}, u32[]{:S(2)}, u32[]{:S(2)}) collective-permute-start(f32[13,64,128]{2,1,0:T(8,128)S(1)} %get-tuple-element.38), channel_id=1, source_target_pairs={{0,7},{1,0},{2,1},{3,2},{4,3},{5,4},{6,5},{7,6},{8,15},{9,8},{10,9... | collective-permute-start | bytes 1277960 | tf_op jit(solution)/shard_map/ppermute | solution.py:300
  23.2 0.0 collective-permute-done.7.a3
  23.2 1.2 %collective-permute-done.6.a2 = f32[4,2,4,8,128]{4,3,2,1,0:T(8,128)S(1)} collective-permute-done((f32[4,2,4,8,128]{4,3,2,1,0:T(8,128)S(1)}, f32[4,2,4,8,128]{4,3,2,1,0:T(8,128)S(1)}, u32[]{:S(2)}, u32[]{:S(2)}) %collective-permute-start.6) | collective-permute-done | bytes 131104 | tf_op jit(solution)/shard_map/ppermute | solution.py:304
  24.4 0.0 collective-permute-done.5.a1
  24.4 0.0 copy-done
  24.4 0.9 %window.1 = (f32[8,4,8,128]{3,2,1,0:T(8,128)S(1)}, f32[8,4,8,128]{3,2,1,0:T(8,128)S(1)}, f32[8,4,8,128]{3,2,1,0:T(8,128)S(1)}, f32[8,4,8,128]{3,2,1,0:T(8,128)S(1)}) custom-call(s32[32]{0:T(128)S(1)} %copy-done, f32[4,2,4,8,128]{4,3,2,1,0:T(8,128)S(1)} %pad_maximum_fusion.a0, f32[4,2,4,8,128]{4,3,2,1,0:T(8,128)S(1)} %collective-permute-done.5.a1, ...), custom_call_target="tpu_custom_call" | custom-call | tf_op jit(solution)/shard_map/window/pallas_call | solution.py:342
  25.3 0.1 collective-permute-start.8
  25.4 0.5 collective-permute-start.9
  25.9 0.8 %collective-permute-done.8.other_m = f32[8,4,8,128]{3,2,1,0:T(8,128)S(1)} collective-permute-done((f32[8,4,8,128]{3,2,1,0:T(8,128)S(1)}, f32[8,4,8,128]{3,2,1,0:T(8,128)S(1)}, u32[]{:S(2)}, u32[]{:S(2)}) %collective-permute-start.8) | collective-permute-done | bytes 131104 | tf_op jit(solution)/shard_map/ppermute | solution.py:296
  26.7 0.2 collective-permute-done.9.other_b
  26.9 1.0 %model.1 = (f32[2,512,128]{2,1,0:T(8,128)S(1)}, f32[6,64,128]{2,1,0:T(8,128)S(1)}, f32[7,64,128]{2,1,0:T(8,128)S(1)}) custom-call(s32[32]{0:T(128)S(1)} %copy-done, f32[8,4,8,128]{3,2,1,0:T(8,128)S(1)} %get-tuple-element.42.own_m, f32[8,4,8,128]{3,2,1,0:T(8,128)S(1)} %get-tuple-element.43.own_b, f32[8,4,8,128]{3,2,1,0:T(8,128)S(1)} %collective-permute-done.8.other_m, ...), custom_call_target="tpu_custom_call" | custom-call | tf_op jit(solution)/shard_map/model/pallas_call | solution.py:352
  27.9 1.7 %collective-permute-start.10 = (f32[7,64,128]{2,1,0:T(8,128)S(1)}, f32[7,64,128]{2,1,0:T(8,128)S(1)}, u32[]{:S(2)}, u32[]{:S(2)}) collective-permute-start(f32[7,64,128]{2,1,0:T(8,128)S(1)} %get-tuple-element.47), channel_id=1, source_target_pairs={{0,1},{1,2},{2,3},{3,4},{4,5},{5,6},{6,7},{7,0},{8,9},{9,10},{10,1... | collective-permute-start | bytes 688136 | tf_op jit(solution)/shard_map/ppermute | solution.py:300
  29.6 0.5 collective-permute-start.11
  30.0 0.0 copy-done.2
  30.0 0.0 copy-done.4
  30.0 0.0 copy-done.1
  30.1 0.0 copy-done.3
  30.1 2.0 %inject.1 = (f32[4,16,64,128]{3,2,1,0:T(8,128)S(1)}, f32[4,16,64,128]{3,2,1,0:T(8,128)S(1)}) custom-call(s32[1,16]{1,0:T(1,128)S(1)} %copy-done.3, f32[4,16]{1,0:T(4,128)S(1)} %bitcast.15, s32[1,128]{1,0:T(1,128)S(1)} %copy-done.4, f32[4,128]{1,0:T(4,128)S(1)} %bitcast.16), custom_call_target="tpu_custom_call" | custom-call | tf_op jit(solution)/shard_map/inject/pallas_call | solution.py:333
  32.0 1.5 %collective-permute-done.4.nxt = f32[13,64,128]{2,1,0:T(8,128)S(1)} collective-permute-done((f32[13,64,128]{2,1,0:T(8,128)S(1)}, f32[13,64,128]{2,1,0:T(8,128)S(1)}, u32[]{:S(2)}, u32[]{:S(2)}) %collective-permute-start.4) | collective-permute-done | bytes 426016 | tf_op jit(solution)/shard_map/ppermute | solution.py:300
  33.6 5.0 %collective-permute-done.11.model_next = f32[6,64,128]{2,1,0:T(8,128)S(1)} collective-permute-done((f32[6,64,128]{2,1,0:T(8,128)S(1)}, f32[6,64,128]{2,1,0:T(8,128)S(1)}, u32[]{:S(2)}, u32[]{:S(2)}) %collective-permute-start.11) | collective-permute-done | bytes 196640 | tf_op jit(solution)/shard_map/ppermute | solution.py:300
  38.6 0.0 collective-permute-done.10.model_prev
  38.6 0.0 collective-permute-done.3.prev
  38.6 4.8 %march.1 = (f32[16,32,128]{2,1,0:T(8,128)S(1)}, f32[16,32,128]{2,1,0:T(8,128)S(1)}) custom-call(s32[32]{0:T(128)S(1)} %copy-done, f32[4,8,64,128]{3,2,1,0:T(8,128)S(1)} %bitcast.13, f32[15,64,128]{2,1,0:T(8,128)S(1)} %collective-permute-done.3.prev, f32[13,64,128]{2,1,0:T(8,128)S(1)} %collective-permute-done.4.nxt, ...), custom_call_target="tpu_custom_call" | custom-call | tf_op jit(solution)/shard_map/march/pallas_call | solution.py:257
  43.4 0.1 collective-permute-start.12
  43.5 1.5 %collective-permute-done.12.got = f32[16,32,128]{2,1,0:T(8,128)S(1)} collective-permute-done((f32[16,32,128]{2,1,0:T(8,128)S(1)}, f32[16,32,128]{2,1,0:T(8,128)S(1)}, u32[]{:S(2)}, u32[]{:S(2)}) %collective-permute-start.12) | collective-permute-done | bytes 262176 | tf_op jit(solution)/shard_map/ppermute | solution.py:296
  45.0 0.9 %collective-permute-start.13 = (f32[4,32,128]{2,1,0:T(8,128)S(1)}, f32[4,32,128]{2,1,0:T(8,128)S(1)}, u32[]{:S(2)}, u32[]{:S(2)}) collective-permute-start(f32[4,32,128]{2,1,0:T(8,128)S(1)} %get-tuple-element.54), channel_id=1, source_target_pairs={{0,128},{64,192},{128,0},{192,64},{1,129},{65,193},{129,1},{193,65... | collective-permute-start | bytes 196616 | tf_op jit(solution)/shard_map/ppermute | solution.py:304
  45.9 2.1 %collective-permute-start.14 = (f32[4,32,128]{2,1,0:T(8,128)S(1)}, f32[4,32,128]{2,1,0:T(8,128)S(1)}, u32[]{:S(2)}, u32[]{:S(2)}) collective-permute-start(f32[4,32,128]{2,1,0:T(8,128)S(1)} %get-tuple-element.55), channel_id=1, source_target_pairs={{0,64},{64,128},{128,192},{192,0},{1,65},{65,129},{129,193},{193,1... | collective-permute-start | bytes 196616 | tf_op jit(solution)/shard_map/ppermute | solution.py:304
  48.0 1.2 %collective-permute-start.15 = (f32[4,32,128]{2,1,0:T(8,128)S(1)}, f32[4,32,128]{2,1,0:T(8,128)S(1)}, u32[]{:S(2)}, u32[]{:S(2)}) collective-permute-start(f32[4,32,128]{2,1,0:T(8,128)S(1)} %get-tuple-element.56), channel_id=1, source_target_pairs={{0,192},{64,0},{128,64},{192,128},{1,193},{65,1},{129,65},{193,129... | collective-permute-start | bytes 196616 | tf_op jit(solution)/shard_map/ppermute | solution.py:304
  49.1 2.3 %collective-permute-done.13.r1 = f32[4,32,128]{2,1,0:T(8,128)S(1)} collective-permute-done((f32[4,32,128]{2,1,0:T(8,128)S(1)}, f32[4,32,128]{2,1,0:T(8,128)S(1)}, u32[]{:S(2)}, u32[]{:S(2)}) %collective-permute-start.13) | collective-permute-done | bytes 65568 | tf_op jit(solution)/shard_map/ppermute | solution.py:304
  51.5 0.7 %collective-permute-done.14.r2 = f32[4,32,128]{2,1,0:T(8,128)S(1)} collective-permute-done((f32[4,32,128]{2,1,0:T(8,128)S(1)}, f32[4,32,128]{2,1,0:T(8,128)S(1)}, u32[]{:S(2)}, u32[]{:S(2)}) %collective-permute-start.14) | collective-permute-done | bytes 65568 | tf_op jit(solution)/shard_map/ppermute | solution.py:304
  52.1 0.1 collective-permute-done.15.r3
  52.3 2.1 %collective-permute-start.16 = (f32[32,128]{1,0:T(8,128)S(1)}, f32[32,128]{1,0:T(8,128)S(1)}, u32[]{:S(2)}, u32[]{:S(2)}) collective-permute-start(f32[32,128]{1,0:T(8,128)S(1)} %get-tuple-element.58), channel_id=1, source_target_pairs={{0,32},{16,48},{32,0},{48,16},{1,33},{17,49},{33,1},{49,17},{2,34}... | collective-permute-start | bytes 49160 | tf_op jit(solution)/shard_map/ppermute | solution.py:304
  54.3 3.7 %collective-permute-start.17 = (f32[32,128]{1,0:T(8,128)S(1)}, f32[32,128]{1,0:T(8,128)S(1)}, u32[]{:S(2)}, u32[]{:S(2)}) collective-permute-start(f32[32,128]{1,0:T(8,128)S(1)} %get-tuple-element.59), channel_id=1, source_target_pairs={{0,16},{16,32},{32,48},{48,0},{1,17},{17,33},{33,49},{49,1},{2,18}... | collective-permute-start | bytes 49160 | tf_op jit(solution)/shard_map/ppermute | solution.py:304
  58.1 0.4 collective-permute-start.18
  58.5 1.5 %collective-permute-done.16.q1 = f32[32,128]{1,0:T(8,128)S(1)} collective-permute-done((f32[32,128]{1,0:T(8,128)S(1)}, f32[32,128]{1,0:T(8,128)S(1)}, u32[]{:S(2)}, u32[]{:S(2)}) %collective-permute-start.16) | collective-permute-done | bytes 16416 | tf_op jit(solution)/shard_map/ppermute | solution.py:304
  60.0 0.2 collective-permute-done.17.q2
  60.2 2.5 %collective-permute-done.18.q3 = f32[32,128]{1,0:T(8,128)S(1)} collective-permute-done((f32[32,128]{1,0:T(8,128)S(1)}, f32[32,128]{1,0:T(8,128)S(1)}, u32[]{:S(2)}, u32[]{:S(2)}) %collective-permute-start.18) | collective-permute-done | bytes 16416 | tf_op jit(solution)/shard_map/ppermute | solution.py:304
  62.7 0.6 last.1
  (3 shorter events, 0.1 us)
Async XLA Ops:
  0.0 24.4 %copy-start = (s32[32]{0:T(128)S(1)}, s32[32]{0:T(128)}, u32[]{:S(2)}) copy-start(s32[32]{0:T(128)} %anchors.5) | copy-start | bytes 388
  0.0 30.0 %copy-start.2 = (f32[1,128,4]{1,2,0:T(4,128)S(1)}, f32[1,128,4]{1,2,0:T(4,128)}, u32[]{:S(2)}) copy-start(f32[1,128,4]{1,2,0:T(4,128)} %param.17) | copy-start | bytes 6148
  0.0 30.0 %copy-start.4 = (s32[1,128]{1,0:T(1,128)S(1)}, s32[1,128]{1,0:T(1,128)}, u32[]{:S(2)}) copy-start(s32[1,128]{1,0:T(1,128)} %rec_pos.1) | copy-start | bytes 1540
  0.0 30.0 %copy-start.1 = (f32[1,16,4]{1,2,0:T(4,128)S(1)}, f32[1,16,4]{1,2,0:T(4,128)}, u32[]{:S(2)}) copy-start(f32[1,16,4]{1,2,0:T(4,128)} %param.15) | copy-start | bytes 772
  0.0 30.0 %copy-start.3 = (s32[1,16]{1,0:T(1,128)S(1)}, s32[1,16]{1,0:T(1,128)}, u32[]{:S(2)}) copy-start(s32[1,16]{1,0:T(1,128)} %src_pos.1) | copy-start | bytes 196
  0.8 14.0 %collective-permute-start.2 = (f32[1,2,4,8,128]{4,3,2,1,0:T(8,128)S(1)}, f32[1,2,4,8,128]{4,3,2,1,0:T(8,128)S(1)}, u32[]{:S(2)}, u32[]{:S(2)}) collective-permute-start(f32[1,2,4,8,128]{4,3,2,1,0:T(8,128)S(1)} %maximum_bitcast_fusion), channel_id=1, source_target_pairs={{0,32},{16,48},{32,0},{48,16},{1,33},{17,49},{33,1},{49,17},{2,34}... | collective-permute-start | bytes 98312 | tf_op jit(solution)/shard_map/ppermute | solution.py:304
  8.0 6.8 %collective-permute-start.1 = (f32[1,2,4,8,128]{4,3,2,1,0:T(8,128)S(1)}, f32[1,2,4,8,128]{4,3,2,1,0:T(8,128)S(1)}, u32[]{:S(2)}, u32[]{:S(2)}) collective-permute-start(f32[1,2,4,8,128]{4,3,2,1,0:T(8,128)S(1)} %maximum_bitcast_fusion), channel_id=1, source_target_pairs={{0,16},{16,32},{32,48},{48,0},{1,17},{17,33},{33,49},{49,1},{2,18}... | collective-permute-start | bytes 98312 | tf_op jit(solution)/shard_map/ppermute | solution.py:304
  9.5 5.3 %collective-permute-start = (f32[1,2,4,8,128]{4,3,2,1,0:T(8,128)S(1)}, f32[1,2,4,8,128]{4,3,2,1,0:T(8,128)S(1)}, u32[]{:S(2)}, u32[]{:S(2)}) collective-permute-start(f32[1,2,4,8,128]{4,3,2,1,0:T(8,128)S(1)} %maximum_bitcast_fusion), channel_id=1, source_target_pairs={{0,48},{16,0},{32,16},{48,32},{1,49},{17,1},{33,17},{49,33},{2,50}... | collective-permute-start | bytes 98312 | tf_op jit(solution)/shard_map/ppermute | solution.py:304
  14.8 8.4 %collective-permute-start.7 = (f32[4,2,4,8,128]{4,3,2,1,0:T(8,128)S(1)}, f32[4,2,4,8,128]{4,3,2,1,0:T(8,128)S(1)}, u32[]{:S(2)}, u32[]{:S(2)}) collective-permute-start(f32[4,2,4,8,128]{4,3,2,1,0:T(8,128)S(1)} %pad_maximum_fusion.a0), channel_id=1, source_target_pairs={{0,128},{64,192},{128,0},{192,64},{1,129},{65,193},{129,1},{193,65... | collective-permute-start | bytes 393224 | tf_op jit(solution)/shard_map/ppermute | solution.py:304
  17.9 6.5 %collective-permute-start.6 = (f32[4,2,4,8,128]{4,3,2,1,0:T(8,128)S(1)}, f32[4,2,4,8,128]{4,3,2,1,0:T(8,128)S(1)}, u32[]{:S(2)}, u32[]{:S(2)}) collective-permute-start(f32[4,2,4,8,128]{4,3,2,1,0:T(8,128)S(1)} %pad_maximum_fusion.a0), channel_id=1, source_target_pairs={{0,64},{64,128},{128,192},{192,0},{1,65},{65,129},{129,193},{193,1... | collective-permute-start | bytes 393224 | tf_op jit(solution)/shard_map/ppermute | solution.py:304
  18.5 5.9 %collective-permute-start.5 = (f32[4,2,4,8,128]{4,3,2,1,0:T(8,128)S(1)}, f32[4,2,4,8,128]{4,3,2,1,0:T(8,128)S(1)}, u32[]{:S(2)}, u32[]{:S(2)}) collective-permute-start(f32[4,2,4,8,128]{4,3,2,1,0:T(8,128)S(1)} %pad_maximum_fusion.a0), channel_id=1, source_target_pairs={{0,192},{64,0},{128,64},{192,128},{1,193},{65,1},{129,65},{193,129... | collective-permute-start | bytes 393224 | tf_op jit(solution)/shard_map/ppermute | solution.py:304
  21.2 17.4 %collective-permute-start.3 = (f32[15,64,128]{2,1,0:T(8,128)S(1)}, f32[15,64,128]{2,1,0:T(8,128)S(1)}, u32[]{:S(2)}, u32[]{:S(2)}) collective-permute-start(f32[15,64,128]{2,1,0:T(8,128)S(1)} %get-tuple-element.37.mine), channel_id=1, source_target_pairs={{0,1},{1,2},{2,3},{3,4},{4,5},{5,6},{6,7},{7,0},{8,9},{9,10},{10,1... | collective-permute-start | bytes 1474568 | tf_op jit(solution)/shard_map/ppermute | solution.py:300
  21.9 11.7 %collective-permute-start.4 = (f32[13,64,128]{2,1,0:T(8,128)S(1)}, f32[13,64,128]{2,1,0:T(8,128)S(1)}, u32[]{:S(2)}, u32[]{:S(2)}) collective-permute-start(f32[13,64,128]{2,1,0:T(8,128)S(1)} %get-tuple-element.38), channel_id=1, source_target_pairs={{0,7},{1,0},{2,1},{3,2},{4,3},{5,4},{6,5},{7,6},{8,15},{9,8},{10,9... | collective-permute-start | bytes 1277960 | tf_op jit(solution)/shard_map/ppermute | solution.py:300
  25.3 1.4 %collective-permute-start.8 = (f32[8,4,8,128]{3,2,1,0:T(8,128)S(1)}, f32[8,4,8,128]{3,2,1,0:T(8,128)S(1)}, u32[]{:S(2)}, u32[]{:S(2)}) collective-permute-start(f32[8,4,8,128]{3,2,1,0:T(8,128)S(1)} %get-tuple-element.44), channel_id=1, source_target_pairs={{0,8},{8,0},{1,9},{9,1},{2,10},{10,2},{3,11},{11,3},{4,12},{12,4},... | collective-permute-start | bytes 393224 | tf_op jit(solution)/shard_map/ppermute | solution.py:296
  25.4 1.5 %collective-permute-start.9 = (f32[8,4,8,128]{3,2,1,0:T(8,128)S(1)}, f32[8,4,8,128]{3,2,1,0:T(8,128)S(1)}, u32[]{:S(2)}, u32[]{:S(2)}) collective-permute-start(f32[8,4,8,128]{3,2,1,0:T(8,128)S(1)} %get-tuple-element.45), channel_id=1, source_target_pairs={{0,8},{8,0},{1,9},{9,1},{2,10},{10,2},{3,11},{11,3},{4,12},{12,4},... | collective-permute-start | bytes 393224 | tf_op jit(solution)/shard_map/ppermute | solution.py:296
  27.9 10.6 %collective-permute-start.10 = (f32[7,64,128]{2,1,0:T(8,128)S(1)}, f32[7,64,128]{2,1,0:T(8,128)S(1)}, u32[]{:S(2)}, u32[]{:S(2)}) collective-permute-start(f32[7,64,128]{2,1,0:T(8,128)S(1)} %get-tuple-element.47), channel_id=1, source_target_pairs={{0,1},{1,2},{2,3},{3,4},{4,5},{5,6},{6,7},{7,0},{8,9},{9,10},{10,1... | collective-permute-start | bytes 688136 | tf_op jit(solution)/shard_map/ppermute | solution.py:300
  29.6 9.0 %collective-permute-start.11 = (f32[6,64,128]{2,1,0:T(8,128)S(1)}, f32[6,64,128]{2,1,0:T(8,128)S(1)}, u32[]{:S(2)}, u32[]{:S(2)}) collective-permute-start(f32[6,64,128]{2,1,0:T(8,128)S(1)} %get-tuple-element.48), channel_id=1, source_target_pairs={{0,7},{1,0},{2,1},{3,2},{4,3},{5,4},{6,5},{7,6},{8,15},{9,8},{10,9... | collective-permute-start | bytes 589832 | tf_op jit(solution)/shard_map/ppermute | solution.py:300
  43.4 1.6 %collective-permute-start.12 = (f32[16,32,128]{2,1,0:T(8,128)S(1)}, f32[16,32,128]{2,1,0:T(8,128)S(1)}, u32[]{:S(2)}, u32[]{:S(2)}) collective-permute-start(f32[16,32,128]{2,1,0:T(8,128)S(1)} %get-tuple-element.52), channel_id=1, source_target_pairs={{0,8},{8,0},{1,9},{9,1},{2,10},{10,2},{3,11},{11,3},{4,12},{12,4},... | collective-permute-start | bytes 786440 | tf_op jit(solution)/shard_map/ppermute | solution.py:296
  45.0 6.4 %collective-permute-start.13 = (f32[4,32,128]{2,1,0:T(8,128)S(1)}, f32[4,32,128]{2,1,0:T(8,128)S(1)}, u32[]{:S(2)}, u32[]{:S(2)}) collective-permute-start(f32[4,32,128]{2,1,0:T(8,128)S(1)} %get-tuple-element.54), channel_id=1, source_target_pairs={{0,128},{64,192},{128,0},{192,64},{1,129},{65,193},{129,1},{193,65... | collective-permute-start | bytes 196616 | tf_op jit(solution)/shard_map/ppermute | solution.py:304
  45.9 6.2 %collective-permute-start.14 = (f32[4,32,128]{2,1,0:T(8,128)S(1)}, f32[4,32,128]{2,1,0:T(8,128)S(1)}, u32[]{:S(2)}, u32[]{:S(2)}) collective-permute-start(f32[4,32,128]{2,1,0:T(8,128)S(1)} %get-tuple-element.55), channel_id=1, source_target_pairs={{0,64},{64,128},{128,192},{192,0},{1,65},{65,129},{129,193},{193,1... | collective-permute-start | bytes 196616 | tf_op jit(solution)/shard_map/ppermute | solution.py:304
  48.0 4.3 %collective-permute-start.15 = (f32[4,32,128]{2,1,0:T(8,128)S(1)}, f32[4,32,128]{2,1,0:T(8,128)S(1)}, u32[]{:S(2)}, u32[]{:S(2)}) collective-permute-start(f32[4,32,128]{2,1,0:T(8,128)S(1)} %get-tuple-element.56), channel_id=1, source_target_pairs={{0,192},{64,0},{128,64},{192,128},{1,193},{65,1},{129,65},{193,129... | collective-permute-start | bytes 196616 | tf_op jit(solution)/shard_map/ppermute | solution.py:304
  52.3 7.7 %collective-permute-start.16 = (f32[32,128]{1,0:T(8,128)S(1)}, f32[32,128]{1,0:T(8,128)S(1)}, u32[]{:S(2)}, u32[]{:S(2)}) collective-permute-start(f32[32,128]{1,0:T(8,128)S(1)} %get-tuple-element.58), channel_id=1, source_target_pairs={{0,32},{16,48},{32,0},{48,16},{1,33},{17,49},{33,1},{49,17},{2,34}... | collective-permute-start | bytes 49160 | tf_op jit(solution)/shard_map/ppermute | solution.py:304
  54.3 5.9 %collective-permute-start.17 = (f32[32,128]{1,0:T(8,128)S(1)}, f32[32,128]{1,0:T(8,128)S(1)}, u32[]{:S(2)}, u32[]{:S(2)}) collective-permute-start(f32[32,128]{1,0:T(8,128)S(1)} %get-tuple-element.59), channel_id=1, source_target_pairs={{0,16},{16,32},{32,48},{48,0},{1,17},{17,33},{33,49},{49,1},{2,18}... | collective-permute-start | bytes 49160 | tf_op jit(solution)/shard_map/ppermute | solution.py:304
  58.1 4.6 %collective-permute-start.18 = (f32[32,128]{1,0:T(8,128)S(1)}, f32[32,128]{1,0:T(8,128)S(1)}, u32[]{:S(2)}, u32[]{:S(2)}) collective-permute-start(f32[32,128]{1,0:T(8,128)S(1)} %get-tuple-element.60), channel_id=1, source_target_pairs={{0,48},{16,0},{32,16},{48,32},{1,49},{17,1},{33,17},{49,33},{2,50}... | collective-permute-start | bytes 49160 | tf_op jit(solution)/shard_map/ppermute | solution.py:304

commit v4 on v3

--- a/solution.py
+++ b/solution.py
@@ -7,7 +7,8 @@
 from jax.sharding import PartitionSpec as P
 
 STEPS = 4
-UNROLL = 2
+INLINE = 1
+COST = None
 GATHER, SCATTER = (3, 1, 2), (2, 1, 3)
 F32 = jnp.float32
 ROWS = 64
@@ -39,7 +40,9 @@
     return (b + ((c + b) & 1)) >> 1
 
 
-def pack_kernel(src_in, rcv_in, own, to_prev, to_next, src, rcv, sem):
+def pack_kernel(src_in, rcv_in, anchors_in, own, to_prev, to_next, anchors, src, rcv, sem, anchors_sem):
+    held = pltpu.make_async_copy(anchors_in, anchors, anchors_sem)
+    held.start()
     half = ROWS // 2
     copies = []
     for h in range(2):
@@ -69,6 +72,8 @@
             copy.wait()
         before = lax.fori_loop(h * half, h * half + half, row, before, unroll=8)
 
+    held.wait()
+
     def plane(f, y):
         return own[f, y * ROWS : (y + 1) * ROWS, :]
 
@@ -140,47 +145,19 @@
         to_next[i] = plane(f, y)
 
 
-def march_kernel(
-    anchors, own, prev, nxt, mine, model, model_prev, model_next, add_s, add_r,
-    keep, send,
-    ps, pr, ds, dr, mod, buoy, corr,
-):
+def inner_tile():
     tile = lax.axis_index("tile")
-    inner_low, inner_high = tile > 0, tile < NT - 1
-
-    def below(value):
-        return jnp.where(inner_low, value, 0.0)
-
-    def above(value):
-        return jnp.where(inner_high, value, 0.0)
-
-    ps[0, 0:4] = below(prev[0:4])
-    ps[0, 4:12] = own[0]
-    ps[0, 12:16] = above(nxt[0:4])
-    pr[0, 1:4] = below(prev[8:11])
-    pr[0, 4:12] = own[2]
-    pr[0, 12:15] = above(nxt[7:10])
-    for d, f, at, vy, after in ((ds, 0, 4, 7, 4), (dr, 1, 11, 14, 10)):
-        d[1:4] = below(prev[at : at + 3])
-        d[4] = own[2 * f + 1, 0] - below(prev[vy])
-        d[5:12] = own[2 * f + 1, 1:8]
-        d[12] = above(nxt[after] - mine[vy])
-        d[13:15] = above(nxt[after + 1 : after + 3])
-    mod[1:4] = below(model_prev[0:3])
-    mod[4:12] = model[0]
-    mod[12:15] = above(model_next[0:3])
-    buoy[0:4] = below(model_prev[3:7])
-    buoy[4:12] = model[1]
-    buoy[12:15] = above(model_next[3:6])
-
-    keep[...] = jnp.zeros(keep.shape, F32)
-    send[...] = jnp.zeros(send.shape, F32)
-
+    low, high = tile > 0, tile < NT - 1
+    return (lambda value: jnp.where(low, value, 0.0)), (lambda value: jnp.where(high, value, 0.0))
+
+
+def stepper(ps, pr, ds, dr, mod, buoy, add_s, add_r):
     lane = lax.broadcasted_iota(jnp.int32, (8, DEPTH), 1)
     row = lax.broadcasted_iota(jnp.int32, (8, DEPTH), 0)
     first_lane, last_lane, first_row, last_row = lane == 0, lane == DEPTH - 1, row == 0, row == 7
     blocks = range(ROWS // 8)
     zero = jnp.zeros((8, DEPTH), F32)
+    fields = ((ps, ds, add_s, lambda s: s), (pr, dr, add_r, lambda s: STEPS - s))
 
     def get(ref, *at):
         return [ref[(*at, slice(8 * v, 8 * v + 8))] for v in blocks]
@@ -199,50 +176,103 @@
             out.append(spread)
         return out, flux_y
 
-    def plane(s, y, carry):
+    def plane(s, y, wanted, carry):
         m, b = get(mod, y), get(buoy, y)
-        fields = ((ps, ds, add_s, s), (pr, dr, add_r, STEPS - s)) if s else ((ps, ds, add_s, 0),)
-        new, ends = [], []
-        for (p_all, d_all, add, amp), (p, before) in zip(fields, carry):
+        ends = []
+        for f, (p, before) in zip(wanted, carry):
+            p_all, d_all, add, amp = fields[f]
             after = get(p_all, s, y + 1)
             spread, flux = spread_of(p, after, before, b)
             ends.append((after, flux))
-            out = []
             for v in blocks:
                 cut = slice(8 * v, 8 * v + 8)
                 d = d_all[y, cut] - spread[v]
-                out.append(p[v] + add[amp, y, cut] - m[v] * d)
+                p_all[s + 1, y, cut] = p[v] + add[amp(s), y, cut] - m[v] * d
                 if s < STEPS - 1:
                     d_all[y, cut] = d
-                    p_all[s + 1, y, cut] = out[v]
-            new.append(out)
-        if s == 0:
+        return ends
+
+    def run(s, groups, count, inline=0):
+        carry = []
+        for y, wanted in groups:
+            b, part = get(buoy, y - 1), []
+            for f in wanted:
+                here, before = get(fields[f][0], s, y), get(fields[f][0], s, y - 1)
+                part.append((here, [b[v] * (here[v] - before[v]) for v in blocks]))
+            carry.append(part)
+
+        def planes(i, carry):
+            return [plane(s, y + i, wanted, part) for (y, wanted), part in zip(groups, carry)]
+
+        if inline:
+            for i in range(count):
+                carry = planes(i, carry)
+        else:
+            lax.fori_loop(0, count, planes, carry)
+
+    def first(low, high):
+        for y in range(low, high):
             for v in blocks:
                 cut = slice(8 * v, 8 * v + 8)
-                pr[1, y, cut] = pr[0, y, cut] - m[v] * dr[y, cut]
-        if s == STEPS - 1:
-            for v in blocks:
-                cut = slice(8 * v, 8 * v + 8)
-                image = new[0][v] * (pr[1, y, cut] + add_r[3, y, cut])
-                image += ps[3, y, cut] * (pr[2, y, cut] + add_r[2, y, cut])
-                image += ps[2, y, cut] * (pr[3, y, cut] + add_r[1, y, cut])
-                image += ps[1, y, cut] * (new[1][v] + add_r[0, y, cut])
-                corr[pl.ds(8 * COLS * v + y - STEPS, 8, stride=COLS), :] = image / STEPS
-        return ends
-
+                pr[1, y, cut] = pr[0, y, cut] - mod[y, cut] * dr[y, cut]
+
+    return run, first
+
+
+def inner_kernel(own, prev, nxt, mine, model, add_s, add_r, ps, pr, ds, dr, mod, buoy):
+    below, above = inner_tile()
+    mod[4:12] = model[0]
+    buoy[4:12] = model[1]
+    ps[0, 0:4] = below(prev[0:4])
+    ps[0, 4:12] = own[0]
+    ps[0, 12:16] = above(nxt[0:4])
+    pr[0, 1:4] = below(prev[8:11])
+    pr[0, 4:12] = own[2]
+    pr[0, 12:15] = above(nxt[7:10])
+    for d, f, at, vy, after in ((ds, 0, 4, 7, 4), (dr, 1, 11, 14, 10)):
+        d[1:4] = below(prev[at : at + 3])
+        d[4] = own[2 * f + 1, 0] - below(prev[vy])
+        d[5:12] = own[2 * f + 1, 1:8]
+        d[12] = above(nxt[after] - mine[vy])
+        d[13:15] = above(nxt[after + 1 : after + 3])
+    run, first = stepper(ps, pr, ds, dr, mod, buoy, add_s, add_r)
+    first(4, 12)
+    run(0, [(5, (0,)), (8, (0,))], 3)
+    run(0, [(11, (0,))], 1, 1)
+    run(1, [(6, (0, 1)), (8, (0, 1))], 2)
+    run(1, [(5, (1,)), (10, (0, 1))], 1, 1)
+    run(2, [(7, (0, 1)), (8, (0, 1))], 1, 1)
+    run(2, [(6, (1,)), (9, (0, 1))], 1, 1)
+    run(3, [(7, (1,)), (8, (0, 1))], 1, 1)
+
+
+def outer_kernel(
+    anchors, model_prev, model_next, add_s, add_r, ps_in, pr_in, ds_in, dr_in, mod_in, buoy_in,
+    keep, send, ps, pr, ds, dr, mod, buoy, corr,
+):
+    del ps_in, pr_in, ds_in, dr_in, mod_in, buoy_in
+    below, above = inner_tile()
+    mod[1:4] = below(model_prev[0:3])
+    mod[12:15] = above(model_next[0:3])
+    buoy[0:4] = below(model_prev[3:7])
+    buoy[12:15] = above(model_next[3:6])
+    keep[...] = jnp.zeros(keep.shape, F32)
+    send[...] = jnp.zeros(send.shape, F32)
+    run, first = stepper(ps, pr, ds, dr, mod, buoy, add_s, add_r)
+    first(1, 4)
+    first(12, 15)
     for s in range(STEPS):
-        low, high = s + 1, 15 - s
-        carry = []
-        for p_all in (ps, pr) if s else (ps,):
-            here, before, b = get(p_all, s, low), get(p_all, s, low - 1), get(buoy, low - 1)
-            carry.append((here, [b[v] * (here[v] - before[v]) for v in blocks]))
-
-        def planes(i, carry, s=s, low=low):
-            for u in range(UNROLL):
-                carry = plane(s, low + UNROLL * i + u, carry)
-            return carry
-
-        lax.fori_loop(0, (high - low) // UNROLL, planes, carry)
+        both = (0, 1) if s else (0,)
+        run(s, [(s + 1, both), (12 - s, both), (s + 4, (0,))], 1, 1)
+        run(s, [(s + 2, both), (13 - s, both)], 2, INLINE)
+
+    def image(y, _):
+        value = ps[4, y] * (pr[1, y] + add_r[3, y]) + ps[3, y] * (pr[2, y] + add_r[2, y])
+        value += ps[2, y] * (pr[3, y] + add_r[1, y]) + ps[1, y] * (pr[4, y] + add_r[0, y])
+        corr[pl.ds(y - STEPS, ROWS, stride=COLS), :] = value / STEPS
+        return 0
+
+    lax.fori_loop(STEPS, STEPS + COLS, image, 0, unroll=2)
 
     c, g = place()
     odd = (c + anchors[g]) & 1
@@ -252,25 +282,32 @@
             out[at + i] = corr[pl.ds(pl.multiple_of(32 * (start + 2 * i), 32), 32), :]
 
 
-def march(*operands):
-    plane = (ROWS, DEPTH)
+STATE = [shape(STEPS + 1, PLANES, ROWS, DEPTH)] * 2 + [shape(PLANES, ROWS, DEPTH)] * 4
+
+
+def inner(*operands):
     return pl.pallas_call(
-        march_kernel,
-        out_shape=[shape(16, 32, DEPTH)] * 2,
-        in_specs=[SMEM] + [VMEM] * 9,
-        out_specs=[VMEM] * 2,
-        scratch_shapes=[
-            pltpu.VMEM((STEPS, PLANES, *plane), F32),
-            pltpu.VMEM((STEPS, PLANES, *plane), F32),
-            pltpu.VMEM((PLANES, *plane), F32),
-            pltpu.VMEM((PLANES, *plane), F32),
-            pltpu.VMEM((PLANES, *plane), F32),
-            pltpu.VMEM((PLANES, *plane), F32),
-            pltpu.VMEM((COLS * ROWS, DEPTH), F32),
-        ],
-        compiler_params=params(10),
-        name="march",
+        inner_kernel,
+        out_shape=STATE,
+        in_specs=[VMEM] * 7,
+        out_specs=[VMEM] * 6,
+        compiler_params=params(4),
+        cost_estimate=COST,
+        name="inner",
     )(*operands)
+
+
+def outer(*operands):
+    return pl.pallas_call(
+        outer_kernel,
+        out_shape=[shape(16, 32, DEPTH)] * 2 + STATE,
+        in_specs=[SMEM] + [VMEM] * 10,
+        out_specs=[VMEM] * 8,
+        scratch_shapes=[pltpu.VMEM((COLS * ROWS, DEPTH), F32)],
+        input_output_aliases={5 + i: 2 + i for i in range(6)},
+        compiler_params=params(4),
+        name="outer",
+    )(*operands)[:2]
 
 
 def halve_kernel(keep, got, s0, s1, s2, s3):
@@ -309,19 +346,25 @@
     strip = jnp.stack([velocity, density])[None]
     zs = along([strip] * 3, "zh", GATHER)
 
-    own, to_prev, to_next = pl.pallas_call(
+    own, to_prev, to_next, anchors = pl.pallas_call(
         pack_kernel,
-        out_shape=[shape(4, COLS * ROWS, DEPTH), shape(13, *plane), shape(15, *plane)],
-        in_specs=[HBM, HBM],
-        out_specs=[VMEM] * 3,
+        out_shape=[
+            shape(4, COLS * ROWS, DEPTH),
+            shape(13, *plane),
+            shape(15, *plane),
+            jax.ShapeDtypeStruct(anchors.shape, anchors.dtype),
+        ],
+        in_specs=[HBM] * 3,
+        out_specs=[VMEM] * 4,
         scratch_shapes=[
             pltpu.VMEM((4, ROWS, COLS, DEPTH), F32),
             pltpu.VMEM((4, ROWS, COLS, DEPTH), F32),
             pltpu.SemaphoreType.DMA((2, 2)),
+            pltpu.SemaphoreType.DMA,
         ],
         compiler_params=params(8),
         name="pack",
-    )(*(pltpu.with_memory_space_constraint(state, pltpu.HBM) for state in (src_state, rcv_state)))
+    )(*(pltpu.with_memory_space_constraint(a, pltpu.HBM) for a in (src_state, rcv_state, anchors)))
     *zs, own, to_prev, to_next = lax.optimization_barrier((*zs, own, to_prev, to_next))
 
     xs = [jnp.concatenate([strip, *zs])]
@@ -360,18 +403,16 @@
     model_next = to_tile(mb_prev, -1)
     model_prev = to_tile(mb_next, 1)
 
-    keep, send = march(
-        anchors,
+    state = inner(
         own.reshape(4, COLS, *plane),
         halo_prev,
         halo_next,
         to_next,
         mb.reshape(2, COLS, *plane),
-        model_prev,
-        model_next,
         inj_src,
         inj_rec,
     )
+    keep, send = outer(anchors, model_prev, model_next, inj_src, inj_rec, *state)
 
     parts = pl.pallas_call(
         halve_kernel,

time: 63.5 us -> 60.9 us (0.959)
  waiting for transfers between devices: 17.7 us -> 15.7 us
  Pallas kernels: 11.9 us -> 11.1 us
    ppermute x4, waiting for transfers between devices: 6.52 us -> 4.73 us  [to_tile(): lax.ppermute(block, 'tile', [(i, (i + distance) % NT) for i in range(NT)])]
    pallas_call x1 -> x2, Pallas kernels: 4.8 us -> 3.98 us  [the longest x1 2.2 us: outer(): pl.pallas_call(outer_kernel, out_shape=[shape(16, 32, DEPTH)] * 2 + STATE...]
  transfers between devices with their start and end apart: 19 -> 19, of which waited for: 12 -> 13; matrix products, arithmetic and copies ran while one was open for 0% -> 0% of each run, Pallas kernels for 10% -> 14%
where the time goes in v4:
time: 60.9 us; the launch traced here: 60.7 us
  starting transfers between devices  33 us (54%)
  waiting for transfers between devices  15.7 us (26%)
  Pallas kernels  11.1 us (18%)
  other arithmetic  0.79 us (1%)
    ppermute x12, starting transfers between devices, along(): lax.ppermute(blocks[d - 1], axis, [(i, (i + d) % 4) for i in range(4)])  28.2 us
    ppermute x12, waiting for transfers between devices, along(): lax.ppermute(blocks[d - 1], axis, [(i, (i + d) % 4) for i in range(4)])  8.4 us
    ppermute x4, waiting for transfers between devices, to_tile(): lax.ppermute(block, 'tile', [(i, (i + distance) % NT) for i in range(NT)])  4.73 us
    ppermute x4, starting transfers between devices, to_tile(): lax.ppermute(block, 'tile', [(i, (i + distance) % NT) for i in range(NT)])  4.13 us
    pallas_call x1, Pallas kernels, local(): pl.pallas_call(pack_kernel, out_shape=[shape(4, COLS * ROWS, DEPTH), shap...  2.64 us
    ppermute x3, waiting for transfers between devices, other_core(): return lax.ppermute(block, 'core', [(0, 1), (1, 0)])  2.55 us
    pallas_call x1, Pallas kernels, outer(): pl.pallas_call(outer_kernel, out_shape=[shape(16, 32, DEPTH)] * 2 + STATE...  2.2 us
    pallas_call x1, Pallas kernels, local(): pl.pallas_call(inject_kernel, out_shape=[shape(STEPS, PLANES, *plane)] *...  1.97 us
  transfers between devices with their start and end apart: 19, of which 13 were waited for; matrix products, arithmetic and copies ran while one was open for 0% of the time, Pallas kernels for 14%

profile of v4, /device:TPU:24, one launch (start us, length us, event | category | flops | bytes accessed | tf_op | source)
XLA Modules:
  0.0 60.7 jit_solution(12610367507562561508)
XLA Ops:
  0.0 0.0 copy-start.1
  0.0 0.0 copy-start.3
  0.0 0.0 copy-start
  0.0 0.0 copy-start.2
  0.0 0.8 %maximum_bitcast_fusion = f32[1,2,4,8,128]{4,3,2,1,0:T(8,128)S(1)} fusion(f32[1,4,8,128]{3,2,1,0:T(8,128)} %bitcast.17, f32[1,4,8,128]{3,2,1,0:T(8,128)} %bitcast.18), kind=kLoop, calls=%fused_computation.1 | loop fusion | flops 8192 | bytes 65536 | tf_op jit(solution)/shard_map/broadcast_in_dim | solution.py:346
  0.8 7.2 %collective-permute-start.2 = (f32[1,2,4,8,128]{4,3,2,1,0:T(8,128)S(1)}, f32[1,2,4,8,128]{4,3,2,1,0:T(8,128)S(1)}, u32[]{:S(2)}, u32[]{:S(2)}) collective-permute-start(f32[1,2,4,8,128]{4,3,2,1,0:T(8,128)S(1)} %maximum_bitcast_fusion), channel_id=1, source_target_pairs={{0,32},{16,48},{32,0},{48,16},{1,33},{17,49},{33,1},{49,17},{2,34}... | collective-permute-start | bytes 98312 | tf_op jit(solution)/shard_map/ppermute | solution.py:341
  8.0 1.5 %collective-permute-start.1 = (f32[1,2,4,8,128]{4,3,2,1,0:T(8,128)S(1)}, f32[1,2,4,8,128]{4,3,2,1,0:T(8,128)S(1)}, u32[]{:S(2)}, u32[]{:S(2)}) collective-permute-start(f32[1,2,4,8,128]{4,3,2,1,0:T(8,128)S(1)} %maximum_bitcast_fusion), channel_id=1, source_target_pairs={{0,16},{16,32},{32,48},{48,0},{1,17},{17,33},{33,49},{49,1},{2,18}... | collective-permute-start | bytes 98312 | tf_op jit(solution)/shard_map/ppermute | solution.py:341
  9.5 2.7 %collective-permute-start = (f32[1,2,4,8,128]{4,3,2,1,0:T(8,128)S(1)}, f32[1,2,4,8,128]{4,3,2,1,0:T(8,128)S(1)}, u32[]{:S(2)}, u32[]{:S(2)}) collective-permute-start(f32[1,2,4,8,128]{4,3,2,1,0:T(8,128)S(1)} %maximum_bitcast_fusion), channel_id=1, source_target_pairs={{0,48},{16,0},{32,16},{48,32},{1,49},{17,1},{33,17},{49,33},{2,50}... | collective-permute-start | bytes 98312 | tf_op jit(solution)/shard_map/ppermute | solution.py:341
  12.1 2.6 %pack.1 = (f32[4,512,128]{2,1,0:T(8,128)S(1)}, f32[13,64,128]{2,1,0:T(8,128)S(1)}, f32[15,64,128]{2,1,0:T(8,128)S(1)}, s32[32]{0:T(128)S(1)}) custom-call(f32[4,64,8,128]{3,2,1,0:T(8,128)} %src_in.1, f32[4,64,8,128]{3,2,1,0:T(8,128)} %rcv_in.1, s32[32]{0:T(128)} %anchors_in.1), custom_call_target="tpu_custom_call" | custom-call | tf_op jit(solution)/shard_map/pack/pallas_call | solution.py:349
  14.8 0.0 collective-permute-done.2
  14.8 0.0 collective-permute-done.1
  14.8 0.0 collective-permute-done
  14.8 3.1 %collective-permute-start.5 = (f32[4,2,4,8,128]{4,3,2,1,0:T(8,128)S(1)}, f32[4,2,4,8,128]{4,3,2,1,0:T(8,128)S(1)}, u32[]{:S(2)}, u32[]{:S(2)}) collective-permute-start(f32[4,2,4,8,128]{4,3,2,1,0:T(8,128)S(1)} %pad_maximum_fusion.a0), channel_id=1, source_target_pairs={{0,128},{64,192},{128,0},{192,64},{1,129},{65,193},{129,1},{193,65... | collective-permute-start | bytes 393224 | tf_op jit(solution)/shard_map/ppermute | solution.py:341
  17.9 0.6 collective-permute-start.4
  18.5 2.6 %collective-permute-start.3 = (f32[4,2,4,8,128]{4,3,2,1,0:T(8,128)S(1)}, f32[4,2,4,8,128]{4,3,2,1,0:T(8,128)S(1)}, u32[]{:S(2)}, u32[]{:S(2)}) collective-permute-start(f32[4,2,4,8,128]{4,3,2,1,0:T(8,128)S(1)} %pad_maximum_fusion.a0), channel_id=1, source_target_pairs={{0,192},{64,0},{128,64},{192,128},{1,193},{65,1},{129,65},{193,129... | collective-permute-start | bytes 393224 | tf_op jit(solution)/shard_map/ppermute | solution.py:341
  21.2 0.7 %collective-permute-start.10 = (f32[15,64,128]{2,1,0:T(8,128)S(1)}, f32[15,64,128]{2,1,0:T(8,128)S(1)}, u32[]{:S(2)}, u32[]{:S(2)}) collective-permute-start(f32[15,64,128]{2,1,0:T(8,128)S(1)} %get-tuple-element.56.mine), channel_id=1, source_target_pairs={{0,1},{1,2},{2,3},{3,4},{4,5},{5,6},{6,7},{7,0},{8,9},{9,10},{10,1... | collective-permute-start | bytes 1474568 | tf_op jit(solution)/shard_map/ppermute | solution.py:337
  21.8 1.3 %collective-permute-start.11 = (f32[13,64,128]{2,1,0:T(8,128)S(1)}, f32[13,64,128]{2,1,0:T(8,128)S(1)}, u32[]{:S(2)}, u32[]{:S(2)}) collective-permute-start(f32[13,64,128]{2,1,0:T(8,128)S(1)} %get-tuple-element.57), channel_id=1, source_target_pairs={{0,7},{1,0},{2,1},{3,2},{4,3},{5,4},{6,5},{7,6},{8,15},{9,8},{10,9... | collective-permute-start | bytes 1277960 | tf_op jit(solution)/shard_map/ppermute | solution.py:337
  23.2 0.0 collective-permute-done.5.a3
  23.2 1.2 %collective-permute-done.4.a2 = f32[4,2,4,8,128]{4,3,2,1,0:T(8,128)S(1)} collective-permute-done((f32[4,2,4,8,128]{4,3,2,1,0:T(8,128)S(1)}, f32[4,2,4,8,128]{4,3,2,1,0:T(8,128)S(1)}, u32[]{:S(2)}, u32[]{:S(2)}) %collective-permute-start.4) | collective-permute-done | bytes 131104 | tf_op jit(solution)/shard_map/ppermute | solution.py:341
  24.4 0.0 collective-permute-done.3.a1
  24.4 0.9 %window.1 = (f32[8,4,8,128]{3,2,1,0:T(8,128)S(1)}, f32[8,4,8,128]{3,2,1,0:T(8,128)S(1)}, f32[8,4,8,128]{3,2,1,0:T(8,128)S(1)}, f32[8,4,8,128]{3,2,1,0:T(8,128)S(1)}) custom-call(s32[32]{0:T(128)S(1)} %get-tuple-element.40.anchors, f32[4,2,4,8,128]{4,3,2,1,0:T(8,128)S(1)} %pad_maximum_fusion.a0, f32[4,2,4,8,128]{4,3,2,1,0:T(8,128)S(1)} %collective-permute-done.3.a1, ...), custom_call_target="tpu_custom_call" | custom-call | tf_op jit(solution)/shard_map/window/pallas_call | solution.py:385
  25.3 0.1 collective-permute-start.6
  25.4 0.5 collective-permute-start.7
  25.9 0.8 %collective-permute-done.6.other_m = f32[8,4,8,128]{3,2,1,0:T(8,128)S(1)} collective-permute-done((f32[8,4,8,128]{3,2,1,0:T(8,128)S(1)}, f32[8,4,8,128]{3,2,1,0:T(8,128)S(1)}, u32[]{:S(2)}, u32[]{:S(2)}) %collective-permute-start.6) | collective-permute-done | bytes 131104 | tf_op jit(solution)/shard_map/ppermute | solution.py:333
  26.7 0.2 collective-permute-done.7.other_b
  26.9 1.0 %model.1 = (f32[2,512,128]{2,1,0:T(8,128)S(1)}, f32[6,64,128]{2,1,0:T(8,128)S(1)}, f32[7,64,128]{2,1,0:T(8,128)S(1)}) custom-call(s32[32]{0:T(128)S(1)} %get-tuple-element.40.anchors, f32[8,4,8,128]{3,2,1,0:T(8,128)S(1)} %get-tuple-element.47.own_m, f32[8,4,8,128]{3,2,1,0:T(8,128)S(1)} %get-tuple-element.48.own_b, ...), custom_call_target="tpu_custom_call" | custom-call | tf_op jit(solution)/shard_map/model/pallas_call | solution.py:395
  27.9 1.6 %collective-permute-start.8 = (f32[7,64,128]{2,1,0:T(8,128)S(1)}, f32[7,64,128]{2,1,0:T(8,128)S(1)}, u32[]{:S(2)}, u32[]{:S(2)}) collective-permute-start(f32[7,64,128]{2,1,0:T(8,128)S(1)} %get-tuple-element.51), channel_id=1, source_target_pairs={{0,1},{1,2},{2,3},{3,4},{4,5},{5,6},{6,7},{7,0},{8,9},{9,10},{10,1... | collective-permute-start | bytes 688136 | tf_op jit(solution)/shard_map/ppermute | solution.py:337
  29.6 0.5 collective-permute-start.9
  30.0 0.0 copy-done.1
  30.0 0.0 copy-done.3
  30.0 0.0 copy-done
  30.0 0.0 copy-done.2
  30.0 2.0 %inject.1 = (f32[4,16,64,128]{3,2,1,0:T(8,128)S(1)}, f32[4,16,64,128]{3,2,1,0:T(8,128)S(1)}) custom-call(s32[1,16]{1,0:T(1,128)S(1)} %copy-done.2, f32[4,16]{1,0:T(4,128)S(1)} %bitcast.15, s32[1,128]{1,0:T(1,128)S(1)} %copy-done.3, f32[4,128]{1,0:T(4,128)S(1)} %bitcast.16), custom_call_target="tpu_custom_call" | custom-call | tf_op jit(solution)/shard_map/inject/pallas_call | solution.py:376
  32.0 1.5 %collective-permute-done.11.nxt = f32[13,64,128]{2,1,0:T(8,128)S(1)} collective-permute-done((f32[13,64,128]{2,1,0:T(8,128)S(1)}, f32[13,64,128]{2,1,0:T(8,128)S(1)}, u32[]{:S(2)}, u32[]{:S(2)}) %collective-permute-start.11) | collective-permute-done | bytes 426016 | tf_op jit(solution)/shard_map/ppermute | solution.py:337
  33.6 0.4 collective-permute-done.10.prev
  33.9 1.8 %inner.1 = (f32[5,16,64,128]{3,2,1,0:T(8,128)S(1)}, f32[5,16,64,128]{3,2,1,0:T(8,128)S(1)}, f32[16,64,128]{2,1,0:T(8,128)S(1)}, f32[16,64,128]{2,1,0:T(8,128)S(1...) custom-call(f32[4,8,64,128]{3,2,1,0:T(8,128)S(1)} %bitcast.13, ...), custom_call_target="tpu_custom_call" | custom-call | tf_op jit(solution)/shard_map/inner/pallas_call | solution.py:289
  35.7 2.8 %collective-permute-done.9.model_next = f32[6,64,128]{2,1,0:T(8,128)S(1)} collective-permute-done((f32[6,64,128]{2,1,0:T(8,128)S(1)}, f32[6,64,128]{2,1,0:T(8,128)S(1)}, u32[]{:S(2)}, u32[]{:S(2)}) %collective-permute-start.9) | collective-permute-done | bytes 196640 | tf_op jit(solution)/shard_map/ppermute | solution.py:337
  38.5 0.0 collective-permute-done.8.model_prev
  38.5 2.2 %outer.1 = (f32[16,32,128]{2,1,0:T(8,128)S(1)}, f32[16,32,128]{2,1,0:T(8,128)S(1)}, f32[5,16,64,128]{3,2,1,0:T(8,128)S(1)}, f32[5,16,64,128]{3,2,1,0:T(8,128)S(1...) custom-call(s32[32]{0:T(128)S(1)} %get-tuple-element.40.anchors, ...), custom_call_target="tpu_custom_call", output_to_operand_aliasing={{2}: (5, {}), {3}: (6, {}), {4}: (7, {}), {5}: (8, {}), {6}... | custom-call | tf_op jit(solution)/shard_map/outer/pallas_call | solution.py:301
  40.7 0.1 collective-permute-start.12
  40.8 1.5 %collective-permute-done.12.got = f32[16,32,128]{2,1,0:T(8,128)S(1)} collective-permute-done((f32[16,32,128]{2,1,0:T(8,128)S(1)}, f32[16,32,128]{2,1,0:T(8,128)S(1)}, u32[]{:S(2)}, u32[]{:S(2)}) %collective-permute-start.12) | collective-permute-done | bytes 262176 | tf_op jit(solution)/shard_map/ppermute | solution.py:333
  42.4 0.9 %collective-permute-start.13 = (f32[4,32,128]{2,1,0:T(8,128)S(1)}, f32[4,32,128]{2,1,0:T(8,128)S(1)}, u32[]{:S(2)}, u32[]{:S(2)}) collective-permute-start(f32[4,32,128]{2,1,0:T(8,128)S(1)} %get-tuple-element.68), channel_id=1, source_target_pairs={{0,128},{64,192},{128,0},{192,64},{1,129},{65,193},{129,1},{193,65... | collective-permute-start | bytes 196616 | tf_op jit(solution)/shard_map/ppermute | solution.py:341
  43.3 2.1 %collective-permute-start.14 = (f32[4,32,128]{2,1,0:T(8,128)S(1)}, f32[4,32,128]{2,1,0:T(8,128)S(1)}, u32[]{:S(2)}, u32[]{:S(2)}) collective-permute-start(f32[4,32,128]{2,1,0:T(8,128)S(1)} %get-tuple-element.69), channel_id=1, source_target_pairs={{0,64},{64,128},{128,192},{192,0},{1,65},{65,129},{129,193},{193,1... | collective-permute-start | bytes 196616 | tf_op jit(solution)/shard_map/ppermute | solution.py:341
  45.4 1.2 %collective-permute-start.15 = (f32[4,32,128]{2,1,0:T(8,128)S(1)}, f32[4,32,128]{2,1,0:T(8,128)S(1)}, u32[]{:S(2)}, u32[]{:S(2)}) collective-permute-start(f32[4,32,128]{2,1,0:T(8,128)S(1)} %get-tuple-element.70), channel_id=1, source_target_pairs={{0,192},{64,0},{128,64},{192,128},{1,193},{65,1},{129,65},{193,129... | collective-permute-start | bytes 196616 | tf_op jit(solution)/shard_map/ppermute | solution.py:341
  46.5 2.3 %collective-permute-done.13.r1 = f32[4,32,128]{2,1,0:T(8,128)S(1)} collective-permute-done((f32[4,32,128]{2,1,0:T(8,128)S(1)}, f32[4,32,128]{2,1,0:T(8,128)S(1)}, u32[]{:S(2)}, u32[]{:S(2)}) %collective-permute-start.13) | collective-permute-done | bytes 65568 | tf_op jit(solution)/shard_map/ppermute | solution.py:341
  48.8 0.7 %collective-permute-done.14.r2 = f32[4,32,128]{2,1,0:T(8,128)S(1)} collective-permute-done((f32[4,32,128]{2,1,0:T(8,128)S(1)}, f32[4,32,128]{2,1,0:T(8,128)S(1)}, u32[]{:S(2)}, u32[]{:S(2)}) %collective-permute-start.14) | collective-permute-done | bytes 65568 | tf_op jit(solution)/shard_map/ppermute | solution.py:341
  49.5 0.1 collective-permute-done.15.r3
  49.7 2.2 %collective-permute-start.16 = (f32[32,128]{1,0:T(8,128)S(1)}, f32[32,128]{1,0:T(8,128)S(1)}, u32[]{:S(2)}, u32[]{:S(2)}) collective-permute-start(f32[32,128]{1,0:T(8,128)S(1)} %get-tuple-element.72), channel_id=1, source_target_pairs={{0,32},{16,48},{32,0},{48,16},{1,33},{17,49},{33,1},{49,17},{2,34}... | collective-permute-start | bytes 49160 | tf_op jit(solution)/shard_map/ppermute | solution.py:341
  51.9 3.6 %collective-permute-start.17 = (f32[32,128]{1,0:T(8,128)S(1)}, f32[32,128]{1,0:T(8,128)S(1)}, u32[]{:S(2)}, u32[]{:S(2)}) collective-permute-start(f32[32,128]{1,0:T(8,128)S(1)} %get-tuple-element.73), channel_id=1, source_target_pairs={{0,16},{16,32},{32,48},{48,0},{1,17},{17,33},{33,49},{49,1},{2,18}... | collective-permute-start | bytes 49160 | tf_op jit(solution)/shard_map/ppermute | solution.py:341
  55.5 0.6 collective-permute-start.18
  56.0 1.4 %collective-permute-done.16.q1 = f32[32,128]{1,0:T(8,128)S(1)} collective-permute-done((f32[32,128]{1,0:T(8,128)S(1)}, f32[32,128]{1,0:T(8,128)S(1)}, u32[]{:S(2)}, u32[]{:S(2)}) %collective-permute-start.16) | collective-permute-done | bytes 16416 | tf_op jit(solution)/shard_map/ppermute | solution.py:341
  57.4 0.5 collective-permute-done.17.q2
  57.9 2.2 %collective-permute-done.18.q3 = f32[32,128]{1,0:T(8,128)S(1)} collective-permute-done((f32[32,128]{1,0:T(8,128)S(1)}, f32[32,128]{1,0:T(8,128)S(1)}, u32[]{:S(2)}, u32[]{:S(2)}) %collective-permute-start.18) | collective-permute-done | bytes 16416 | tf_op jit(solution)/shard_map/ppermute | solution.py:341
  60.1 0.6 %last.1 = f32[32,128]{1,0:T(8,128)} custom-call(f32[32,128]{1,0:T(8,128)S(1)} %get-tuple-element.71.u0, f32[32,128]{1,0:T(8,128)S(1)} %collective-permute-done.16.q1, f32[32,128]{1,0:T(8,128)S(1)} %collective-permute-done.17.q2, f32[32,128]{1,0:T(8,128)S(1)} %collective-permute-done.18.q3), custom_call_target="tpu_custom_call" | custom-call | tf_op jit(solution)/shard_map/last/pallas_call | solution.py:435
  (3 shorter events, 0.1 us)
Async XLA Ops:
  0.0 30.0 %copy-start.1 = (f32[1,128,4]{1,2,0:T(4,128)S(1)}, f32[1,128,4]{1,2,0:T(4,128)}, u32[]{:S(2)}) copy-start(f32[1,128,4]{1,2,0:T(4,128)} %param.17) | copy-start | bytes 6148
  0.0 30.0 %copy-start.3 = (s32[1,128]{1,0:T(1,128)S(1)}, s32[1,128]{1,0:T(1,128)}, u32[]{:S(2)}) copy-start(s32[1,128]{1,0:T(1,128)} %rec_pos.1) | copy-start | bytes 1540
  0.0 30.0 %copy-start = (f32[1,16,4]{1,2,0:T(4,128)S(1)}, f32[1,16,4]{1,2,0:T(4,128)}, u32[]{:S(2)}) copy-start(f32[1,16,4]{1,2,0:T(4,128)} %param.15) | copy-start | bytes 772
  0.0 30.0 %copy-start.2 = (s32[1,16]{1,0:T(1,128)S(1)}, s32[1,16]{1,0:T(1,128)}, u32[]{:S(2)}) copy-start(s32[1,16]{1,0:T(1,128)} %src_pos.1) | copy-start | bytes 196
  0.8 14.0 %collective-permute-start.2 = (f32[1,2,4,8,128]{4,3,2,1,0:T(8,128)S(1)}, f32[1,2,4,8,128]{4,3,2,1,0:T(8,128)S(1)}, u32[]{:S(2)}, u32[]{:S(2)}) collective-permute-start(f32[1,2,4,8,128]{4,3,2,1,0:T(8,128)S(1)} %maximum_bitcast_fusion), channel_id=1, source_target_pairs={{0,32},{16,48},{32,0},{48,16},{1,33},{17,49},{33,1},{49,17},{2,34}... | collective-permute-start | bytes 98312 | tf_op jit(solution)/shard_map/ppermute | solution.py:341
  8.0 6.8 %collective-permute-start.1 = (f32[1,2,4,8,128]{4,3,2,1,0:T(8,128)S(1)}, f32[1,2,4,8,128]{4,3,2,1,0:T(8,128)S(1)}, u32[]{:S(2)}, u32[]{:S(2)}) collective-permute-start(f32[1,2,4,8,128]{4,3,2,1,0:T(8,128)S(1)} %maximum_bitcast_fusion), channel_id=1, source_target_pairs={{0,16},{16,32},{32,48},{48,0},{1,17},{17,33},{33,49},{49,1},{2,18}... | collective-permute-start | bytes 98312 | tf_op jit(solution)/shard_map/ppermute | solution.py:341
  9.5 5.3 %collective-permute-start = (f32[1,2,4,8,128]{4,3,2,1,0:T(8,128)S(1)}, f32[1,2,4,8,128]{4,3,2,1,0:T(8,128)S(1)}, u32[]{:S(2)}, u32[]{:S(2)}) collective-permute-start(f32[1,2,4,8,128]{4,3,2,1,0:T(8,128)S(1)} %maximum_bitcast_fusion), channel_id=1, source_target_pairs={{0,48},{16,0},{32,16},{48,32},{1,49},{17,1},{33,17},{49,33},{2,50}... | collective-permute-start | bytes 98312 | tf_op jit(solution)/shard_map/ppermute | solution.py:341
  14.8 8.4 %collective-permute-start.5 = (f32[4,2,4,8,128]{4,3,2,1,0:T(8,128)S(1)}, f32[4,2,4,8,128]{4,3,2,1,0:T(8,128)S(1)}, u32[]{:S(2)}, u32[]{:S(2)}) collective-permute-start(f32[4,2,4,8,128]{4,3,2,1,0:T(8,128)S(1)} %pad_maximum_fusion.a0), channel_id=1, source_target_pairs={{0,128},{64,192},{128,0},{192,64},{1,129},{65,193},{129,1},{193,65... | collective-permute-start | bytes 393224 | tf_op jit(solution)/shard_map/ppermute | solution.py:341
  17.9 6.5 %collective-permute-start.4 = (f32[4,2,4,8,128]{4,3,2,1,0:T(8,128)S(1)}, f32[4,2,4,8,128]{4,3,2,1,0:T(8,128)S(1)}, u32[]{:S(2)}, u32[]{:S(2)}) collective-permute-start(f32[4,2,4,8,128]{4,3,2,1,0:T(8,128)S(1)} %pad_maximum_fusion.a0), channel_id=1, source_target_pairs={{0,64},{64,128},{128,192},{192,0},{1,65},{65,129},{129,193},{193,1... | collective-permute-start | bytes 393224 | tf_op jit(solution)/shard_map/ppermute | solution.py:341
  18.5 5.9 %collective-permute-start.3 = (f32[4,2,4,8,128]{4,3,2,1,0:T(8,128)S(1)}, f32[4,2,4,8,128]{4,3,2,1,0:T(8,128)S(1)}, u32[]{:S(2)}, u32[]{:S(2)}) collective-permute-start(f32[4,2,4,8,128]{4,3,2,1,0:T(8,128)S(1)} %pad_maximum_fusion.a0), channel_id=1, source_target_pairs={{0,192},{64,0},{128,64},{192,128},{1,193},{65,1},{129,65},{193,129... | collective-permute-start | bytes 393224 | tf_op jit(solution)/shard_map/ppermute | solution.py:341
  21.2 12.7 %collective-permute-start.10 = (f32[15,64,128]{2,1,0:T(8,128)S(1)}, f32[15,64,128]{2,1,0:T(8,128)S(1)}, u32[]{:S(2)}, u32[]{:S(2)}) collective-permute-start(f32[15,64,128]{2,1,0:T(8,128)S(1)} %get-tuple-element.56.mine), channel_id=1, source_target_pairs={{0,1},{1,2},{2,3},{3,4},{4,5},{5,6},{6,7},{7,0},{8,9},{9,10},{10,1... | collective-permute-start | bytes 1474568 | tf_op jit(solution)/shard_map/ppermute | solution.py:337
  21.8 11.7 %collective-permute-start.11 = (f32[13,64,128]{2,1,0:T(8,128)S(1)}, f32[13,64,128]{2,1,0:T(8,128)S(1)}, u32[]{:S(2)}, u32[]{:S(2)}) collective-permute-start(f32[13,64,128]{2,1,0:T(8,128)S(1)} %get-tuple-element.57), channel_id=1, source_target_pairs={{0,7},{1,0},{2,1},{3,2},{4,3},{5,4},{6,5},{7,6},{8,15},{9,8},{10,9... | collective-permute-start | bytes 1277960 | tf_op jit(solution)/shard_map/ppermute | solution.py:337
  25.3 1.4 %collective-permute-start.6 = (f32[8,4,8,128]{3,2,1,0:T(8,128)S(1)}, f32[8,4,8,128]{3,2,1,0:T(8,128)S(1)}, u32[]{:S(2)}, u32[]{:S(2)}) collective-permute-start(f32[8,4,8,128]{3,2,1,0:T(8,128)S(1)} %get-tuple-element.49), channel_id=1, source_target_pairs={{0,8},{8,0},{1,9},{9,1},{2,10},{10,2},{3,11},{11,3},{4,12},{12,4},... | collective-permute-start | bytes 393224 | tf_op jit(solution)/shard_map/ppermute | solution.py:333
  25.4 1.5 %collective-permute-start.7 = (f32[8,4,8,128]{3,2,1,0:T(8,128)S(1)}, f32[8,4,8,128]{3,2,1,0:T(8,128)S(1)}, u32[]{:S(2)}, u32[]{:S(2)}) collective-permute-start(f32[8,4,8,128]{3,2,1,0:T(8,128)S(1)} %get-tuple-element.50), channel_id=1, source_target_pairs={{0,8},{8,0},{1,9},{9,1},{2,10},{10,2},{3,11},{11,3},{4,12},{12,4},... | collective-permute-start | bytes 393224 | tf_op jit(solution)/shard_map/ppermute | solution.py:333
  27.9 10.6 %collective-permute-start.8 = (f32[7,64,128]{2,1,0:T(8,128)S(1)}, f32[7,64,128]{2,1,0:T(8,128)S(1)}, u32[]{:S(2)}, u32[]{:S(2)}) collective-permute-start(f32[7,64,128]{2,1,0:T(8,128)S(1)} %get-tuple-element.51), channel_id=1, source_target_pairs={{0,1},{1,2},{2,3},{3,4},{4,5},{5,6},{6,7},{7,0},{8,9},{9,10},{10,1... | collective-permute-start | bytes 688136 | tf_op jit(solution)/shard_map/ppermute | solution.py:337
  29.6 9.0 %collective-permute-start.9 = (f32[6,64,128]{2,1,0:T(8,128)S(1)}, f32[6,64,128]{2,1,0:T(8,128)S(1)}, u32[]{:S(2)}, u32[]{:S(2)}) collective-permute-start(f32[6,64,128]{2,1,0:T(8,128)S(1)} %get-tuple-element.52), channel_id=1, source_target_pairs={{0,7},{1,0},{2,1},{3,2},{4,3},{5,4},{6,5},{7,6},{8,15},{9,8},{10,9... | collective-permute-start | bytes 589832 | tf_op jit(solution)/shard_map/ppermute | solution.py:337
  40.7 1.6 %collective-permute-start.12 = (f32[16,32,128]{2,1,0:T(8,128)S(1)}, f32[16,32,128]{2,1,0:T(8,128)S(1)}, u32[]{:S(2)}, u32[]{:S(2)}) collective-permute-start(f32[16,32,128]{2,1,0:T(8,128)S(1)} %get-tuple-element.66), channel_id=1, source_target_pairs={{0,8},{8,0},{1,9},{9,1},{2,10},{10,2},{3,11},{11,3},{4,12},{12,4},... | collective-permute-start | bytes 786440 | tf_op jit(solution)/shard_map/ppermute | solution.py:333
  42.4 6.4 %collective-permute-start.13 = (f32[4,32,128]{2,1,0:T(8,128)S(1)}, f32[4,32,128]{2,1,0:T(8,128)S(1)}, u32[]{:S(2)}, u32[]{:S(2)}) collective-permute-start(f32[4,32,128]{2,1,0:T(8,128)S(1)} %get-tuple-element.68), channel_id=1, source_target_pairs={{0,128},{64,192},{128,0},{192,64},{1,129},{65,193},{129,1},{193,65... | collective-permute-start | bytes 196616 | tf_op jit(solution)/shard_map/ppermute | solution.py:341
  43.3 6.2 %collective-permute-start.14 = (f32[4,32,128]{2,1,0:T(8,128)S(1)}, f32[4,32,128]{2,1,0:T(8,128)S(1)}, u32[]{:S(2)}, u32[]{:S(2)}) collective-permute-start(f32[4,32,128]{2,1,0:T(8,128)S(1)} %get-tuple-element.69), channel_id=1, source_target_pairs={{0,64},{64,128},{128,192},{192,0},{1,65},{65,129},{129,193},{193,1... | collective-permute-start | bytes 196616 | tf_op jit(solution)/shard_map/ppermute | solution.py:341
  45.4 4.3 %collective-permute-start.15 = (f32[4,32,128]{2,1,0:T(8,128)S(1)}, f32[4,32,128]{2,1,0:T(8,128)S(1)}, u32[]{:S(2)}, u32[]{:S(2)}) collective-permute-start(f32[4,32,128]{2,1,0:T(8,128)S(1)} %get-tuple-element.70), channel_id=1, source_target_pairs={{0,192},{64,0},{128,64},{192,128},{1,193},{65,1},{129,65},{193,129... | collective-permute-start | bytes 196616 | tf_op jit(solution)/shard_map/ppermute | solution.py:341
  49.7 7.8 %collective-permute-start.16 = (f32[32,128]{1,0:T(8,128)S(1)}, f32[32,128]{1,0:T(8,128)S(1)}, u32[]{:S(2)}, u32[]{:S(2)}) collective-permute-start(f32[32,128]{1,0:T(8,128)S(1)} %get-tuple-element.72), channel_id=1, source_target_pairs={{0,32},{16,48},{32,0},{48,16},{1,33},{17,49},{33,1},{49,17},{2,34}... | collective-permute-start | bytes 49160 | tf_op jit(solution)/shard_map/ppermute | solution.py:341
  51.9 6.0 %collective-permute-start.17 = (f32[32,128]{1,0:T(8,128)S(1)}, f32[32,128]{1,0:T(8,128)S(1)}, u32[]{:S(2)}, u32[]{:S(2)}) collective-permute-start(f32[32,128]{1,0:T(8,128)S(1)} %get-tuple-element.73), channel_id=1, source_target_pairs={{0,16},{16,32},{32,48},{48,0},{1,17},{17,33},{33,49},{49,1},{2,18}... | collective-permute-start | bytes 49160 | tf_op jit(solution)/shard_map/ppermute | solution.py:341
  55.5 4.6 %collective-permute-start.18 = (f32[32,128]{1,0:T(8,128)S(1)}, f32[32,128]{1,0:T(8,128)S(1)}, u32[]{:S(2)}, u32[]{:S(2)}) collective-permute-start(f32[32,128]{1,0:T(8,128)S(1)} %get-tuple-element.74), channel_id=1, source_target_pairs={{0,48},{16,0},{32,16},{48,32},{1,49},{17,1},{33,17},{49,33},{2,50}... | collective-permute-start | bytes 49160 | tf_op jit(solution)/shard_map/ppermute | solution.py:341

commit v5 on v4

--- a/solution.py
+++ b/solution.py
@@ -1,3 +1,5 @@
+import functools
+
 import jax
 import jax.numpy as jnp
 from jax import lax
@@ -34,6 +36,11 @@
 def place():
     c = lax.axis_index("core")
     return c, (lax.axis_index("x") * NZH + lax.axis_index("zh")) * NC + c
+
+
+def anchor(anchors, g):
+    lane = lax.broadcasted_iota(jnp.int32, anchors.shape, 1)
+    return jnp.sum(jnp.where(lane == g, anchors[...], 0))
 
 
 def first_strip(b, c):
@@ -110,39 +117,42 @@
         lax.fori_loop(0, pos.shape[1], point, 0, unroll=8)
 
 
-def window_kernel(anchors, a0, a1, a2, a3, own_m, own_b, other_m, other_b):
+def window_kernel(offset, anchors, a0, a1, a2, a3, modulus, buoyancy):
     x, z = lax.axis_index("x"), lax.axis_index("zh")
     c, g = place()
-    for group, out in ((g, (own_m, own_b)), (g + 1 - 2 * c, (other_m, other_b))):
-        first = first_strip(anchors[group], c)
-        for dx, strips in zip((0, *GATHER), (a0, a1, a2, a3)):
-            for dz, at in zip((0, *GATHER), range(NZH)):
-                i = ((x - dx) & (NX - 1)) * NZH + ((z - dz) & (NZH - 1)) - first
-
-                @pl.when((i >= 0) & (i < 8))
-                def _(i=i, strips=strips, at=at, out=out):
-                    vel, den = strips[at, 0], strips[at, 1]
-                    out[0][i] = den * vel * vel
-                    out[1][i] = 1.0 / den
-
-
-def model_kernel(anchors, own_m, own_b, other_m, other_b, out, to_prev, to_next):
+    first = first_strip(anchor(anchors, g + offset * (1 - 2 * c)), c)
+    for dx, strips in zip((0, *GATHER), (a0, a1, a2, a3)):
+        for dz, at in zip((0, *GATHER), range(NZH)):
+            i = ((x - dx) & (NX - 1)) * NZH + ((z - dz) & (NZH - 1)) - first
+
+            @pl.when((i >= 0) & (i < 8))
+            def _(i=i, strips=strips, at=at):
+                vel, den = strips[at, 0], strips[at, 1]
+                modulus[i] = den * vel * vel
+                buoyancy[i] = 1.0 / den
+
+
+def strip_rows(anchors, own_m, own_b, other_m, other_b):
     c, g = place()
-    odd = (c + anchors[g]) & 1
-    for strips, start in (((own_m, own_b), odd), ((other_m, other_b), 1 - odd)):
+    odd = (c + anchor(anchors, g)) & 1
+    for m, b, start in ((own_m, own_b, odd), (other_m, other_b, 1 - odd)):
         for i in range(8):
             for r in range(4):
-                x = 4 * (start + 2 * i) + r
-                for f in range(2):
-                    out[f, pl.ds(x, COLS, stride=ROWS), :] = strips[f][i, r]
-
-    def plane(f, y):
-        return out[f, y * ROWS : (y + 1) * ROWS, :]
-
-    for i, (f, y) in enumerate([(0, 0), (0, 1), (0, 2), (1, 0), (1, 1), (1, 2)]):
-        to_prev[i] = plane(f, y)
-    for i, (f, y) in enumerate([(0, 5), (0, 6), (0, 7), (1, 4), (1, 5), (1, 6), (1, 7)]):
-        to_next[i] = plane(f, y)
+                yield 4 * (start + 2 * i) + r, m[i, r], b[i, r]
+
+
+def edge_kernel(anchors, own_m, own_b, other_m, other_b, to_prev, to_next):
+    for x, m, b in strip_rows(anchors, own_m, own_b, other_m, other_b):
+        to_prev[pl.ds(x, 3, stride=ROWS), :] = m[:3]
+        to_prev[pl.ds(x + 3 * ROWS, 3, stride=ROWS), :] = b[:3]
+        to_next[pl.ds(x, 3, stride=ROWS), :] = m[5:]
+        to_next[pl.ds(x + 3 * ROWS, 4, stride=ROWS), :] = b[4:]
+
+
+def model_kernel(anchors, own_m, own_b, other_m, other_b, out):
+    for x, m, b in strip_rows(anchors, own_m, own_b, other_m, other_b):
+        out[0, pl.ds(x, COLS, stride=ROWS), :] = m
+        out[1, pl.ds(x, COLS, stride=ROWS), :] = b
 
 
 def inner_tile():
@@ -275,9 +285,10 @@
     lax.fori_loop(STEPS, STEPS + COLS, image, 0, unroll=2)
 
     c, g = place()
-    odd = (c + anchors[g]) & 1
+    b = anchor(anchors, g)
+    odd = (c + b) & 1
     for out, start in ((keep, odd), (send, 1 - odd)):
-        at = (anchors[g] + start) >> 1
+        at = (b + start) >> 1
         for i in range(8):
             out[at + i] = corr[pl.ds(pl.multiple_of(32 * (start + 2 * i), 32), 32), :]
 
@@ -301,7 +312,7 @@
     return pl.pallas_call(
         outer_kernel,
         out_shape=[shape(16, 32, DEPTH)] * 2 + STATE,
-        in_specs=[SMEM] + [VMEM] * 10,
+        in_specs=[VMEM] * 11,
         out_specs=[VMEM] * 8,
         scratch_shapes=[pltpu.VMEM((COLS * ROWS, DEPTH), F32)],
         input_output_aliases={5 + i: 2 + i for i in range(6)},
@@ -352,7 +363,7 @@
             shape(4, COLS * ROWS, DEPTH),
             shape(13, *plane),
             shape(15, *plane),
-            jax.ShapeDtypeStruct(anchors.shape, anchors.dtype),
+            jax.ShapeDtypeStruct((1, *anchors.shape), anchors.dtype),
         ],
         in_specs=[HBM] * 3,
         out_specs=[VMEM] * 4,
@@ -364,7 +375,7 @@
         ],
         compiler_params=params(8),
         name="pack",
-    )(*(pltpu.with_memory_space_constraint(a, pltpu.HBM) for a in (src_state, rcv_state, anchors)))
+    )(*(pltpu.with_memory_space_constraint(a, pltpu.HBM) for a in (src_state, rcv_state, anchors[None])))
     *zs, own, to_prev, to_next = lax.optimization_barrier((*zs, own, to_prev, to_next))
 
     xs = [jnp.concatenate([strip, *zs])]
@@ -382,26 +393,36 @@
         name="inject",
     )(src_pos, wavelet[0].T, rec_pos, traces[0].T)
 
-    *mine, other_m, other_b = pl.pallas_call(
-        window_kernel,
-        out_shape=[shape(8, *strip.shape[2:])] * 4,
-        in_specs=[SMEM] + [VMEM] * 4,
-        out_specs=[VMEM] * 4,
-        compiler_params=params(2),
-        name="window",
-    )(anchors, *xs)
-    got = [other_core(o) for o in (other_m, other_b)]
-
-    mb, mb_prev, mb_next = pl.pallas_call(
+    other, mine = [
+        pl.pallas_call(
+            functools.partial(window_kernel, offset),
+            out_shape=[shape(8, *strip.shape[2:])] * 2,
+            in_specs=[VMEM] * 5,
+            out_specs=[VMEM] * 2,
+            compiler_params=params(2),
+            name="window%d" % offset,
+        )(anchors, *xs)
+        for offset in (1, 0)
+    ]
+    model = (anchors, *mine, *(other_core(block) for block in other))
+    edge_prev, edge_next = pl.pallas_call(
+        edge_kernel,
+        out_shape=[shape(6 * ROWS, DEPTH), shape(7 * ROWS, DEPTH)],
+        in_specs=[VMEM] * 5,
+        out_specs=[VMEM] * 2,
+        compiler_params=params(2),
+        name="edge",
+    )(*model)
+    model_next = to_tile(edge_prev.reshape(6, *plane), -1)
+    model_prev = to_tile(edge_next.reshape(7, *plane), 1)
+    mb = pl.pallas_call(
         model_kernel,
-        out_shape=[shape(2, COLS * ROWS, DEPTH), shape(6, *plane), shape(7, *plane)],
-        in_specs=[SMEM] + [VMEM] * 4,
-        out_specs=[VMEM] * 3,
+        out_shape=shape(2, COLS * ROWS, DEPTH),
+        in_specs=[VMEM] * 5,
+        out_specs=VMEM,
         compiler_params=params(2),
         name="model",
-    )(anchors, *mine, *got)
-    model_next = to_tile(mb_prev, -1)
-    model_prev = to_tile(mb_next, 1)
+    )(*model)
 
     state = inner(
         own.reshape(4, COLS, *plane),

time: 60.9 us -> 59.8 us (0.982)
  Pallas kernels: 11.1 us -> 10.4 us
    pallas_call x2 -> x4, Pallas kernels: 1.86 us -> 1.54 us  [the longest x1 0.54 us: local(): pl.pallas_call(model_kernel, out_shape=shape(2, COLS * ROWS, DEPTH), in_s...]
  transfers between devices with their start and end apart: 19 -> 19, of which waited for: 13 -> 12; matrix products, arithmetic and copies ran while one was open for 0% -> 0% of each run, Pallas kernels for 14% -> 13%
where the time goes in v5:
time: 59.8 us; the launch traced here: 59.2 us
  starting transfers between devices  32.5 us (54%)
  waiting for transfers between devices  15.3 us (26%)
  Pallas kernels  10.4 us (17%)
  other arithmetic  0.79 us (1%)
    ppermute x12, starting transfers between devices, along(): lax.ppermute(blocks[d - 1], axis, [(i, (i + d) % 4) for i in range(4)])  27.7 us
    ppermute x12, waiting for transfers between devices, along(): lax.ppermute(blocks[d - 1], axis, [(i, (i + d) % 4) for i in range(4)])  8.53 us
    ppermute x4, waiting for transfers between devices, to_tile(): lax.ppermute(block, 'tile', [(i, (i + distance) % NT) for i in range(NT)])  4.54 us
    ppermute x4, starting transfers between devices, to_tile(): lax.ppermute(block, 'tile', [(i, (i + distance) % NT) for i in range(NT)])  4.13 us
    pallas_call x1, Pallas kernels, local(): pl.pallas_call(pack_kernel, out_shape=[shape(4, COLS * ROWS, DEPTH), shap...  2.64 us
    ppermute x3, waiting for transfers between devices, other_core(): return lax.ppermute(block, 'core', [(0, 1), (1, 0)])  2.27 us
    pallas_call x1, Pallas kernels, local(): pl.pallas_call(inject_kernel, out_shape=[shape(STEPS, PLANES, *plane)] *...  1.97 us
    pallas_call x1, Pallas kernels, outer(): pl.pallas_call(outer_kernel, out_shape=[shape(16, 32, DEPTH)] * 2 + STATE...  1.79 us
  transfers between devices with their start and end apart: 19, of which 12 were waited for; matrix products, arithmetic and copies ran while one was open for 0% of the time, Pallas kernels for 13%

profile of v5, /device:TPU:24, one launch (start us, length us, event | category | flops | bytes accessed | tf_op | source)
XLA Modules:
  0.0 59.2 jit_solution(16112751747946242510)
XLA Ops:
  0.0 0.0 copy-start.1
  0.0 0.0 copy-start.3
  0.0 0.0 copy-start
  0.0 0.0 copy-start.2
  0.0 0.8 %maximum_bitcast_fusion = f32[1,2,4,8,128]{4,3,2,1,0:T(8,128)S(1)} fusion(f32[1,4,8,128]{3,2,1,0:T(8,128)} %bitcast.22, f32[1,4,8,128]{3,2,1,0:T(8,128)} %bitcast.23), kind=kLoop, calls=%fused_computation.1 | loop fusion | flops 8192 | bytes 65536 | tf_op jit(solution)/shard_map/broadcast_in_dim | solution.py:357
  0.8 7.2 %collective-permute-start.2 = (f32[1,2,4,8,128]{4,3,2,1,0:T(8,128)S(1)}, f32[1,2,4,8,128]{4,3,2,1,0:T(8,128)S(1)}, u32[]{:S(2)}, u32[]{:S(2)}) collective-permute-start(f32[1,2,4,8,128]{4,3,2,1,0:T(8,128)S(1)} %maximum_bitcast_fusion), channel_id=1, source_target_pairs={{0,32},{16,48},{32,0},{48,16},{1,33},{17,49},{33,1},{49,17},{2,34}... | collective-permute-start | bytes 98312 | tf_op jit(solution)/shard_map/ppermute | solution.py:352
  8.0 1.5 %collective-permute-start.1 = (f32[1,2,4,8,128]{4,3,2,1,0:T(8,128)S(1)}, f32[1,2,4,8,128]{4,3,2,1,0:T(8,128)S(1)}, u32[]{:S(2)}, u32[]{:S(2)}) collective-permute-start(f32[1,2,4,8,128]{4,3,2,1,0:T(8,128)S(1)} %maximum_bitcast_fusion), channel_id=1, source_target_pairs={{0,16},{16,32},{32,48},{48,0},{1,17},{17,33},{33,49},{49,1},{2,18}... | collective-permute-start | bytes 98312 | tf_op jit(solution)/shard_map/ppermute | solution.py:352
  9.5 2.7 %collective-permute-start = (f32[1,2,4,8,128]{4,3,2,1,0:T(8,128)S(1)}, f32[1,2,4,8,128]{4,3,2,1,0:T(8,128)S(1)}, u32[]{:S(2)}, u32[]{:S(2)}) collective-permute-start(f32[1,2,4,8,128]{4,3,2,1,0:T(8,128)S(1)} %maximum_bitcast_fusion), channel_id=1, source_target_pairs={{0,48},{16,0},{32,16},{48,32},{1,49},{17,1},{33,17},{49,33},{2,50}... | collective-permute-start | bytes 98312 | tf_op jit(solution)/shard_map/ppermute | solution.py:352
  12.1 2.6 %pack.1 = (f32[4,512,128]{2,1,0:T(8,128)S(1)}, f32[13,64,128]{2,1,0:T(8,128)S(1)}, f32[15,64,128]{2,1,0:T(8,128)S(1)}, s32[1,32]{1,0:T(1,128)S(1)}) custom-call(f32[4,64,8,128]{3,2,1,0:T(8,128)} %src_in.1, f32[4,64,8,128]{3,2,1,0:T(8,128)} %rcv_in.1, s32[1,32]{1,0:T(1,128)} %bitcast.24), custom_call_target="tpu_custom_call" | custom-call | tf_op jit(solution)/shard_map/pack/pallas_call | solution.py:360
  14.8 0.0 collective-permute-done.2
  14.8 0.0 collective-permute-done.1
  14.8 0.0 collective-permute-done
  14.8 3.1 %collective-permute-start.5 = (f32[4,2,4,8,128]{4,3,2,1,0:T(8,128)S(1)}, f32[4,2,4,8,128]{4,3,2,1,0:T(8,128)S(1)}, u32[]{:S(2)}, u32[]{:S(2)}) collective-permute-start(f32[4,2,4,8,128]{4,3,2,1,0:T(8,128)S(1)} %pad_maximum_fusion.a0), channel_id=1, source_target_pairs={{0,128},{64,192},{128,0},{192,64},{1,129},{65,193},{129,1},{193,65... | collective-permute-start | bytes 393224 | tf_op jit(solution)/shard_map/ppermute | solution.py:352
  17.9 0.6 %collective-permute-start.4 = (f32[4,2,4,8,128]{4,3,2,1,0:T(8,128)S(1)}, f32[4,2,4,8,128]{4,3,2,1,0:T(8,128)S(1)}, u32[]{:S(2)}, u32[]{:S(2)}) collective-permute-start(f32[4,2,4,8,128]{4,3,2,1,0:T(8,128)S(1)} %pad_maximum_fusion.a0), channel_id=1, source_target_pairs={{0,64},{64,128},{128,192},{192,0},{1,65},{65,129},{129,193},{193,1... | collective-permute-start | bytes 393224 | tf_op jit(solution)/shard_map/ppermute | solution.py:352
  18.5 2.6 %collective-permute-start.3 = (f32[4,2,4,8,128]{4,3,2,1,0:T(8,128)S(1)}, f32[4,2,4,8,128]{4,3,2,1,0:T(8,128)S(1)}, u32[]{:S(2)}, u32[]{:S(2)}) collective-permute-start(f32[4,2,4,8,128]{4,3,2,1,0:T(8,128)S(1)} %pad_maximum_fusion.a0), channel_id=1, source_target_pairs={{0,192},{64,0},{128,64},{192,128},{1,193},{65,1},{129,65},{193,129... | collective-permute-start | bytes 393224 | tf_op jit(solution)/shard_map/ppermute | solution.py:352
  21.2 0.7 %collective-permute-start.10 = (f32[15,64,128]{2,1,0:T(8,128)S(1)}, f32[15,64,128]{2,1,0:T(8,128)S(1)}, u32[]{:S(2)}, u32[]{:S(2)}) collective-permute-start(f32[15,64,128]{2,1,0:T(8,128)S(1)} %get-tuple-element.55.mine), channel_id=1, source_target_pairs={{0,1},{1,2},{2,3},{3,4},{4,5},{5,6},{6,7},{7,0},{8,9},{9,10},{10,1... | collective-permute-start | bytes 1474568 | tf_op jit(solution)/shard_map/ppermute | solution.py:348
  21.8 1.3 %collective-permute-start.11 = (f32[13,64,128]{2,1,0:T(8,128)S(1)}, f32[13,64,128]{2,1,0:T(8,128)S(1)}, u32[]{:S(2)}, u32[]{:S(2)}) collective-permute-start(f32[13,64,128]{2,1,0:T(8,128)S(1)} %get-tuple-element.56), channel_id=1, source_target_pairs={{0,7},{1,0},{2,1},{3,2},{4,3},{5,4},{6,5},{7,6},{8,15},{9,8},{10,9... | collective-permute-start | bytes 1277960 | tf_op jit(solution)/shard_map/ppermute | solution.py:348
  23.2 0.0 collective-permute-done.5.a3
  23.2 1.2 %collective-permute-done.4.a2 = f32[4,2,4,8,128]{4,3,2,1,0:T(8,128)S(1)} collective-permute-done((f32[4,2,4,8,128]{4,3,2,1,0:T(8,128)S(1)}, f32[4,2,4,8,128]{4,3,2,1,0:T(8,128)S(1)}, u32[]{:S(2)}, u32[]{:S(2)}) %collective-permute-start.4) | collective-permute-done | bytes 131104 | tf_op jit(solution)/shard_map/ppermute | solution.py:352
  24.4 0.0 collective-permute-done.3.a1
  24.4 0.3 window1.1
  24.7 0.1 collective-permute-start.6
  24.8 0.5 collective-permute-start.7
  25.3 0.3 window0.1
  25.6 0.6 collective-permute-done.6.other_m
  26.1 0.2 collective-permute-done.7.other_b
  26.3 0.5 edge.1
  26.8 1.7 %collective-permute-start.8 = (f32[7,64,128]{2,1,0:T(8,128)S(1)}, f32[7,64,128]{2,1,0:T(8,128)S(1)}, u32[]{:S(2)}, u32[]{:S(2)}) collective-permute-start(f32[7,64,128]{2,1,0:T(8,128)S(1)} %bitcast.20), channel_id=1, source_target_pairs={{0,1},{1,2},{2,3},{3,4},{4,5},{5,6},{6,7},{7,0},{8,9},{9,10},{10,1... | collective-permute-start | bytes 688136 | tf_op jit(solution)/shard_map/ppermute | solution.py:348
  28.5 0.4 collective-permute-start.9
  28.9 0.0 copy-done.1
  28.9 0.0 copy-done.3
  28.9 0.0 copy-done
  28.9 0.0 copy-done.2
  28.9 2.0 %inject.1 = (f32[4,16,64,128]{3,2,1,0:T(8,128)S(1)}, f32[4,16,64,128]{3,2,1,0:T(8,128)S(1)}) custom-call(s32[1,16]{1,0:T(1,128)S(1)} %copy-done.2, f32[4,16]{1,0:T(4,128)S(1)} %bitcast.18, s32[1,128]{1,0:T(1,128)S(1)} %copy-done.3, f32[4,128]{1,0:T(4,128)S(1)} %bitcast.19), custom_call_target="tpu_custom_call" | custom-call | tf_op jit(solution)/shard_map/inject/pallas_call | solution.py:387
  30.9 0.5 model.1
  31.4 2.4 %collective-permute-done.11.nxt = f32[13,64,128]{2,1,0:T(8,128)S(1)} collective-permute-done((f32[13,64,128]{2,1,0:T(8,128)S(1)}, f32[13,64,128]{2,1,0:T(8,128)S(1)}, u32[]{:S(2)}, u32[]{:S(2)}) %collective-permute-start.11) | collective-permute-done | bytes 426016 | tf_op jit(solution)/shard_map/ppermute | solution.py:348
  33.8 1.1 %collective-permute-done.10.prev = f32[15,64,128]{2,1,0:T(8,128)S(1)} collective-permute-done((f32[15,64,128]{2,1,0:T(8,128)S(1)}, f32[15,64,128]{2,1,0:T(8,128)S(1)}, u32[]{:S(2)}, u32[]{:S(2)}) %collective-permute-start.10) | collective-permute-done | bytes 491552 | tf_op jit(solution)/shard_map/ppermute | solution.py:348
  34.9 1.8 %inner.1 = (f32[5,16,64,128]{3,2,1,0:T(8,128)S(1)}, f32[5,16,64,128]{3,2,1,0:T(8,128)S(1)}, f32[16,64,128]{2,1,0:T(8,128)S(1)}, f32[16,64,128]{2,1,0:T(8,128)S(1...) custom-call(f32[4,8,64,128]{3,2,1,0:T(8,128)S(1)} %bitcast.17, ...), custom_call_target="tpu_custom_call" | custom-call | tf_op jit(solution)/shard_map/inner/pallas_call | solution.py:300
  36.7 1.1 %collective-permute-done.9.model_next = f32[6,64,128]{2,1,0:T(8,128)S(1)} collective-permute-done((f32[6,64,128]{2,1,0:T(8,128)S(1)}, f32[6,64,128]{2,1,0:T(8,128)S(1)}, u32[]{:S(2)}, u32[]{:S(2)}) %collective-permute-start.9) | collective-permute-done | bytes 196640 | tf_op jit(solution)/shard_map/ppermute | solution.py:348
  37.8 0.0 collective-permute-done.8.model_prev
  37.8 1.8 %outer.1 = (f32[16,32,128]{2,1,0:T(8,128)S(1)}, f32[16,32,128]{2,1,0:T(8,128)S(1)}, f32[5,16,64,128]{3,2,1,0:T(8,128)S(1)}, f32[5,16,64,128]{3,2,1,0:T(8,128)S(1...) custom-call(s32[1,32]{1,0:T(1,128)S(1)} %get-tuple-element.39.anchor, ...), custom_call_target="tpu_custom_call", output_to_operand_aliasing={{2}: (5, {}), {3}: (6, {}), {4}: (7, {}), {5}: (8, {}), {6}... | custom-call | tf_op jit(solution)/shard_map/outer/pallas_call | solution.py:312
  39.6 0.1 collective-permute-start.12
  39.7 1.5 %collective-permute-done.12.got = f32[16,32,128]{2,1,0:T(8,128)S(1)} collective-permute-done((f32[16,32,128]{2,1,0:T(8,128)S(1)}, f32[16,32,128]{2,1,0:T(8,128)S(1)}, u32[]{:S(2)}, u32[]{:S(2)}) %collective-permute-start.12) | collective-permute-done | bytes 262176 | tf_op jit(solution)/shard_map/ppermute | solution.py:344
  41.2 0.5 collective-permute-start.13
  41.8 2.1 %collective-permute-start.14 = (f32[4,32,128]{2,1,0:T(8,128)S(1)}, f32[4,32,128]{2,1,0:T(8,128)S(1)}, u32[]{:S(2)}, u32[]{:S(2)}) collective-permute-start(f32[4,32,128]{2,1,0:T(8,128)S(1)} %get-tuple-element.67), channel_id=1, source_target_pairs={{0,64},{64,128},{128,192},{192,0},{1,65},{65,129},{129,193},{193,1... | collective-permute-start | bytes 196616 | tf_op jit(solution)/shard_map/ppermute | solution.py:352
  43.8 1.2 %collective-permute-start.15 = (f32[4,32,128]{2,1,0:T(8,128)S(1)}, f32[4,32,128]{2,1,0:T(8,128)S(1)}, u32[]{:S(2)}, u32[]{:S(2)}) collective-permute-start(f32[4,32,128]{2,1,0:T(8,128)S(1)} %get-tuple-element.68), channel_id=1, source_target_pairs={{0,192},{64,0},{128,64},{192,128},{1,193},{65,1},{129,65},{193,129... | collective-permute-start | bytes 196616 | tf_op jit(solution)/shard_map/ppermute | solution.py:352
  45.0 2.7 %collective-permute-done.13.r1 = f32[4,32,128]{2,1,0:T(8,128)S(1)} collective-permute-done((f32[4,32,128]{2,1,0:T(8,128)S(1)}, f32[4,32,128]{2,1,0:T(8,128)S(1)}, u32[]{:S(2)}, u32[]{:S(2)}) %collective-permute-start.13) | collective-permute-done | bytes 65568 | tf_op jit(solution)/shard_map/ppermute | solution.py:352
  47.7 0.6 collective-permute-done.14.r2
  48.2 0.0 collective-permute-done.15.r3
  48.3 2.1 %collective-permute-start.16 = (f32[32,128]{1,0:T(8,128)S(1)}, f32[32,128]{1,0:T(8,128)S(1)}, u32[]{:S(2)}, u32[]{:S(2)}) collective-permute-start(f32[32,128]{1,0:T(8,128)S(1)} %get-tuple-element.70), channel_id=1, source_target_pairs={{0,32},{16,48},{32,0},{48,16},{1,33},{17,49},{33,1},{49,17},{2,34}... | collective-permute-start | bytes 49160 | tf_op jit(solution)/shard_map/ppermute | solution.py:352
  50.4 3.6 %collective-permute-start.17 = (f32[32,128]{1,0:T(8,128)S(1)}, f32[32,128]{1,0:T(8,128)S(1)}, u32[]{:S(2)}, u32[]{:S(2)}) collective-permute-start(f32[32,128]{1,0:T(8,128)S(1)} %get-tuple-element.71), channel_id=1, source_target_pairs={{0,16},{16,32},{32,48},{48,0},{1,17},{17,33},{33,49},{49,1},{2,18}... | collective-permute-start | bytes 49160 | tf_op jit(solution)/shard_map/ppermute | solution.py:352
  53.9 0.6 collective-permute-start.18
  54.5 1.5 %collective-permute-done.16.q1 = f32[32,128]{1,0:T(8,128)S(1)} collective-permute-done((f32[32,128]{1,0:T(8,128)S(1)}, f32[32,128]{1,0:T(8,128)S(1)}, u32[]{:S(2)}, u32[]{:S(2)}) %collective-permute-start.16) | collective-permute-done | bytes 16416 | tf_op jit(solution)/shard_map/ppermute | solution.py:352
  56.0 0.4 collective-permute-done.17.q2
  56.4 2.2 %collective-permute-done.18.q3 = f32[32,128]{1,0:T(8,128)S(1)} collective-permute-done((f32[32,128]{1,0:T(8,128)S(1)}, f32[32,128]{1,0:T(8,128)S(1)}, u32[]{:S(2)}, u32[]{:S(2)}) %collective-permute-start.18) | collective-permute-done | bytes 16416 | tf_op jit(solution)/shard_map/ppermute | solution.py:352
  58.5 0.6 %last.1 = f32[32,128]{1,0:T(8,128)} custom-call(f32[32,128]{1,0:T(8,128)S(1)} %get-tuple-element.69.u0, f32[32,128]{1,0:T(8,128)S(1)} %collective-permute-done.16.q1, f32[32,128]{1,0:T(8,128)S(1)} %collective-permute-done.17.q2, f32[32,128]{1,0:T(8,128)S(1)} %collective-permute-done.18.q3), custom_call_target="tpu_custom_call" | custom-call | tf_op jit(solution)/shard_map/last/pallas_call | solution.py:456
  (3 shorter events, 0.1 us)
Async XLA Ops:
  0.0 28.9 %copy-start.1 = (f32[1,128,4]{1,2,0:T(4,128)S(1)}, f32[1,128,4]{1,2,0:T(4,128)}, u32[]{:S(2)}) copy-start(f32[1,128,4]{1,2,0:T(4,128)} %param.17) | copy-start | bytes 6148
  0.0 28.9 %copy-start.3 = (s32[1,128]{1,0:T(1,128)S(1)}, s32[1,128]{1,0:T(1,128)}, u32[]{:S(2)}) copy-start(s32[1,128]{1,0:T(1,128)} %rec_pos.1) | copy-start | bytes 1540
  0.0 28.9 %copy-start = (f32[1,16,4]{1,2,0:T(4,128)S(1)}, f32[1,16,4]{1,2,0:T(4,128)}, u32[]{:S(2)}) copy-start(f32[1,16,4]{1,2,0:T(4,128)} %param.15) | copy-start | bytes 772
  0.0 28.9 %copy-start.2 = (s32[1,16]{1,0:T(1,128)S(1)}, s32[1,16]{1,0:T(1,128)}, u32[]{:S(2)}) copy-start(s32[1,16]{1,0:T(1,128)} %src_pos.1) | copy-start | bytes 196
  0.8 14.0 %collective-permute-start.2 = (f32[1,2,4,8,128]{4,3,2,1,0:T(8,128)S(1)}, f32[1,2,4,8,128]{4,3,2,1,0:T(8,128)S(1)}, u32[]{:S(2)}, u32[]{:S(2)}) collective-permute-start(f32[1,2,4,8,128]{4,3,2,1,0:T(8,128)S(1)} %maximum_bitcast_fusion), channel_id=1, source_target_pairs={{0,32},{16,48},{32,0},{48,16},{1,33},{17,49},{33,1},{49,17},{2,34}... | collective-permute-start | bytes 98312 | tf_op jit(solution)/shard_map/ppermute | solution.py:352
  8.0 6.8 %collective-permute-start.1 = (f32[1,2,4,8,128]{4,3,2,1,0:T(8,128)S(1)}, f32[1,2,4,8,128]{4,3,2,1,0:T(8,128)S(1)}, u32[]{:S(2)}, u32[]{:S(2)}) collective-permute-start(f32[1,2,4,8,128]{4,3,2,1,0:T(8,128)S(1)} %maximum_bitcast_fusion), channel_id=1, source_target_pairs={{0,16},{16,32},{32,48},{48,0},{1,17},{17,33},{33,49},{49,1},{2,18}... | collective-permute-start | bytes 98312 | tf_op jit(solution)/shard_map/ppermute | solution.py:352
  9.5 5.3 %collective-permute-start = (f32[1,2,4,8,128]{4,3,2,1,0:T(8,128)S(1)}, f32[1,2,4,8,128]{4,3,2,1,0:T(8,128)S(1)}, u32[]{:S(2)}, u32[]{:S(2)}) collective-permute-start(f32[1,2,4,8,128]{4,3,2,1,0:T(8,128)S(1)} %maximum_bitcast_fusion), channel_id=1, source_target_pairs={{0,48},{16,0},{32,16},{48,32},{1,49},{17,1},{33,17},{49,33},{2,50}... | collective-permute-start | bytes 98312 | tf_op jit(solution)/shard_map/ppermute | solution.py:352
  14.8 8.4 %collective-permute-start.5 = (f32[4,2,4,8,128]{4,3,2,1,0:T(8,128)S(1)}, f32[4,2,4,8,128]{4,3,2,1,0:T(8,128)S(1)}, u32[]{:S(2)}, u32[]{:S(2)}) collective-permute-start(f32[4,2,4,8,128]{4,3,2,1,0:T(8,128)S(1)} %pad_maximum_fusion.a0), channel_id=1, source_target_pairs={{0,128},{64,192},{128,0},{192,64},{1,129},{65,193},{129,1},{193,65... | collective-permute-start | bytes 393224 | tf_op jit(solution)/shard_map/ppermute | solution.py:352
  17.9 6.5 %collective-permute-start.4 = (f32[4,2,4,8,128]{4,3,2,1,0:T(8,128)S(1)}, f32[4,2,4,8,128]{4,3,2,1,0:T(8,128)S(1)}, u32[]{:S(2)}, u32[]{:S(2)}) collective-permute-start(f32[4,2,4,8,128]{4,3,2,1,0:T(8,128)S(1)} %pad_maximum_fusion.a0), channel_id=1, source_target_pairs={{0,64},{64,128},{128,192},{192,0},{1,65},{65,129},{129,193},{193,1... | collective-permute-start | bytes 393224 | tf_op jit(solution)/shard_map/ppermute | solution.py:352
  18.5 5.9 %collective-permute-start.3 = (f32[4,2,4,8,128]{4,3,2,1,0:T(8,128)S(1)}, f32[4,2,4,8,128]{4,3,2,1,0:T(8,128)S(1)}, u32[]{:S(2)}, u32[]{:S(2)}) collective-permute-start(f32[4,2,4,8,128]{4,3,2,1,0:T(8,128)S(1)} %pad_maximum_fusion.a0), channel_id=1, source_target_pairs={{0,192},{64,0},{128,64},{192,128},{1,193},{65,1},{129,65},{193,129... | collective-permute-start | bytes 393224 | tf_op jit(solution)/shard_map/ppermute | solution.py:352
  21.2 13.7 %collective-permute-start.10 = (f32[15,64,128]{2,1,0:T(8,128)S(1)}, f32[15,64,128]{2,1,0:T(8,128)S(1)}, u32[]{:S(2)}, u32[]{:S(2)}) collective-permute-start(f32[15,64,128]{2,1,0:T(8,128)S(1)} %get-tuple-element.55.mine), channel_id=1, source_target_pairs={{0,1},{1,2},{2,3},{3,4},{4,5},{5,6},{6,7},{7,0},{8,9},{9,10},{10,1... | collective-permute-start | bytes 1474568 | tf_op jit(solution)/shard_map/ppermute | solution.py:348
  21.8 12.0 %collective-permute-start.11 = (f32[13,64,128]{2,1,0:T(8,128)S(1)}, f32[13,64,128]{2,1,0:T(8,128)S(1)}, u32[]{:S(2)}, u32[]{:S(2)}) collective-permute-start(f32[13,64,128]{2,1,0:T(8,128)S(1)} %get-tuple-element.56), channel_id=1, source_target_pairs={{0,7},{1,0},{2,1},{3,2},{4,3},{5,4},{6,5},{7,6},{8,15},{9,8},{10,9... | collective-permute-start | bytes 1277960 | tf_op jit(solution)/shard_map/ppermute | solution.py:348
  24.7 1.4 %collective-permute-start.6 = (f32[8,4,8,128]{3,2,1,0:T(8,128)S(1)}, f32[8,4,8,128]{3,2,1,0:T(8,128)S(1)}, u32[]{:S(2)}, u32[]{:S(2)}) collective-permute-start(f32[8,4,8,128]{3,2,1,0:T(8,128)S(1)} %get-tuple-element.48), channel_id=1, source_target_pairs={{0,8},{8,0},{1,9},{9,1},{2,10},{10,2},{3,11},{11,3},{4,12},{12,4},... | collective-permute-start | bytes 393224 | tf_op jit(solution)/shard_map/ppermute | solution.py:344
  24.8 1.5 %collective-permute-start.7 = (f32[8,4,8,128]{3,2,1,0:T(8,128)S(1)}, f32[8,4,8,128]{3,2,1,0:T(8,128)S(1)}, u32[]{:S(2)}, u32[]{:S(2)}) collective-permute-start(f32[8,4,8,128]{3,2,1,0:T(8,128)S(1)} %get-tuple-element.49), channel_id=1, source_target_pairs={{0,8},{8,0},{1,9},{9,1},{2,10},{10,2},{3,11},{11,3},{4,12},{12,4},... | collective-permute-start | bytes 393224 | tf_op jit(solution)/shard_map/ppermute | solution.py:344
  26.8 11.0 %collective-permute-start.8 = (f32[7,64,128]{2,1,0:T(8,128)S(1)}, f32[7,64,128]{2,1,0:T(8,128)S(1)}, u32[]{:S(2)}, u32[]{:S(2)}) collective-permute-start(f32[7,64,128]{2,1,0:T(8,128)S(1)} %bitcast.20), channel_id=1, source_target_pairs={{0,1},{1,2},{2,3},{3,4},{4,5},{5,6},{6,7},{7,0},{8,9},{9,10},{10,1... | collective-permute-start | bytes 688136 | tf_op jit(solution)/shard_map/ppermute | solution.py:348
  28.5 9.3 %collective-permute-start.9 = (f32[6,64,128]{2,1,0:T(8,128)S(1)}, f32[6,64,128]{2,1,0:T(8,128)S(1)}, u32[]{:S(2)}, u32[]{:S(2)}) collective-permute-start(f32[6,64,128]{2,1,0:T(8,128)S(1)} %bitcast.21), channel_id=1, source_target_pairs={{0,7},{1,0},{2,1},{3,2},{4,3},{5,4},{6,5},{7,6},{8,15},{9,8},{10,9... | collective-permute-start | bytes 589832 | tf_op jit(solution)/shard_map/ppermute | solution.py:348
  39.6 1.6 %collective-permute-start.12 = (f32[16,32,128]{2,1,0:T(8,128)S(1)}, f32[16,32,128]{2,1,0:T(8,128)S(1)}, u32[]{:S(2)}, u32[]{:S(2)}) collective-permute-start(f32[16,32,128]{2,1,0:T(8,128)S(1)} %get-tuple-element.64), channel_id=1, source_target_pairs={{0,8},{8,0},{1,9},{9,1},{2,10},{10,2},{3,11},{11,3},{4,12},{12,4},... | collective-permute-start | bytes 786440 | tf_op jit(solution)/shard_map/ppermute | solution.py:344
  41.2 6.4 %collective-permute-start.13 = (f32[4,32,128]{2,1,0:T(8,128)S(1)}, f32[4,32,128]{2,1,0:T(8,128)S(1)}, u32[]{:S(2)}, u32[]{:S(2)}) collective-permute-start(f32[4,32,128]{2,1,0:T(8,128)S(1)} %get-tuple-element.66), channel_id=1, source_target_pairs={{0,128},{64,192},{128,0},{192,64},{1,129},{65,193},{129,1},{193,65... | collective-permute-start | bytes 196616 | tf_op jit(solution)/shard_map/ppermute | solution.py:352
  41.8 6.5 %collective-permute-start.14 = (f32[4,32,128]{2,1,0:T(8,128)S(1)}, f32[4,32,128]{2,1,0:T(8,128)S(1)}, u32[]{:S(2)}, u32[]{:S(2)}) collective-permute-start(f32[4,32,128]{2,1,0:T(8,128)S(1)} %get-tuple-element.67), channel_id=1, source_target_pairs={{0,64},{64,128},{128,192},{192,0},{1,65},{65,129},{129,193},{193,1... | collective-permute-start | bytes 196616 | tf_op jit(solution)/shard_map/ppermute | solution.py:352
  43.8 4.4 %collective-permute-start.15 = (f32[4,32,128]{2,1,0:T(8,128)S(1)}, f32[4,32,128]{2,1,0:T(8,128)S(1)}, u32[]{:S(2)}, u32[]{:S(2)}) collective-permute-start(f32[4,32,128]{2,1,0:T(8,128)S(1)} %get-tuple-element.68), channel_id=1, source_target_pairs={{0,192},{64,0},{128,64},{192,128},{1,193},{65,1},{129,65},{193,129... | collective-permute-start | bytes 196616 | tf_op jit(solution)/shard_map/ppermute | solution.py:352
  48.3 7.7 %collective-permute-start.16 = (f32[32,128]{1,0:T(8,128)S(1)}, f32[32,128]{1,0:T(8,128)S(1)}, u32[]{:S(2)}, u32[]{:S(2)}) collective-permute-start(f32[32,128]{1,0:T(8,128)S(1)} %get-tuple-element.70), channel_id=1, source_target_pairs={{0,32},{16,48},{32,0},{48,16},{1,33},{17,49},{33,1},{49,17},{2,34}... | collective-permute-start | bytes 49160 | tf_op jit(solution)/shard_map/ppermute | solution.py:352
  50.4 6.0 %collective-permute-start.17 = (f32[32,128]{1,0:T(8,128)S(1)}, f32[32,128]{1,0:T(8,128)S(1)}, u32[]{:S(2)}, u32[]{:S(2)}) collective-permute-start(f32[32,128]{1,0:T(8,128)S(1)} %get-tuple-element.71), channel_id=1, source_target_pairs={{0,16},{16,32},{32,48},{48,0},{1,17},{17,33},{33,49},{49,1},{2,18}... | collective-permute-start | bytes 49160 | tf_op jit(solution)/shard_map/ppermute | solution.py:352
  53.9 4.6 %collective-permute-start.18 = (f32[32,128]{1,0:T(8,128)S(1)}, f32[32,128]{1,0:T(8,128)S(1)}, u32[]{:S(2)}, u32[]{:S(2)}) collective-permute-start(f32[32,128]{1,0:T(8,128)S(1)} %get-tuple-element.72), channel_id=1, source_target_pairs={{0,48},{16,0},{32,16},{48,32},{1,49},{17,1},{33,17},{49,33},{2,50}... | collective-permute-start | bytes 49160 | tf_op jit(solution)/shard_map/ppermute | solution.py:352

commit v6 on v5

--- a/solution.py
+++ b/solution.py
@@ -258,7 +258,7 @@
 
 def outer_kernel(
     anchors, model_prev, model_next, add_s, add_r, ps_in, pr_in, ds_in, dr_in, mod_in, buoy_in,
-    keep, send, ps, pr, ds, dr, mod, buoy, corr,
+    keep, send, send_far, ps, pr, ds, dr, mod, buoy, corr,
 ):
     del ps_in, pr_in, ds_in, dr_in, mod_in, buoy_in
     below, above = inner_tile()
@@ -268,6 +268,7 @@
     buoy[12:15] = above(model_next[3:6])
     keep[...] = jnp.zeros(keep.shape, F32)
     send[...] = jnp.zeros(send.shape, F32)
+    send_far[...] = jnp.zeros(send_far.shape, F32)
     run, first = stepper(ps, pr, ds, dr, mod, buoy, add_s, add_r)
     first(1, 4)
     first(12, 15)
@@ -282,15 +283,25 @@
         corr[pl.ds(y - STEPS, ROWS, stride=COLS), :] = value / STEPS
         return 0
 
-    lax.fori_loop(STEPS, STEPS + COLS, image, 0, unroll=2)
+    lax.fori_loop(STEPS, STEPS + COLS, image, 0, unroll=8)
 
     c, g = place()
     b = anchor(anchors, g)
     odd = (c + b) & 1
-    for out, start in ((keep, odd), (send, 1 - odd)):
-        at = (b + start) >> 1
-        for i in range(8):
-            out[at + i] = corr[pl.ds(pl.multiple_of(32 * (start + 2 * i), 32), 32), :]
+    x = lax.axis_index("x")
+    for i in range(8):
+        keep[((b + odd) >> 1) + i] = corr[pl.ds(pl.multiple_of(32 * (odd + 2 * i), 32), 32), :]
+        k = 1 - odd + 2 * i
+        j = (b + k) >> 1
+        d = ((j >> 2) - x) & (NX - 1)
+
+        @pl.when(d == 2)
+        def _(k=k, j=j):
+            send_far[j & (NZH - 1)] = corr[pl.ds(pl.multiple_of(32 * k, 32), 32), :]
+
+        @pl.when(d != 2)
+        def _(k=k, j=j, d=d):
+            send[jnp.minimum(d, 2) * NZH + (j & (NZH - 1))] = corr[pl.ds(pl.multiple_of(32 * k, 32), 32), :]
 
 
 STATE = [shape(STEPS + 1, PLANES, ROWS, DEPTH)] * 2 + [shape(PLANES, ROWS, DEPTH)] * 4
@@ -311,22 +322,21 @@
 def outer(*operands):
     return pl.pallas_call(
         outer_kernel,
-        out_shape=[shape(16, 32, DEPTH)] * 2 + STATE,
+        out_shape=[shape(16, 32, DEPTH), shape(12, 32, DEPTH), shape(4, 32, DEPTH)] + STATE,
         in_specs=[VMEM] * 11,
-        out_specs=[VMEM] * 8,
+        out_specs=[VMEM] * 9,
         scratch_shapes=[pltpu.VMEM((COLS * ROWS, DEPTH), F32)],
-        input_output_aliases={5 + i: 2 + i for i in range(6)},
+        input_output_aliases={5 + i: 3 + i for i in range(6)},
         compiler_params=params(4),
         name="outer",
-    )(*operands)[:2]
-
-
-def halve_kernel(keep, got, s0, s1, s2, s3):
+    )(*operands)[:3]
+
+
+def halve_kernel(distances, keep, got, *outs):
     x = lax.axis_index("x")
-    for d, out in enumerate((s0, s1, s2, s3)):
-        at = ((x + d) & (NX - 1)) * NZH
+    for at, (d, out) in enumerate(zip(distances, outs)):
         for i in range(NZH):
-            out[i] = keep[at + i] + got[at + i]
+            out[i] = keep[((x + d) & (NX - 1)) * NZH + i] + got[at * NZH + i]
 
 
 def quarter_kernel(s0, r1, r2, r3, u0, u1, u2, u3):
@@ -433,16 +443,21 @@
         inj_src,
         inj_rec,
     )
-    keep, send = outer(anchors, model_prev, model_next, inj_src, inj_rec, *state)
-
-    parts = pl.pallas_call(
-        halve_kernel,
-        out_shape=[shape(NZH, 32, DEPTH)] * NX,
-        in_specs=[VMEM, VMEM],
-        out_specs=[VMEM] * NX,
-        compiler_params=params(2),
-        name="halve",
-    )(keep, other_core(send))
+    keep, send, send_far = outer(anchors, model_prev, model_next, inj_src, inj_rec, *state)
+
+    def halve(distances, block):
+        return pl.pallas_call(
+            functools.partial(halve_kernel, distances),
+            out_shape=[shape(NZH, 32, DEPTH)] * len(distances),
+            in_specs=[VMEM, VMEM],
+            out_specs=[VMEM] * len(distances),
+            compiler_params=params(2),
+            name="halve%d" % len(distances),
+        )(keep, other_core(block))
+
+    (far,) = halve((2,), send_far)
+    stay, after, before = halve((0, 1, 3), send)
+    parts = [stay, after, far, before]
     moved = along(parts[1:], "x", SCATTER)
     parts = pl.pallas_call(
         quarter_kernel,

time: 59.8 us -> 59.9 us (level)
    ppermute x3 -> x4, waiting for transfers between devices: 2.27 us -> 1.77 us  [other_core(): return lax.ppermute(block, 'core', [(0, 1), (1, 0)])]
    pallas_call x2 -> x3, Pallas kernels: 1.82 us -> 1.77 us  [the longest x1 1.73 us: outer(): pl.pallas_call(outer_kernel, out_shape=[shape(16, 32, DEPTH), shape(12, 3...]
  transfers between devices with their start and end apart: 19 -> 20, of which waited for: 12 -> 12; matrix products, arithmetic and copies ran while one was open for 0% -> 0% of each run, Pallas kernels for 13% -> 13%
where the time goes in v6:
time: 59.9 us; the launch traced here: 59.2 us
  starting transfers between devices  33 us (55%)
  waiting for transfers between devices  14.9 us (25%)
  Pallas kernels  10.3 us (17%)
  other arithmetic  0.79 us (1%)
    ppermute x12, starting transfers between devices, along(): lax.ppermute(blocks[d - 1], axis, [(i, (i + d) % 4) for i in range(4)])  27.6 us
    ppermute x12, waiting for transfers between devices, along(): lax.ppermute(blocks[d - 1], axis, [(i, (i + d) % 4) for i in range(4)])  8.63 us
    ppermute x4, waiting for transfers between devices, to_tile(): lax.ppermute(block, 'tile', [(i, (i + distance) % NT) for i in range(NT)])  4.54 us
    ppermute x4, starting transfers between devices, to_tile(): lax.ppermute(block, 'tile', [(i, (i + distance) % NT) for i in range(NT)])  4.13 us
    pallas_call x1, Pallas kernels, local(): pl.pallas_call(pack_kernel, out_shape=[shape(4, COLS * ROWS, DEPTH), shap...  2.64 us
    pallas_call x1, Pallas kernels, local(): pl.pallas_call(inject_kernel, out_shape=[shape(STEPS, PLANES, *plane)] *...  1.97 us
    pallas_call x1, Pallas kernels, inner(): pl.pallas_call(inner_kernel, out_shape=STATE, in_specs=[VMEM] * 7, out_sp...  1.78 us
    ppermute x4, waiting for transfers between devices, other_core(): return lax.ppermute(block, 'core', [(0, 1), (1, 0)])  1.77 us
  transfers between devices with their start and end apart: 20, of which 12 were waited for; matrix products, arithmetic and copies ran while one was open for 0% of the time, Pallas kernels for 13%

profile of v6, /device:TPU:24, one launch (start us, length us, event | category | flops | bytes accessed | tf_op | source)
XLA Modules:
  0.0 59.2 jit_solution(11283732727079521330)
XLA Ops:
  0.0 0.0 copy-start.1
  0.0 0.0 copy-start.3
  0.0 0.0 copy-start
  0.0 0.0 copy-start.2
  0.0 0.8 %maximum_bitcast_fusion = f32[1,2,4,8,128]{4,3,2,1,0:T(8,128)S(1)} fusion(f32[1,4,8,128]{3,2,1,0:T(8,128)} %bitcast.22, f32[1,4,8,128]{3,2,1,0:T(8,128)} %bitcast.23), kind=kLoop, calls=%fused_computation.1 | loop fusion | flops 8192 | bytes 65536 | tf_op jit(solution)/shard_map/broadcast_in_dim | solution.py:367
  0.8 7.2 %collective-permute-start.2 = (f32[1,2,4,8,128]{4,3,2,1,0:T(8,128)S(1)}, f32[1,2,4,8,128]{4,3,2,1,0:T(8,128)S(1)}, u32[]{:S(2)}, u32[]{:S(2)}) collective-permute-start(f32[1,2,4,8,128]{4,3,2,1,0:T(8,128)S(1)} %maximum_bitcast_fusion), channel_id=1, source_target_pairs={{0,32},{16,48},{32,0},{48,16},{1,33},{17,49},{33,1},{49,17},{2,34}... | collective-permute-start | bytes 98312 | tf_op jit(solution)/shard_map/ppermute | solution.py:362
  8.0 1.5 %collective-permute-start.1 = (f32[1,2,4,8,128]{4,3,2,1,0:T(8,128)S(1)}, f32[1,2,4,8,128]{4,3,2,1,0:T(8,128)S(1)}, u32[]{:S(2)}, u32[]{:S(2)}) collective-permute-start(f32[1,2,4,8,128]{4,3,2,1,0:T(8,128)S(1)} %maximum_bitcast_fusion), channel_id=1, source_target_pairs={{0,16},{16,32},{32,48},{48,0},{1,17},{17,33},{33,49},{49,1},{2,18}... | collective-permute-start | bytes 98312 | tf_op jit(solution)/shard_map/ppermute | solution.py:362
  9.5 2.7 %collective-permute-start = (f32[1,2,4,8,128]{4,3,2,1,0:T(8,128)S(1)}, f32[1,2,4,8,128]{4,3,2,1,0:T(8,128)S(1)}, u32[]{:S(2)}, u32[]{:S(2)}) collective-permute-start(f32[1,2,4,8,128]{4,3,2,1,0:T(8,128)S(1)} %maximum_bitcast_fusion), channel_id=1, source_target_pairs={{0,48},{16,0},{32,16},{48,32},{1,49},{17,1},{33,17},{49,33},{2,50}... | collective-permute-start | bytes 98312 | tf_op jit(solution)/shard_map/ppermute | solution.py:362
  12.1 2.6 %pack.1 = (f32[4,512,128]{2,1,0:T(8,128)S(1)}, f32[13,64,128]{2,1,0:T(8,128)S(1)}, f32[15,64,128]{2,1,0:T(8,128)S(1)}, s32[1,32]{1,0:T(1,128)S(1)}) custom-call(f32[4,64,8,128]{3,2,1,0:T(8,128)} %src_in.1, f32[4,64,8,128]{3,2,1,0:T(8,128)} %rcv_in.1, s32[1,32]{1,0:T(1,128)} %bitcast.24), custom_call_target="tpu_custom_call" | custom-call | tf_op jit(solution)/shard_map/pack/pallas_call | solution.py:370
  14.8 0.0 collective-permute-done.2
  14.8 0.0 collective-permute-done.1
  14.8 0.0 collective-permute-done
  14.8 3.1 %collective-permute-start.5 = (f32[4,2,4,8,128]{4,3,2,1,0:T(8,128)S(1)}, f32[4,2,4,8,128]{4,3,2,1,0:T(8,128)S(1)}, u32[]{:S(2)}, u32[]{:S(2)}) collective-permute-start(f32[4,2,4,8,128]{4,3,2,1,0:T(8,128)S(1)} %pad_maximum_fusion.a0), channel_id=1, source_target_pairs={{0,128},{64,192},{128,0},{192,64},{1,129},{65,193},{129,1},{193,65... | collective-permute-start | bytes 393224 | tf_op jit(solution)/shard_map/ppermute | solution.py:362
  17.9 0.6 %collective-permute-start.4 = (f32[4,2,4,8,128]{4,3,2,1,0:T(8,128)S(1)}, f32[4,2,4,8,128]{4,3,2,1,0:T(8,128)S(1)}, u32[]{:S(2)}, u32[]{:S(2)}) collective-permute-start(f32[4,2,4,8,128]{4,3,2,1,0:T(8,128)S(1)} %pad_maximum_fusion.a0), channel_id=1, source_target_pairs={{0,64},{64,128},{128,192},{192,0},{1,65},{65,129},{129,193},{193,1... | collective-permute-start | bytes 393224 | tf_op jit(solution)/shard_map/ppermute | solution.py:362
  18.5 2.6 %collective-permute-start.3 = (f32[4,2,4,8,128]{4,3,2,1,0:T(8,128)S(1)}, f32[4,2,4,8,128]{4,3,2,1,0:T(8,128)S(1)}, u32[]{:S(2)}, u32[]{:S(2)}) collective-permute-start(f32[4,2,4,8,128]{4,3,2,1,0:T(8,128)S(1)} %pad_maximum_fusion.a0), channel_id=1, source_target_pairs={{0,192},{64,0},{128,64},{192,128},{1,193},{65,1},{129,65},{193,129... | collective-permute-start | bytes 393224 | tf_op jit(solution)/shard_map/ppermute | solution.py:362
  21.2 0.7 %collective-permute-start.10 = (f32[15,64,128]{2,1,0:T(8,128)S(1)}, f32[15,64,128]{2,1,0:T(8,128)S(1)}, u32[]{:S(2)}, u32[]{:S(2)}) collective-permute-start(f32[15,64,128]{2,1,0:T(8,128)S(1)} %get-tuple-element.55.mine), channel_id=1, source_target_pairs={{0,1},{1,2},{2,3},{3,4},{4,5},{5,6},{6,7},{7,0},{8,9},{9,10},{10,1... | collective-permute-start | bytes 1474568 | tf_op jit(solution)/shard_map/ppermute | solution.py:358
  21.8 1.3 %collective-permute-start.11 = (f32[13,64,128]{2,1,0:T(8,128)S(1)}, f32[13,64,128]{2,1,0:T(8,128)S(1)}, u32[]{:S(2)}, u32[]{:S(2)}) collective-permute-start(f32[13,64,128]{2,1,0:T(8,128)S(1)} %get-tuple-element.56), channel_id=1, source_target_pairs={{0,7},{1,0},{2,1},{3,2},{4,3},{5,4},{6,5},{7,6},{8,15},{9,8},{10,9... | collective-permute-start | bytes 1277960 | tf_op jit(solution)/shard_map/ppermute | solution.py:358
  23.2 0.0 collective-permute-done.5.a3
  23.2 1.2 %collective-permute-done.4.a2 = f32[4,2,4,8,128]{4,3,2,1,0:T(8,128)S(1)} collective-permute-done((f32[4,2,4,8,128]{4,3,2,1,0:T(8,128)S(1)}, f32[4,2,4,8,128]{4,3,2,1,0:T(8,128)S(1)}, u32[]{:S(2)}, u32[]{:S(2)}) %collective-permute-start.4) | collective-permute-done | bytes 131104 | tf_op jit(solution)/shard_map/ppermute | solution.py:362
  24.4 0.0 collective-permute-done.3.a1
  24.4 0.3 window1.1
  24.7 0.1 collective-permute-start.6
  24.8 0.5 collective-permute-start.7
  25.3 0.3 window0.1
  25.6 0.6 collective-permute-done.6.other_m
  26.1 0.2 collective-permute-done.7.other_b
  26.3 0.5 edge.1
  26.8 1.7 %collective-permute-start.8 = (f32[7,64,128]{2,1,0:T(8,128)S(1)}, f32[7,64,128]{2,1,0:T(8,128)S(1)}, u32[]{:S(2)}, u32[]{:S(2)}) collective-permute-start(f32[7,64,128]{2,1,0:T(8,128)S(1)} %bitcast.20), channel_id=1, source_target_pairs={{0,1},{1,2},{2,3},{3,4},{4,5},{5,6},{6,7},{7,0},{8,9},{9,10},{10,1... | collective-permute-start | bytes 688136 | tf_op jit(solution)/shard_map/ppermute | solution.py:358
  28.5 0.4 collective-permute-start.9
  28.9 0.0 copy-done.1
  28.9 0.0 copy-done.3
  28.9 0.0 copy-done
  28.9 0.0 copy-done.2
  28.9 2.0 %inject.1 = (f32[4,16,64,128]{3,2,1,0:T(8,128)S(1)}, f32[4,16,64,128]{3,2,1,0:T(8,128)S(1)}) custom-call(s32[1,16]{1,0:T(1,128)S(1)} %copy-done.2, f32[4,16]{1,0:T(4,128)S(1)} %bitcast.18, s32[1,128]{1,0:T(1,128)S(1)} %copy-done.3, f32[4,128]{1,0:T(4,128)S(1)} %bitcast.19), custom_call_target="tpu_custom_call" | custom-call | tf_op jit(solution)/shard_map/inject/pallas_call | solution.py:397
  30.9 0.5 model.1
  31.4 2.4 %collective-permute-done.11.nxt = f32[13,64,128]{2,1,0:T(8,128)S(1)} collective-permute-done((f32[13,64,128]{2,1,0:T(8,128)S(1)}, f32[13,64,128]{2,1,0:T(8,128)S(1)}, u32[]{:S(2)}, u32[]{:S(2)}) %collective-permute-start.11) | collective-permute-done | bytes 426016 | tf_op jit(solution)/shard_map/ppermute | solution.py:358
  33.8 1.1 %collective-permute-done.10.prev = f32[15,64,128]{2,1,0:T(8,128)S(1)} collective-permute-done((f32[15,64,128]{2,1,0:T(8,128)S(1)}, f32[15,64,128]{2,1,0:T(8,128)S(1)}, u32[]{:S(2)}, u32[]{:S(2)}) %collective-permute-start.10) | collective-permute-done | bytes 491552 | tf_op jit(solution)/shard_map/ppermute | solution.py:358
  34.9 1.8 %inner.1 = (f32[5,16,64,128]{3,2,1,0:T(8,128)S(1)}, f32[5,16,64,128]{3,2,1,0:T(8,128)S(1)}, f32[16,64,128]{2,1,0:T(8,128)S(1)}, f32[16,64,128]{2,1,0:T(8,128)S(1...) custom-call(f32[4,8,64,128]{3,2,1,0:T(8,128)S(1)} %bitcast.17, ...), custom_call_target="tpu_custom_call" | custom-call | tf_op jit(solution)/shard_map/inner/pallas_call | solution.py:311
  36.7 1.1 %collective-permute-done.9.model_next = f32[6,64,128]{2,1,0:T(8,128)S(1)} collective-permute-done((f32[6,64,128]{2,1,0:T(8,128)S(1)}, f32[6,64,128]{2,1,0:T(8,128)S(1)}, u32[]{:S(2)}, u32[]{:S(2)}) %collective-permute-start.9) | collective-permute-done | bytes 196640 | tf_op jit(solution)/shard_map/ppermute | solution.py:358
  37.8 0.0 collective-permute-done.8.model_prev
  37.8 1.7 %outer.1 = (f32[16,32,128]{2,1,0:T(8,128)S(1)}, f32[12,32,128]{2,1,0:T(8,128)S(1)}, f32[4,32,128]{2,1,0:T(8,128)S(1)}, f32[5,16,64,128]{3,2,1,0:T(8,128)S(1)}, f...) custom-call(s32[1,32]{1,0:T(1,128)S(1)} %get-tuple-element.39.anchor, ...), custom_call_target="tpu_custom_call", output_to_operand_aliasing={{3}: (5, {}), {4}: (6, {}), {5}: (7, {}), {6}: (8, {}), {7}... | custom-call | tf_op jit(solution)/shard_map/outer/pallas_call | solution.py:323
  39.5 0.1 collective-permute-start.12
  39.6 0.5 collective-permute-start.13
  40.1 1.0 %collective-permute-done.13.got = f32[4,32,128]{2,1,0:T(8,128)S(1)} collective-permute-done((f32[4,32,128]{2,1,0:T(8,128)S(1)}, f32[4,32,128]{2,1,0:T(8,128)S(1)}, u32[]{:S(2)}, u32[]{:S(2)}) %collective-permute-start.13) | collective-permute-done | bytes 65568 | tf_op jit(solution)/shard_map/ppermute | solution.py:354
  41.1 0.5 collective-permute-start.14
  41.7 0.0 collective-permute-done.12.got
  41.7 2.1 %collective-permute-start.15 = (f32[4,32,128]{2,1,0:T(8,128)S(1)}, f32[4,32,128]{2,1,0:T(8,128)S(1)}, u32[]{:S(2)}, u32[]{:S(2)}) collective-permute-start(f32[4,32,128]{2,1,0:T(8,128)S(1)} %get-tuple-element.67), channel_id=1, source_target_pairs={{0,64},{64,128},{128,192},{192,0},{1,65},{65,129},{129,193},{193,1... | collective-permute-start | bytes 196616 | tf_op jit(solution)/shard_map/ppermute | solution.py:362
  43.9 1.2 %collective-permute-start.16 = (f32[4,32,128]{2,1,0:T(8,128)S(1)}, f32[4,32,128]{2,1,0:T(8,128)S(1)}, u32[]{:S(2)}, u32[]{:S(2)}) collective-permute-start(f32[4,32,128]{2,1,0:T(8,128)S(1)} %get-tuple-element.68), channel_id=1, source_target_pairs={{0,192},{64,0},{128,64},{192,128},{1,193},{65,1},{129,65},{193,129... | collective-permute-start | bytes 196616 | tf_op jit(solution)/shard_map/ppermute | solution.py:362
  45.0 2.6 %collective-permute-done.14.r1 = f32[4,32,128]{2,1,0:T(8,128)S(1)} collective-permute-done((f32[4,32,128]{2,1,0:T(8,128)S(1)}, f32[4,32,128]{2,1,0:T(8,128)S(1)}, u32[]{:S(2)}, u32[]{:S(2)}) %collective-permute-start.14) | collective-permute-done | bytes 65568 | tf_op jit(solution)/shard_map/ppermute | solution.py:362
  47.7 0.7 %collective-permute-done.15.r2 = f32[4,32,128]{2,1,0:T(8,128)S(1)} collective-permute-done((f32[4,32,128]{2,1,0:T(8,128)S(1)}, f32[4,32,128]{2,1,0:T(8,128)S(1)}, u32[]{:S(2)}, u32[]{:S(2)}) %collective-permute-start.15) | collective-permute-done | bytes 65568 | tf_op jit(solution)/shard_map/ppermute | solution.py:362
  48.4 0.0 collective-permute-done.16.r3
  48.4 2.0 %collective-permute-start.17 = (f32[32,128]{1,0:T(8,128)S(1)}, f32[32,128]{1,0:T(8,128)S(1)}, u32[]{:S(2)}, u32[]{:S(2)}) collective-permute-start(f32[32,128]{1,0:T(8,128)S(1)} %get-tuple-element.70), channel_id=1, source_target_pairs={{0,32},{16,48},{32,0},{48,16},{1,33},{17,49},{33,1},{49,17},{2,34}... | collective-permute-start | bytes 49160 | tf_op jit(solution)/shard_map/ppermute | solution.py:362
  50.4 3.6 %collective-permute-start.18 = (f32[32,128]{1,0:T(8,128)S(1)}, f32[32,128]{1,0:T(8,128)S(1)}, u32[]{:S(2)}, u32[]{:S(2)}) collective-permute-start(f32[32,128]{1,0:T(8,128)S(1)} %get-tuple-element.71), channel_id=1, source_target_pairs={{0,16},{16,32},{32,48},{48,0},{1,17},{17,33},{33,49},{49,1},{2,18}... | collective-permute-start | bytes 49160 | tf_op jit(solution)/shard_map/ppermute | solution.py:362
  53.9 0.6 collective-permute-start.19
  54.5 1.6 %collective-permute-done.17.q1 = f32[32,128]{1,0:T(8,128)S(1)} collective-permute-done((f32[32,128]{1,0:T(8,128)S(1)}, f32[32,128]{1,0:T(8,128)S(1)}, u32[]{:S(2)}, u32[]{:S(2)}) %collective-permute-start.17) | collective-permute-done | bytes 16416 | tf_op jit(solution)/shard_map/ppermute | solution.py:362
  56.1 0.3 collective-permute-done.18.q2
  56.5 2.1 %collective-permute-done.19.q3 = f32[32,128]{1,0:T(8,128)S(1)} collective-permute-done((f32[32,128]{1,0:T(8,128)S(1)}, f32[32,128]{1,0:T(8,128)S(1)}, u32[]{:S(2)}, u32[]{:S(2)}) %collective-permute-start.19) | collective-permute-done | bytes 16416 | tf_op jit(solution)/shard_map/ppermute | solution.py:362
  58.6 0.6 %last.1 = f32[32,128]{1,0:T(8,128)} custom-call(f32[32,128]{1,0:T(8,128)S(1)} %get-tuple-element.69.u0, f32[32,128]{1,0:T(8,128)S(1)} %collective-permute-done.17.q1, f32[32,128]{1,0:T(8,128)S(1)} %collective-permute-done.18.q2, f32[32,128]{1,0:T(8,128)S(1)} %collective-permute-done.19.q3), custom_call_target="tpu_custom_call" | custom-call | tf_op jit(solution)/shard_map/last/pallas_call | solution.py:471
  (4 shorter events, 0.1 us)
Async XLA Ops:
  0.0 28.9 %copy-start.1 = (f32[1,128,4]{1,2,0:T(4,128)S(1)}, f32[1,128,4]{1,2,0:T(4,128)}, u32[]{:S(2)}) copy-start(f32[1,128,4]{1,2,0:T(4,128)} %param.17) | copy-start | bytes 6148
  0.0 28.9 %copy-start.3 = (s32[1,128]{1,0:T(1,128)S(1)}, s32[1,128]{1,0:T(1,128)}, u32[]{:S(2)}) copy-start(s32[1,128]{1,0:T(1,128)} %rec_pos.1) | copy-start | bytes 1540
  0.0 28.9 %copy-start = (f32[1,16,4]{1,2,0:T(4,128)S(1)}, f32[1,16,4]{1,2,0:T(4,128)}, u32[]{:S(2)}) copy-start(f32[1,16,4]{1,2,0:T(4,128)} %param.15) | copy-start | bytes 772
  0.0 28.9 %copy-start.2 = (s32[1,16]{1,0:T(1,128)S(1)}, s32[1,16]{1,0:T(1,128)}, u32[]{:S(2)}) copy-start(s32[1,16]{1,0:T(1,128)} %src_pos.1) | copy-start | bytes 196
  0.8 14.0 %collective-permute-start.2 = (f32[1,2,4,8,128]{4,3,2,1,0:T(8,128)S(1)}, f32[1,2,4,8,128]{4,3,2,1,0:T(8,128)S(1)}, u32[]{:S(2)}, u32[]{:S(2)}) collective-permute-start(f32[1,2,4,8,128]{4,3,2,1,0:T(8,128)S(1)} %maximum_bitcast_fusion), channel_id=1, source_target_pairs={{0,32},{16,48},{32,0},{48,16},{1,33},{17,49},{33,1},{49,17},{2,34}... | collective-permute-start | bytes 98312 | tf_op jit(solution)/shard_map/ppermute | solution.py:362
  8.0 6.8 %collective-permute-start.1 = (f32[1,2,4,8,128]{4,3,2,1,0:T(8,128)S(1)}, f32[1,2,4,8,128]{4,3,2,1,0:T(8,128)S(1)}, u32[]{:S(2)}, u32[]{:S(2)}) collective-permute-start(f32[1,2,4,8,128]{4,3,2,1,0:T(8,128)S(1)} %maximum_bitcast_fusion), channel_id=1, source_target_pairs={{0,16},{16,32},{32,48},{48,0},{1,17},{17,33},{33,49},{49,1},{2,18}... | collective-permute-start | bytes 98312 | tf_op jit(solution)/shard_map/ppermute | solution.py:362
  9.5 5.3 %collective-permute-start = (f32[1,2,4,8,128]{4,3,2,1,0:T(8,128)S(1)}, f32[1,2,4,8,128]{4,3,2,1,0:T(8,128)S(1)}, u32[]{:S(2)}, u32[]{:S(2)}) collective-permute-start(f32[1,2,4,8,128]{4,3,2,1,0:T(8,128)S(1)} %maximum_bitcast_fusion), channel_id=1, source_target_pairs={{0,48},{16,0},{32,16},{48,32},{1,49},{17,1},{33,17},{49,33},{2,50}... | collective-permute-start | bytes 98312 | tf_op jit(solution)/shard_map/ppermute | solution.py:362
  14.8 8.4 %collective-permute-start.5 = (f32[4,2,4,8,128]{4,3,2,1,0:T(8,128)S(1)}, f32[4,2,4,8,128]{4,3,2,1,0:T(8,128)S(1)}, u32[]{:S(2)}, u32[]{:S(2)}) collective-permute-start(f32[4,2,4,8,128]{4,3,2,1,0:T(8,128)S(1)} %pad_maximum_fusion.a0), channel_id=1, source_target_pairs={{0,128},{64,192},{128,0},{192,64},{1,129},{65,193},{129,1},{193,65... | collective-permute-start | bytes 393224 | tf_op jit(solution)/shard_map/ppermute | solution.py:362
  17.9 6.5 %collective-permute-start.4 = (f32[4,2,4,8,128]{4,3,2,1,0:T(8,128)S(1)}, f32[4,2,4,8,128]{4,3,2,1,0:T(8,128)S(1)}, u32[]{:S(2)}, u32[]{:S(2)}) collective-permute-start(f32[4,2,4,8,128]{4,3,2,1,0:T(8,128)S(1)} %pad_maximum_fusion.a0), channel_id=1, source_target_pairs={{0,64},{64,128},{128,192},{192,0},{1,65},{65,129},{129,193},{193,1... | collective-permute-start | bytes 393224 | tf_op jit(solution)/shard_map/ppermute | solution.py:362
  18.5 5.9 %collective-permute-start.3 = (f32[4,2,4,8,128]{4,3,2,1,0:T(8,128)S(1)}, f32[4,2,4,8,128]{4,3,2,1,0:T(8,128)S(1)}, u32[]{:S(2)}, u32[]{:S(2)}) collective-permute-start(f32[4,2,4,8,128]{4,3,2,1,0:T(8,128)S(1)} %pad_maximum_fusion.a0), channel_id=1, source_target_pairs={{0,192},{64,0},{128,64},{192,128},{1,193},{65,1},{129,65},{193,129... | collective-permute-start | bytes 393224 | tf_op jit(solution)/shard_map/ppermute | solution.py:362
  21.2 13.7 %collective-permute-start.10 = (f32[15,64,128]{2,1,0:T(8,128)S(1)}, f32[15,64,128]{2,1,0:T(8,128)S(1)}, u32[]{:S(2)}, u32[]{:S(2)}) collective-permute-start(f32[15,64,128]{2,1,0:T(8,128)S(1)} %get-tuple-element.55.mine), channel_id=1, source_target_pairs={{0,1},{1,2},{2,3},{3,4},{4,5},{5,6},{6,7},{7,0},{8,9},{9,10},{10,1... | collective-permute-start | bytes 1474568 | tf_op jit(solution)/shard_map/ppermute | solution.py:358
  21.8 12.0 %collective-permute-start.11 = (f32[13,64,128]{2,1,0:T(8,128)S(1)}, f32[13,64,128]{2,1,0:T(8,128)S(1)}, u32[]{:S(2)}, u32[]{:S(2)}) collective-permute-start(f32[13,64,128]{2,1,0:T(8,128)S(1)} %get-tuple-element.56), channel_id=1, source_target_pairs={{0,7},{1,0},{2,1},{3,2},{4,3},{5,4},{6,5},{7,6},{8,15},{9,8},{10,9... | collective-permute-start | bytes 1277960 | tf_op jit(solution)/shard_map/ppermute | solution.py:358
  24.7 1.4 %collective-permute-start.6 = (f32[8,4,8,128]{3,2,1,0:T(8,128)S(1)}, f32[8,4,8,128]{3,2,1,0:T(8,128)S(1)}, u32[]{:S(2)}, u32[]{:S(2)}) collective-permute-start(f32[8,4,8,128]{3,2,1,0:T(8,128)S(1)} %get-tuple-element.48), channel_id=1, source_target_pairs={{0,8},{8,0},{1,9},{9,1},{2,10},{10,2},{3,11},{11,3},{4,12},{12,4},... | collective-permute-start | bytes 393224 | tf_op jit(solution)/shard_map/ppermute | solution.py:354
  24.8 1.5 %collective-permute-start.7 = (f32[8,4,8,128]{3,2,1,0:T(8,128)S(1)}, f32[8,4,8,128]{3,2,1,0:T(8,128)S(1)}, u32[]{:S(2)}, u32[]{:S(2)}) collective-permute-start(f32[8,4,8,128]{3,2,1,0:T(8,128)S(1)} %get-tuple-element.49), channel_id=1, source_target_pairs={{0,8},{8,0},{1,9},{9,1},{2,10},{10,2},{3,11},{11,3},{4,12},{12,4},... | collective-permute-start | bytes 393224 | tf_op jit(solution)/shard_map/ppermute | solution.py:354
  26.8 11.0 %collective-permute-start.8 = (f32[7,64,128]{2,1,0:T(8,128)S(1)}, f32[7,64,128]{2,1,0:T(8,128)S(1)}, u32[]{:S(2)}, u32[]{:S(2)}) collective-permute-start(f32[7,64,128]{2,1,0:T(8,128)S(1)} %bitcast.20), channel_id=1, source_target_pairs={{0,1},{1,2},{2,3},{3,4},{4,5},{5,6},{6,7},{7,0},{8,9},{9,10},{10,1... | collective-permute-start | bytes 688136 | tf_op jit(solution)/shard_map/ppermute | solution.py:358
  28.5 9.3 %collective-permute-start.9 = (f32[6,64,128]{2,1,0:T(8,128)S(1)}, f32[6,64,128]{2,1,0:T(8,128)S(1)}, u32[]{:S(2)}, u32[]{:S(2)}) collective-permute-start(f32[6,64,128]{2,1,0:T(8,128)S(1)} %bitcast.21), channel_id=1, source_target_pairs={{0,7},{1,0},{2,1},{3,2},{4,3},{5,4},{6,5},{7,6},{8,15},{9,8},{10,9... | collective-permute-start | bytes 589832 | tf_op jit(solution)/shard_map/ppermute | solution.py:358
  39.5 2.2 %collective-permute-start.12 = (f32[12,32,128]{2,1,0:T(8,128)S(1)}, f32[12,32,128]{2,1,0:T(8,128)S(1)}, u32[]{:S(2)}, u32[]{:S(2)}) collective-permute-start(f32[12,32,128]{2,1,0:T(8,128)S(1)} %get-tuple-element.64), channel_id=1, source_target_pairs={{0,8},{8,0},{1,9},{9,1},{2,10},{10,2},{3,11},{11,3},{4,12},{12,4},... | collective-permute-start | bytes 589832 | tf_op jit(solution)/shard_map/ppermute | solution.py:354
  39.6 1.5 %collective-permute-start.13 = (f32[4,32,128]{2,1,0:T(8,128)S(1)}, f32[4,32,128]{2,1,0:T(8,128)S(1)}, u32[]{:S(2)}, u32[]{:S(2)}) collective-permute-start(f32[4,32,128]{2,1,0:T(8,128)S(1)} %get-tuple-element.66), channel_id=1, source_target_pairs={{0,8},{8,0},{1,9},{9,1},{2,10},{10,2},{3,11},{11,3},{4,12},{12,4},... | collective-permute-start | bytes 196616 | tf_op jit(solution)/shard_map/ppermute | solution.py:354
  41.1 6.5 %collective-permute-start.14 = (f32[4,32,128]{2,1,0:T(8,128)S(1)}, f32[4,32,128]{2,1,0:T(8,128)S(1)}, u32[]{:S(2)}, u32[]{:S(2)}) collective-permute-start(f32[4,32,128]{2,1,0:T(8,128)S(1)} %halve1.1), channel_id=1, source_target_pairs={{0,128},{64,192},{128,0},{192,64},{1,129},{65,193},{129,1},{193,65... | collective-permute-start | bytes 196616 | tf_op jit(solution)/shard_map/ppermute | solution.py:362
  41.7 6.6 %collective-permute-start.15 = (f32[4,32,128]{2,1,0:T(8,128)S(1)}, f32[4,32,128]{2,1,0:T(8,128)S(1)}, u32[]{:S(2)}, u32[]{:S(2)}) collective-permute-start(f32[4,32,128]{2,1,0:T(8,128)S(1)} %get-tuple-element.67), channel_id=1, source_target_pairs={{0,64},{64,128},{128,192},{192,0},{1,65},{65,129},{129,193},{193,1... | collective-permute-start | bytes 196616 | tf_op jit(solution)/shard_map/ppermute | solution.py:362
  43.9 4.5 %collective-permute-start.16 = (f32[4,32,128]{2,1,0:T(8,128)S(1)}, f32[4,32,128]{2,1,0:T(8,128)S(1)}, u32[]{:S(2)}, u32[]{:S(2)}) collective-permute-start(f32[4,32,128]{2,1,0:T(8,128)S(1)} %get-tuple-element.68), channel_id=1, source_target_pairs={{0,192},{64,0},{128,64},{192,128},{1,193},{65,1},{129,65},{193,129... | collective-permute-start | bytes 196616 | tf_op jit(solution)/shard_map/ppermute | solution.py:362
  48.4 7.7 %collective-permute-start.17 = (f32[32,128]{1,0:T(8,128)S(1)}, f32[32,128]{1,0:T(8,128)S(1)}, u32[]{:S(2)}, u32[]{:S(2)}) collective-permute-start(f32[32,128]{1,0:T(8,128)S(1)} %get-tuple-element.70), channel_id=1, source_target_pairs={{0,32},{16,48},{32,0},{48,16},{1,33},{17,49},{33,1},{49,17},{2,34}... | collective-permute-start | bytes 49160 | tf_op jit(solution)/shard_map/ppermute | solution.py:362
  50.4 6.1 %collective-permute-start.18 = (f32[32,128]{1,0:T(8,128)S(1)}, f32[32,128]{1,0:T(8,128)S(1)}, u32[]{:S(2)}, u32[]{:S(2)}) collective-permute-start(f32[32,128]{1,0:T(8,128)S(1)} %get-tuple-element.71), channel_id=1, source_target_pairs={{0,16},{16,32},{32,48},{48,0},{1,17},{17,33},{33,49},{49,1},{2,18}... | collective-permute-start | bytes 49160 | tf_op jit(solution)/shard_map/ppermute | solution.py:362
  53.9 4.6 %collective-permute-start.19 = (f32[32,128]{1,0:T(8,128)S(1)}, f32[32,128]{1,0:T(8,128)S(1)}, u32[]{:S(2)}, u32[]{:S(2)}) collective-permute-start(f32[32,128]{1,0:T(8,128)S(1)} %get-tuple-element.72), channel_id=1, source_target_pairs={{0,48},{16,0},{32,16},{48,32},{1,49},{17,1},{33,17},{49,33},{2,50}... | collective-permute-start | bytes 49160 | tf_op jit(solution)/shard_map/ppermute | solution.py:362

commit v7 on v5

--- a/solution.py
+++ b/solution.py
@@ -282,7 +282,7 @@
         corr[pl.ds(y - STEPS, ROWS, stride=COLS), :] = value / STEPS
         return 0
 
-    lax.fori_loop(STEPS, STEPS + COLS, image, 0, unroll=2)
+    lax.fori_loop(STEPS, STEPS + COLS, image, 0, unroll=8)
 
     c, g = place()
     b = anchor(anchors, g)

time: 59.8 us -> 59.7 us (level)
  no operation moved by 1% of the time
where the time goes in v7:
time: 59.7 us; the launch traced here: 59 us
  starting transfers between devices  32.5 us (54%)
  waiting for transfers between devices  15.3 us (26%)
  Pallas kernels  10.2 us (17%)
  other arithmetic  0.79 us (1%)
    ppermute x12, starting transfers between devices, along(): lax.ppermute(blocks[d - 1], axis, [(i, (i + d) % 4) for i in range(4)])  27.7 us
    ppermute x12, waiting for transfers between devices, along(): lax.ppermute(blocks[d - 1], axis, [(i, (i + d) % 4) for i in range(4)])  8.53 us
    ppermute x4, waiting for transfers between devices, to_tile(): lax.ppermute(block, 'tile', [(i, (i + distance) % NT) for i in range(NT)])  4.54 us
    ppermute x4, starting transfers between devices, to_tile(): lax.ppermute(block, 'tile', [(i, (i + distance) % NT) for i in range(NT)])  4.13 us
    pallas_call x1, Pallas kernels, local(): pl.pallas_call(pack_kernel, out_shape=[shape(4, COLS * ROWS, DEPTH), shap...  2.64 us
    ppermute x3, waiting for transfers between devices, other_core(): return lax.ppermute(block, 'core', [(0, 1), (1, 0)])  2.27 us
    pallas_call x1, Pallas kernels, local(): pl.pallas_call(inject_kernel, out_shape=[shape(STEPS, PLANES, *plane)] *...  1.97 us
    pallas_call x1, Pallas kernels, inner(): pl.pallas_call(inner_kernel, out_shape=STATE, in_specs=[VMEM] * 7, out_sp...  1.78 us
  transfers between devices with their start and end apart: 19, of which 12 were waited for; matrix products, arithmetic and copies ran while one was open for 0% of the time, Pallas kernels for 13%

profile of v7, /device:TPU:24, one launch (start us, length us, event | category | flops | bytes accessed | tf_op | source)
XLA Modules:
  0.0 59.0 jit_solution(9808010658666788716)
XLA Ops:
  0.0 0.0 copy-start.1
  0.0 0.0 copy-start.3
  0.0 0.0 copy-start
  0.0 0.0 copy-start.2
  0.0 0.8 %maximum_bitcast_fusion = f32[1,2,4,8,128]{4,3,2,1,0:T(8,128)S(1)} fusion(f32[1,4,8,128]{3,2,1,0:T(8,128)} %bitcast.22, f32[1,4,8,128]{3,2,1,0:T(8,128)} %bitcast.23), kind=kLoop, calls=%fused_computation.1 | loop fusion | flops 8192 | bytes 65536 | tf_op jit(solution)/shard_map/broadcast_in_dim | solution.py:357
  0.8 7.2 %collective-permute-start.2 = (f32[1,2,4,8,128]{4,3,2,1,0:T(8,128)S(1)}, f32[1,2,4,8,128]{4,3,2,1,0:T(8,128)S(1)}, u32[]{:S(2)}, u32[]{:S(2)}) collective-permute-start(f32[1,2,4,8,128]{4,3,2,1,0:T(8,128)S(1)} %maximum_bitcast_fusion), channel_id=1, source_target_pairs={{0,32},{16,48},{32,0},{48,16},{1,33},{17,49},{33,1},{49,17},{2,34}... | collective-permute-start | bytes 98312 | tf_op jit(solution)/shard_map/ppermute | solution.py:352
  8.0 1.5 %collective-permute-start.1 = (f32[1,2,4,8,128]{4,3,2,1,0:T(8,128)S(1)}, f32[1,2,4,8,128]{4,3,2,1,0:T(8,128)S(1)}, u32[]{:S(2)}, u32[]{:S(2)}) collective-permute-start(f32[1,2,4,8,128]{4,3,2,1,0:T(8,128)S(1)} %maximum_bitcast_fusion), channel_id=1, source_target_pairs={{0,16},{16,32},{32,48},{48,0},{1,17},{17,33},{33,49},{49,1},{2,18}... | collective-permute-start | bytes 98312 | tf_op jit(solution)/shard_map/ppermute | solution.py:352
  9.5 2.7 %collective-permute-start = (f32[1,2,4,8,128]{4,3,2,1,0:T(8,128)S(1)}, f32[1,2,4,8,128]{4,3,2,1,0:T(8,128)S(1)}, u32[]{:S(2)}, u32[]{:S(2)}) collective-permute-start(f32[1,2,4,8,128]{4,3,2,1,0:T(8,128)S(1)} %maximum_bitcast_fusion), channel_id=1, source_target_pairs={{0,48},{16,0},{32,16},{48,32},{1,49},{17,1},{33,17},{49,33},{2,50}... | collective-permute-start | bytes 98312 | tf_op jit(solution)/shard_map/ppermute | solution.py:352
  12.1 2.6 %pack.1 = (f32[4,512,128]{2,1,0:T(8,128)S(1)}, f32[13,64,128]{2,1,0:T(8,128)S(1)}, f32[15,64,128]{2,1,0:T(8,128)S(1)}, s32[1,32]{1,0:T(1,128)S(1)}) custom-call(f32[4,64,8,128]{3,2,1,0:T(8,128)} %src_in.1, f32[4,64,8,128]{3,2,1,0:T(8,128)} %rcv_in.1, s32[1,32]{1,0:T(1,128)} %bitcast.24), custom_call_target="tpu_custom_call" | custom-call | tf_op jit(solution)/shard_map/pack/pallas_call | solution.py:360
  14.8 0.0 collective-permute-done.2
  14.8 0.0 collective-permute-done.1
  14.8 0.0 collective-permute-done
  14.8 3.1 %collective-permute-start.5 = (f32[4,2,4,8,128]{4,3,2,1,0:T(8,128)S(1)}, f32[4,2,4,8,128]{4,3,2,1,0:T(8,128)S(1)}, u32[]{:S(2)}, u32[]{:S(2)}) collective-permute-start(f32[4,2,4,8,128]{4,3,2,1,0:T(8,128)S(1)} %pad_maximum_fusion.a0), channel_id=1, source_target_pairs={{0,128},{64,192},{128,0},{192,64},{1,129},{65,193},{129,1},{193,65... | collective-permute-start | bytes 393224 | tf_op jit(solution)/shard_map/ppermute | solution.py:352
  17.9 0.6 %collective-permute-start.4 = (f32[4,2,4,8,128]{4,3,2,1,0:T(8,128)S(1)}, f32[4,2,4,8,128]{4,3,2,1,0:T(8,128)S(1)}, u32[]{:S(2)}, u32[]{:S(2)}) collective-permute-start(f32[4,2,4,8,128]{4,3,2,1,0:T(8,128)S(1)} %pad_maximum_fusion.a0), channel_id=1, source_target_pairs={{0,64},{64,128},{128,192},{192,0},{1,65},{65,129},{129,193},{193,1... | collective-permute-start | bytes 393224 | tf_op jit(solution)/shard_map/ppermute | solution.py:352
  18.5 2.6 %collective-permute-start.3 = (f32[4,2,4,8,128]{4,3,2,1,0:T(8,128)S(1)}, f32[4,2,4,8,128]{4,3,2,1,0:T(8,128)S(1)}, u32[]{:S(2)}, u32[]{:S(2)}) collective-permute-start(f32[4,2,4,8,128]{4,3,2,1,0:T(8,128)S(1)} %pad_maximum_fusion.a0), channel_id=1, source_target_pairs={{0,192},{64,0},{128,64},{192,128},{1,193},{65,1},{129,65},{193,129... | collective-permute-start | bytes 393224 | tf_op jit(solution)/shard_map/ppermute | solution.py:352
  21.2 0.7 %collective-permute-start.10 = (f32[15,64,128]{2,1,0:T(8,128)S(1)}, f32[15,64,128]{2,1,0:T(8,128)S(1)}, u32[]{:S(2)}, u32[]{:S(2)}) collective-permute-start(f32[15,64,128]{2,1,0:T(8,128)S(1)} %get-tuple-element.55.mine), channel_id=1, source_target_pairs={{0,1},{1,2},{2,3},{3,4},{4,5},{5,6},{6,7},{7,0},{8,9},{9,10},{10,1... | collective-permute-start | bytes 1474568 | tf_op jit(solution)/shard_map/ppermute | solution.py:348
  21.8 1.3 %collective-permute-start.11 = (f32[13,64,128]{2,1,0:T(8,128)S(1)}, f32[13,64,128]{2,1,0:T(8,128)S(1)}, u32[]{:S(2)}, u32[]{:S(2)}) collective-permute-start(f32[13,64,128]{2,1,0:T(8,128)S(1)} %get-tuple-element.56), channel_id=1, source_target_pairs={{0,7},{1,0},{2,1},{3,2},{4,3},{5,4},{6,5},{7,6},{8,15},{9,8},{10,9... | collective-permute-start | bytes 1277960 | tf_op jit(solution)/shard_map/ppermute | solution.py:348
  23.2 0.0 collective-permute-done.5.a3
  23.2 1.2 %collective-permute-done.4.a2 = f32[4,2,4,8,128]{4,3,2,1,0:T(8,128)S(1)} collective-permute-done((f32[4,2,4,8,128]{4,3,2,1,0:T(8,128)S(1)}, f32[4,2,4,8,128]{4,3,2,1,0:T(8,128)S(1)}, u32[]{:S(2)}, u32[]{:S(2)}) %collective-permute-start.4) | collective-permute-done | bytes 131104 | tf_op jit(solution)/shard_map/ppermute | solution.py:352
  24.4 0.0 collective-permute-done.3.a1
  24.4 0.3 window1.1
  24.7 0.1 collective-permute-start.6
  24.8 0.5 collective-permute-start.7
  25.3 0.3 window0.1
  25.6 0.6 collective-permute-done.6.other_m
  26.1 0.2 collective-permute-done.7.other_b
  26.3 0.5 edge.1
  26.8 1.7 %collective-permute-start.8 = (f32[7,64,128]{2,1,0:T(8,128)S(1)}, f32[7,64,128]{2,1,0:T(8,128)S(1)}, u32[]{:S(2)}, u32[]{:S(2)}) collective-permute-start(f32[7,64,128]{2,1,0:T(8,128)S(1)} %bitcast.20), channel_id=1, source_target_pairs={{0,1},{1,2},{2,3},{3,4},{4,5},{5,6},{6,7},{7,0},{8,9},{9,10},{10,1... | collective-permute-start | bytes 688136 | tf_op jit(solution)/shard_map/ppermute | solution.py:348
  28.5 0.4 collective-permute-start.9
  28.9 0.0 copy-done.1
  28.9 0.0 copy-done.3
  28.9 0.0 copy-done
  28.9 0.0 copy-done.2
  28.9 2.0 %inject.1 = (f32[4,16,64,128]{3,2,1,0:T(8,128)S(1)}, f32[4,16,64,128]{3,2,1,0:T(8,128)S(1)}) custom-call(s32[1,16]{1,0:T(1,128)S(1)} %copy-done.2, f32[4,16]{1,0:T(4,128)S(1)} %bitcast.18, s32[1,128]{1,0:T(1,128)S(1)} %copy-done.3, f32[4,128]{1,0:T(4,128)S(1)} %bitcast.19), custom_call_target="tpu_custom_call" | custom-call | tf_op jit(solution)/shard_map/inject/pallas_call | solution.py:387
  30.9 0.5 model.1
  31.4 2.4 %collective-permute-done.11.nxt = f32[13,64,128]{2,1,0:T(8,128)S(1)} collective-permute-done((f32[13,64,128]{2,1,0:T(8,128)S(1)}, f32[13,64,128]{2,1,0:T(8,128)S(1)}, u32[]{:S(2)}, u32[]{:S(2)}) %collective-permute-start.11) | collective-permute-done | bytes 426016 | tf_op jit(solution)/shard_map/ppermute | solution.py:348
  33.8 1.1 %collective-permute-done.10.prev = f32[15,64,128]{2,1,0:T(8,128)S(1)} collective-permute-done((f32[15,64,128]{2,1,0:T(8,128)S(1)}, f32[15,64,128]{2,1,0:T(8,128)S(1)}, u32[]{:S(2)}, u32[]{:S(2)}) %collective-permute-start.10) | collective-permute-done | bytes 491552 | tf_op jit(solution)/shard_map/ppermute | solution.py:348
  34.9 1.8 %inner.1 = (f32[5,16,64,128]{3,2,1,0:T(8,128)S(1)}, f32[5,16,64,128]{3,2,1,0:T(8,128)S(1)}, f32[16,64,128]{2,1,0:T(8,128)S(1)}, f32[16,64,128]{2,1,0:T(8,128)S(1...) custom-call(f32[4,8,64,128]{3,2,1,0:T(8,128)S(1)} %bitcast.17, ...), custom_call_target="tpu_custom_call" | custom-call | tf_op jit(solution)/shard_map/inner/pallas_call | solution.py:300
  36.7 1.1 %collective-permute-done.9.model_next = f32[6,64,128]{2,1,0:T(8,128)S(1)} collective-permute-done((f32[6,64,128]{2,1,0:T(8,128)S(1)}, f32[6,64,128]{2,1,0:T(8,128)S(1)}, u32[]{:S(2)}, u32[]{:S(2)}) %collective-permute-start.9) | collective-permute-done | bytes 196640 | tf_op jit(solution)/shard_map/ppermute | solution.py:348
  37.8 0.0 collective-permute-done.8.model_prev
  37.8 1.6 %outer.1 = (f32[16,32,128]{2,1,0:T(8,128)S(1)}, f32[16,32,128]{2,1,0:T(8,128)S(1)}, f32[5,16,64,128]{3,2,1,0:T(8,128)S(1)}, f32[5,16,64,128]{3,2,1,0:T(8,128)S(1...) custom-call(s32[1,32]{1,0:T(1,128)S(1)} %get-tuple-element.39.anchor, ...), custom_call_target="tpu_custom_call", output_to_operand_aliasing={{2}: (5, {}), {3}: (6, {}), {4}: (7, {}), {5}: (8, {}), {6}... | custom-call | tf_op jit(solution)/shard_map/outer/pallas_call | solution.py:312
  39.4 0.1 collective-permute-start.12
  39.5 1.5 %collective-permute-done.12.got = f32[16,32,128]{2,1,0:T(8,128)S(1)} collective-permute-done((f32[16,32,128]{2,1,0:T(8,128)S(1)}, f32[16,32,128]{2,1,0:T(8,128)S(1)}, u32[]{:S(2)}, u32[]{:S(2)}) %collective-permute-start.12) | collective-permute-done | bytes 262176 | tf_op jit(solution)/shard_map/ppermute | solution.py:344
  41.1 0.5 collective-permute-start.13
  41.6 2.1 %collective-permute-start.14 = (f32[4,32,128]{2,1,0:T(8,128)S(1)}, f32[4,32,128]{2,1,0:T(8,128)S(1)}, u32[]{:S(2)}, u32[]{:S(2)}) collective-permute-start(f32[4,32,128]{2,1,0:T(8,128)S(1)} %get-tuple-element.67), channel_id=1, source_target_pairs={{0,64},{64,128},{128,192},{192,0},{1,65},{65,129},{129,193},{193,1... | collective-permute-start | bytes 196616 | tf_op jit(solution)/shard_map/ppermute | solution.py:352
  43.7 1.2 %collective-permute-start.15 = (f32[4,32,128]{2,1,0:T(8,128)S(1)}, f32[4,32,128]{2,1,0:T(8,128)S(1)}, u32[]{:S(2)}, u32[]{:S(2)}) collective-permute-start(f32[4,32,128]{2,1,0:T(8,128)S(1)} %get-tuple-element.68), channel_id=1, source_target_pairs={{0,192},{64,0},{128,64},{192,128},{1,193},{65,1},{129,65},{193,129... | collective-permute-start | bytes 196616 | tf_op jit(solution)/shard_map/ppermute | solution.py:352
  44.8 2.7 %collective-permute-done.13.r1 = f32[4,32,128]{2,1,0:T(8,128)S(1)} collective-permute-done((f32[4,32,128]{2,1,0:T(8,128)S(1)}, f32[4,32,128]{2,1,0:T(8,128)S(1)}, u32[]{:S(2)}, u32[]{:S(2)}) %collective-permute-start.13) | collective-permute-done | bytes 65568 | tf_op jit(solution)/shard_map/ppermute | solution.py:352
  47.5 0.6 collective-permute-done.14.r2
  48.1 0.0 collective-permute-done.15.r3
  48.1 2.1 %collective-permute-start.16 = (f32[32,128]{1,0:T(8,128)S(1)}, f32[32,128]{1,0:T(8,128)S(1)}, u32[]{:S(2)}, u32[]{:S(2)}) collective-permute-start(f32[32,128]{1,0:T(8,128)S(1)} %get-tuple-element.70), channel_id=1, source_target_pairs={{0,32},{16,48},{32,0},{48,16},{1,33},{17,49},{33,1},{49,17},{2,34}... | collective-permute-start | bytes 49160 | tf_op jit(solution)/shard_map/ppermute | solution.py:352
  50.2 3.6 %collective-permute-start.17 = (f32[32,128]{1,0:T(8,128)S(1)}, f32[32,128]{1,0:T(8,128)S(1)}, u32[]{:S(2)}, u32[]{:S(2)}) collective-permute-start(f32[32,128]{1,0:T(8,128)S(1)} %get-tuple-element.71), channel_id=1, source_target_pairs={{0,16},{16,32},{32,48},{48,0},{1,17},{17,33},{33,49},{49,1},{2,18}... | collective-permute-start | bytes 49160 | tf_op jit(solution)/shard_map/ppermute | solution.py:352
  53.8 0.6 collective-permute-start.18
  54.3 1.5 %collective-permute-done.16.q1 = f32[32,128]{1,0:T(8,128)S(1)} collective-permute-done((f32[32,128]{1,0:T(8,128)S(1)}, f32[32,128]{1,0:T(8,128)S(1)}, u32[]{:S(2)}, u32[]{:S(2)}) %collective-permute-start.16) | collective-permute-done | bytes 16416 | tf_op jit(solution)/shard_map/ppermute | solution.py:352
  55.8 0.4 collective-permute-done.17.q2
  56.2 2.2 %collective-permute-done.18.q3 = f32[32,128]{1,0:T(8,128)S(1)} collective-permute-done((f32[32,128]{1,0:T(8,128)S(1)}, f32[32,128]{1,0:T(8,128)S(1)}, u32[]{:S(2)}, u32[]{:S(2)}) %collective-permute-start.18) | collective-permute-done | bytes 16416 | tf_op jit(solution)/shard_map/ppermute | solution.py:352
  58.4 0.6 %last.1 = f32[32,128]{1,0:T(8,128)} custom-call(f32[32,128]{1,0:T(8,128)S(1)} %get-tuple-element.69.u0, f32[32,128]{1,0:T(8,128)S(1)} %collective-permute-done.16.q1, f32[32,128]{1,0:T(8,128)S(1)} %collective-permute-done.17.q2, f32[32,128]{1,0:T(8,128)S(1)} %collective-permute-done.18.q3), custom_call_target="tpu_custom_call" | custom-call | tf_op jit(solution)/shard_map/last/pallas_call | solution.py:456
  (3 shorter events, 0.1 us)
Async XLA Ops:
  0.0 28.9 %copy-start.1 = (f32[1,128,4]{1,2,0:T(4,128)S(1)}, f32[1,128,4]{1,2,0:T(4,128)}, u32[]{:S(2)}) copy-start(f32[1,128,4]{1,2,0:T(4,128)} %param.17) | copy-start | bytes 6148
  0.0 28.9 %copy-start.3 = (s32[1,128]{1,0:T(1,128)S(1)}, s32[1,128]{1,0:T(1,128)}, u32[]{:S(2)}) copy-start(s32[1,128]{1,0:T(1,128)} %rec_pos.1) | copy-start | bytes 1540
  0.0 28.9 %copy-start = (f32[1,16,4]{1,2,0:T(4,128)S(1)}, f32[1,16,4]{1,2,0:T(4,128)}, u32[]{:S(2)}) copy-start(f32[1,16,4]{1,2,0:T(4,128)} %param.15) | copy-start | bytes 772
  0.0 28.9 %copy-start.2 = (s32[1,16]{1,0:T(1,128)S(1)}, s32[1,16]{1,0:T(1,128)}, u32[]{:S(2)}) copy-start(s32[1,16]{1,0:T(1,128)} %src_pos.1) | copy-start | bytes 196
  0.8 14.0 %collective-permute-start.2 = (f32[1,2,4,8,128]{4,3,2,1,0:T(8,128)S(1)}, f32[1,2,4,8,128]{4,3,2,1,0:T(8,128)S(1)}, u32[]{:S(2)}, u32[]{:S(2)}) collective-permute-start(f32[1,2,4,8,128]{4,3,2,1,0:T(8,128)S(1)} %maximum_bitcast_fusion), channel_id=1, source_target_pairs={{0,32},{16,48},{32,0},{48,16},{1,33},{17,49},{33,1},{49,17},{2,34}... | collective-permute-start | bytes 98312 | tf_op jit(solution)/shard_map/ppermute | solution.py:352
  8.0 6.8 %collective-permute-start.1 = (f32[1,2,4,8,128]{4,3,2,1,0:T(8,128)S(1)}, f32[1,2,4,8,128]{4,3,2,1,0:T(8,128)S(1)}, u32[]{:S(2)}, u32[]{:S(2)}) collective-permute-start(f32[1,2,4,8,128]{4,3,2,1,0:T(8,128)S(1)} %maximum_bitcast_fusion), channel_id=1, source_target_pairs={{0,16},{16,32},{32,48},{48,0},{1,17},{17,33},{33,49},{49,1},{2,18}... | collective-permute-start | bytes 98312 | tf_op jit(solution)/shard_map/ppermute | solution.py:352
  9.5 5.3 %collective-permute-start = (f32[1,2,4,8,128]{4,3,2,1,0:T(8,128)S(1)}, f32[1,2,4,8,128]{4,3,2,1,0:T(8,128)S(1)}, u32[]{:S(2)}, u32[]{:S(2)}) collective-permute-start(f32[1,2,4,8,128]{4,3,2,1,0:T(8,128)S(1)} %maximum_bitcast_fusion), channel_id=1, source_target_pairs={{0,48},{16,0},{32,16},{48,32},{1,49},{17,1},{33,17},{49,33},{2,50}... | collective-permute-start | bytes 98312 | tf_op jit(solution)/shard_map/ppermute | solution.py:352
  14.8 8.4 %collective-permute-start.5 = (f32[4,2,4,8,128]{4,3,2,1,0:T(8,128)S(1)}, f32[4,2,4,8,128]{4,3,2,1,0:T(8,128)S(1)}, u32[]{:S(2)}, u32[]{:S(2)}) collective-permute-start(f32[4,2,4,8,128]{4,3,2,1,0:T(8,128)S(1)} %pad_maximum_fusion.a0), channel_id=1, source_target_pairs={{0,128},{64,192},{128,0},{192,64},{1,129},{65,193},{129,1},{193,65... | collective-permute-start | bytes 393224 | tf_op jit(solution)/shard_map/ppermute | solution.py:352
  17.9 6.5 %collective-permute-start.4 = (f32[4,2,4,8,128]{4,3,2,1,0:T(8,128)S(1)}, f32[4,2,4,8,128]{4,3,2,1,0:T(8,128)S(1)}, u32[]{:S(2)}, u32[]{:S(2)}) collective-permute-start(f32[4,2,4,8,128]{4,3,2,1,0:T(8,128)S(1)} %pad_maximum_fusion.a0), channel_id=1, source_target_pairs={{0,64},{64,128},{128,192},{192,0},{1,65},{65,129},{129,193},{193,1... | collective-permute-start | bytes 393224 | tf_op jit(solution)/shard_map/ppermute | solution.py:352
  18.5 5.9 %collective-permute-start.3 = (f32[4,2,4,8,128]{4,3,2,1,0:T(8,128)S(1)}, f32[4,2,4,8,128]{4,3,2,1,0:T(8,128)S(1)}, u32[]{:S(2)}, u32[]{:S(2)}) collective-permute-start(f32[4,2,4,8,128]{4,3,2,1,0:T(8,128)S(1)} %pad_maximum_fusion.a0), channel_id=1, source_target_pairs={{0,192},{64,0},{128,64},{192,128},{1,193},{65,1},{129,65},{193,129... | collective-permute-start | bytes 393224 | tf_op jit(solution)/shard_map/ppermute | solution.py:352
  21.2 13.7 %collective-permute-start.10 = (f32[15,64,128]{2,1,0:T(8,128)S(1)}, f32[15,64,128]{2,1,0:T(8,128)S(1)}, u32[]{:S(2)}, u32[]{:S(2)}) collective-permute-start(f32[15,64,128]{2,1,0:T(8,128)S(1)} %get-tuple-element.55.mine), channel_id=1, source_target_pairs={{0,1},{1,2},{2,3},{3,4},{4,5},{5,6},{6,7},{7,0},{8,9},{9,10},{10,1... | collective-permute-start | bytes 1474568 | tf_op jit(solution)/shard_map/ppermute | solution.py:348
  21.8 12.0 %collective-permute-start.11 = (f32[13,64,128]{2,1,0:T(8,128)S(1)}, f32[13,64,128]{2,1,0:T(8,128)S(1)}, u32[]{:S(2)}, u32[]{:S(2)}) collective-permute-start(f32[13,64,128]{2,1,0:T(8,128)S(1)} %get-tuple-element.56), channel_id=1, source_target_pairs={{0,7},{1,0},{2,1},{3,2},{4,3},{5,4},{6,5},{7,6},{8,15},{9,8},{10,9... | collective-permute-start | bytes 1277960 | tf_op jit(solution)/shard_map/ppermute | solution.py:348
  24.7 1.4 %collective-permute-start.6 = (f32[8,4,8,128]{3,2,1,0:T(8,128)S(1)}, f32[8,4,8,128]{3,2,1,0:T(8,128)S(1)}, u32[]{:S(2)}, u32[]{:S(2)}) collective-permute-start(f32[8,4,8,128]{3,2,1,0:T(8,128)S(1)} %get-tuple-element.48), channel_id=1, source_target_pairs={{0,8},{8,0},{1,9},{9,1},{2,10},{10,2},{3,11},{11,3},{4,12},{12,4},... | collective-permute-start | bytes 393224 | tf_op jit(solution)/shard_map/ppermute | solution.py:344
  24.8 1.5 %collective-permute-start.7 = (f32[8,4,8,128]{3,2,1,0:T(8,128)S(1)}, f32[8,4,8,128]{3,2,1,0:T(8,128)S(1)}, u32[]{:S(2)}, u32[]{:S(2)}) collective-permute-start(f32[8,4,8,128]{3,2,1,0:T(8,128)S(1)} %get-tuple-element.49), channel_id=1, source_target_pairs={{0,8},{8,0},{1,9},{9,1},{2,10},{10,2},{3,11},{11,3},{4,12},{12,4},... | collective-permute-start | bytes 393224 | tf_op jit(solution)/shard_map/ppermute | solution.py:344
  26.8 11.0 %collective-permute-start.8 = (f32[7,64,128]{2,1,0:T(8,128)S(1)}, f32[7,64,128]{2,1,0:T(8,128)S(1)}, u32[]{:S(2)}, u32[]{:S(2)}) collective-permute-start(f32[7,64,128]{2,1,0:T(8,128)S(1)} %bitcast.20), channel_id=1, source_target_pairs={{0,1},{1,2},{2,3},{3,4},{4,5},{5,6},{6,7},{7,0},{8,9},{9,10},{10,1... | collective-permute-start | bytes 688136 | tf_op jit(solution)/shard_map/ppermute | solution.py:348
  28.5 9.3 %collective-permute-start.9 = (f32[6,64,128]{2,1,0:T(8,128)S(1)}, f32[6,64,128]{2,1,0:T(8,128)S(1)}, u32[]{:S(2)}, u32[]{:S(2)}) collective-permute-start(f32[6,64,128]{2,1,0:T(8,128)S(1)} %bitcast.21), channel_id=1, source_target_pairs={{0,7},{1,0},{2,1},{3,2},{4,3},{5,4},{6,5},{7,6},{8,15},{9,8},{10,9... | collective-permute-start | bytes 589832 | tf_op jit(solution)/shard_map/ppermute | solution.py:348
  39.4 1.6 %collective-permute-start.12 = (f32[16,32,128]{2,1,0:T(8,128)S(1)}, f32[16,32,128]{2,1,0:T(8,128)S(1)}, u32[]{:S(2)}, u32[]{:S(2)}) collective-permute-start(f32[16,32,128]{2,1,0:T(8,128)S(1)} %get-tuple-element.64), channel_id=1, source_target_pairs={{0,8},{8,0},{1,9},{9,1},{2,10},{10,2},{3,11},{11,3},{4,12},{12,4},... | collective-permute-start | bytes 786440 | tf_op jit(solution)/shard_map/ppermute | solution.py:344
  41.1 6.4 %collective-permute-start.13 = (f32[4,32,128]{2,1,0:T(8,128)S(1)}, f32[4,32,128]{2,1,0:T(8,128)S(1)}, u32[]{:S(2)}, u32[]{:S(2)}) collective-permute-start(f32[4,32,128]{2,1,0:T(8,128)S(1)} %get-tuple-element.66), channel_id=1, source_target_pairs={{0,128},{64,192},{128,0},{192,64},{1,129},{65,193},{129,1},{193,65... | collective-permute-start | bytes 196616 | tf_op jit(solution)/shard_map/ppermute | solution.py:352
  41.6 6.5 %collective-permute-start.14 = (f32[4,32,128]{2,1,0:T(8,128)S(1)}, f32[4,32,128]{2,1,0:T(8,128)S(1)}, u32[]{:S(2)}, u32[]{:S(2)}) collective-permute-start(f32[4,32,128]{2,1,0:T(8,128)S(1)} %get-tuple-element.67), channel_id=1, source_target_pairs={{0,64},{64,128},{128,192},{192,0},{1,65},{65,129},{129,193},{193,1... | collective-permute-start | bytes 196616 | tf_op jit(solution)/shard_map/ppermute | solution.py:352
  43.7 4.4 %collective-permute-start.15 = (f32[4,32,128]{2,1,0:T(8,128)S(1)}, f32[4,32,128]{2,1,0:T(8,128)S(1)}, u32[]{:S(2)}, u32[]{:S(2)}) collective-permute-start(f32[4,32,128]{2,1,0:T(8,128)S(1)} %get-tuple-element.68), channel_id=1, source_target_pairs={{0,192},{64,0},{128,64},{192,128},{1,193},{65,1},{129,65},{193,129... | collective-permute-start | bytes 196616 | tf_op jit(solution)/shard_map/ppermute | solution.py:352
  48.1 7.7 %collective-permute-start.16 = (f32[32,128]{1,0:T(8,128)S(1)}, f32[32,128]{1,0:T(8,128)S(1)}, u32[]{:S(2)}, u32[]{:S(2)}) collective-permute-start(f32[32,128]{1,0:T(8,128)S(1)} %get-tuple-element.70), channel_id=1, source_target_pairs={{0,32},{16,48},{32,0},{48,16},{1,33},{17,49},{33,1},{49,17},{2,34}... | collective-permute-start | bytes 49160 | tf_op jit(solution)/shard_map/ppermute | solution.py:352
  50.2 6.0 %collective-permute-start.17 = (f32[32,128]{1,0:T(8,128)S(1)}, f32[32,128]{1,0:T(8,128)S(1)}, u32[]{:S(2)}, u32[]{:S(2)}) collective-permute-start(f32[32,128]{1,0:T(8,128)S(1)} %get-tuple-element.71), channel_id=1, source_target_pairs={{0,16},{16,32},{32,48},{48,0},{1,17},{17,33},{33,49},{49,1},{2,18}... | collective-permute-start | bytes 49160 | tf_op jit(solution)/shard_map/ppermute | solution.py:352
  53.8 4.6 %collective-permute-start.18 = (f32[32,128]{1,0:T(8,128)S(1)}, f32[32,128]{1,0:T(8,128)S(1)}, u32[]{:S(2)}, u32[]{:S(2)}) collective-permute-start(f32[32,128]{1,0:T(8,128)S(1)} %get-tuple-element.72), channel_id=1, source_target_pairs={{0,48},{16,0},{32,16},{48,32},{1,49},{17,1},{33,17},{49,33},{2,50}... | collective-permute-start | bytes 49160 | tf_op jit(solution)/shard_map/ppermute | solution.py:352
